TPU v7x, 32 devices: a whole 2x2x4 slice. The times are simulated.
32 devices in a mesh: hst: 16 (over z, x, core), tensor: 2 (over y).
Axes of the slice: x: 2, y: 2, z: 4, core: 2. Of those that a mesh axis runs over, the one named last changes fastest.
Arguments:
- ctx_query: bfloat16 [8192, 8192], P('hst', 'tensor'), may hold values from -60 to 60
- ctx_key: bfloat16 [8192, 1024], P('hst', 'tensor'), may hold values from -12 to 12
- context_value: bfloat16 [8192, 1024], P('hst', 'tensor'), may hold values from -6 to 6
- lengths: int32 [16], replicated, may hold values from 1 to 512, 6144 in all
- owner: int32 [1], replicated, may hold values from 0 to 15
- ask_query: bfloat16 [16, 256, 8192], P('hst', None, 'tensor'), may hold values from -60 to 60
- ask_key: bfloat16 [16, 256, 1024], P('hst', None, 'tensor'), may hold values from -12 to 12
- candidate_value_rows: bfloat16 [16, 256, 1024], P('hst', None, 'tensor'), may hold values from -6 to 6
- out_weight: bfloat16 [8192, 8192], P('tensor', 'hst'), may hold values from -0.0625 to 0.0625
Outputs:
- ctx_out: bfloat16 [8192, 8192], P('hst', 'tensor')
- layer_out: bfloat16 [256, 8192], P('tensor', 'hst')
Inputs may be any that keep to these rules, and one draw needn't show every extreme that they name: `lengths`: every block has at least one valid slot and some block is full.
All inputs are finite; a program needn't handle non-finite values.
Results may differ from a plain program's by a relative error of at most 0.009.
Values may be sent and summed in bfloat16 or wider, within the bound.
No kernel may reach another device: no remote copies, remote signals or barrier semaphores. Data moves between devices by JAX's collectives and lax.ppermute only.
A program may use at most 384 MiB of HBM per device.

v0:
```python
import math

import jax
import jax.numpy as jnp
from jax import lax
from jax.sharding import PartitionSpec as P

HEAD_SIZE = 128


masked_score = -1e30


def broadcast(block, axis, owner):
    block = jnp.where(lax.axis_index(axis) == owner, block, jnp.zeros_like(block))
    return lax.psum(block, axis)


def combined_all(array, axis, combine):
    everything = jax.tree.map(lambda part: lax.all_gather(part, axis), array)
    first = jax.tree.map(lambda part: part[0], everything)

    def hop(k, so_far):
        return combine(so_far, jax.tree.map(lambda part: part[k], everything))

    return lax.fori_loop(1, lax.axis_size(axis), hop, first)


def partial_attend(queries, keys, values, allowed):
    rows = queries.shape[0]
    groups = keys.shape[1] // HEAD_SIZE
    query_heads = queries.reshape(rows, groups, -1, HEAD_SIZE)
    key_heads = keys.reshape(keys.shape[0], groups, HEAD_SIZE)
    value_heads = values.reshape(values.shape[0], groups, HEAD_SIZE)
    scores = jnp.einsum(
        "rkgd,skd->rkgs", query_heads, key_heads, preferred_element_type=jnp.float32
    ) / math.sqrt(HEAD_SIZE)
    scores = jnp.where(allowed[:, None, None, :], scores, masked_score)
    peaks = jnp.max(scores, axis=-1)
    weights = jnp.exp(scores - peaks[..., None]).astype(jnp.bfloat16)
    totals = jnp.sum(weights.astype(jnp.float32), axis=-1)
    outputs = jnp.einsum("rkgs,skd->rkgd", weights, value_heads, preferred_element_type=jnp.float32)
    return (peaks.reshape(rows, -1), totals.reshape(rows, -1), outputs.reshape(rows, -1))


def normalize(outputs, totals):
    rows, heads = totals.shape
    return (outputs.reshape(rows, heads, -1) / totals[..., None]).reshape(rows, -1)


def combine(first_piece, second_piece):
    rows, heads = first_piece[0].shape
    top = jnp.maximum(first_piece[0], second_piece[0])
    scale_one = jnp.exp(first_piece[0] - top)
    scale_two = jnp.exp(second_piece[0] - top)
    totals = scale_one * first_piece[1] + scale_two * second_piece[1]
    outputs = (
        first_piece[2].reshape(rows, heads, -1) * scale_one[..., None]
        + second_piece[2].reshape(rows, heads, -1) * scale_two[..., None]
    )
    return (top, totals, outputs.reshape(rows, -1))


def body(
    ctx_query,
    ctx_key,
    context_value,
    lengths,
    owner,
    ask_query,
    ask_key,
    candidate_value_rows,
    out_weight,
):
    host = lax.axis_index("hst")
    anchor_key, anchor_value = (broadcast(ctx_key, "hst", 0), broadcast(context_value, "hst", 0))
    block_len = ctx_query.shape[0]
    own_len = lengths[host]
    anchor_len = lengths[0]
    keys_all = jnp.concatenate([anchor_key, ctx_key], axis=0)
    values_all = jnp.concatenate([anchor_value, context_value], axis=0)
    rows_each = min(512, block_len)
    columns = jnp.arange(block_len, dtype=jnp.int32)
    row_pos = 0 + jnp.arange(rows_each, dtype=jnp.int32)
    anchor_ok = jnp.broadcast_to(
        (columns[None, :] < anchor_len) & (host > 0), (rows_each, block_len)
    )
    own_ok = (columns[None, :] <= row_pos[:, None]) & (columns[None, :] < own_len)
    allowed = jnp.concatenate([anchor_ok, own_ok], axis=1)
    peaks, totals, outputs = partial_attend(ctx_query, keys_all, values_all, allowed)
    result = jnp.where(row_pos[:, None] < own_len, normalize(outputs, totals), 0.0)
    pieces = result.astype(jnp.bfloat16)
    chosen = owner[0]
    query_rows = ask_query.shape[1]
    query_pos = jnp.arange(query_rows, dtype=jnp.int32)
    causal = query_pos[None, :] <= query_pos[:, None]
    block_ok = jnp.broadcast_to((columns < own_len)[None, :], (query_rows, block_len))
    asked, ask_keys, ask_values = (
        broadcast(ask_query[0], "hst", chosen),
        broadcast(ask_key[0], "hst", chosen),
        broadcast(candidate_value_rows[0], "hst", chosen),
    )
    local = partial_attend(asked, ctx_key, context_value, block_ok)
    pending = partial_attend(asked, ask_keys, ask_values, causal)
    merged = combined_all(local, "hst", combine)
    merged = combine(merged, pending)
    answer = normalize(merged[2], merged[1]).astype(jnp.bfloat16)
    projected = jnp.dot(answer, out_weight, preferred_element_type=jnp.float32)
    layer_out = lax.psum_scatter(
        projected.astype(jnp.bfloat16), "tensor", scatter_dimension=0, tiled=True
    )
    return (pieces, layer_out)


def solution(mesh):
    placed = (
        P("hst", "tensor"),
        P("hst", "tensor"),
        P("hst", "tensor"),
        P(),
        P(),
        P("hst", None, "tensor"),
        P("hst", None, "tensor"),
        P("hst", None, "tensor"),
        P("tensor", "hst"),
    )
    return jax.shard_map(
        body,
        mesh=mesh,
        in_specs=placed,
        out_specs=(P("hst", "tensor"), P("tensor", "hst")),
        check_vma=False,
    )
```

profile of v0, /device:TPU:0, one launch (start us, length us, event | category | flops | bytes accessed | tf_op | source)
XLA Modules:
  0.0 765.4 jit_solution(2872959636270732688)
XLA Ops:
  7.2 1.3 copy.52
  8.5 1.3 copy.54
  14.2 4.1 copy.61
  18.4 2.4 copy.62
  21.9 1.2 reshape.119
  24.2 108.5 %all-reduce.3.cloned.1.call-done = (bf16[512,512]{0,1:T(8,128)(2,1)}, bf16[512,512]{0,1:T(8,128)(2,1)}, bf16[256,4,8,128]{3,0,2,1:T(8,128)(2,1)}, bf16[256,4,128]{2,0,1:T(8,128)(2,1)}, bf16[256,4,128]{0,2,1:T(8,128)(2,1)}) async-done(((bf16[512,512]{0,1:T(8,128)(2,1)}, bf16[512,512]{0,1:T(8,128)(2,1)}, bf16[256,4,8,128]{3,0,2,1:T(8,128)(2,1)}, bf16[256,4,128]{2,0,1:T(8,128)(2,1)}, ...) | async-done | bytes 3670032 | tf_op jit(solution)/shard_map/psum | solution.py:16
  132.8 3.9 bitcast_reduce_fusion
  136.7 7.4 fusion.26
  144.2 5.7 copy.65
  149.9 5.5 copy.98
  156.5 9.0 %convert_reduce_fusion.1 = f32[256,4,8]{0,2,1:T(8,128)S(1)} fusion(f32[256,4,8]{0,2,1:T(8,128)S(1)} %get-tuple-element.231, f32[4,256,8,512]{3,1,2,0:T(8,128)} %copy-done.4, pred[512]{0:T(512)(128)(4,1)S(1)} %iota_compare_fusion.3), kind=kLoop, calls=%fused_computation.19 | loop fusion | flops 25157632 | bytes 16843264 | tf_op jit(solution)/shard_map/reduce_sum | solution.py:41
  165.6 25.0 %all_gather.10 = f32[16,256,32]{1,2,0:T(8,128)S(1)} all-gather(f32[1,256,32]{1,2,0:T(8,128)S(1)} %bitcast.187), channel_id=1, replica_groups=mesh['hst'=16,'tensor'=2] {'hst'}, dimensions={0}, use_global_device_ids=true | all-gather | bytes 557056 | tf_op jit(solution)/shard_map/all_gather | solution.py:20
  191.5 22.3 %all_gather.9 = f32[16,256,32]{1,2,0:T(8,128)S(1)} all-gather(f32[1,256,32]{1,2,0:T(8,128)S(1)} %bitcast.185), channel_id=1, replica_groups=mesh['hst'=16,'tensor'=2] {'hst'}, dimensions={0}, use_global_device_ids=true | all-gather | bytes 557056 | tf_op jit(solution)/shard_map/all_gather | solution.py:20
  214.8 2.3 fusion.8
  217.1 3.2 copy-done.3
  220.4 4.1 fusion.22
  224.5 5.8 copy.78
  230.4 35.3 %fusion.3 = (f32[512,4,8]{0,2,1:T(8,128)S(1)}, f32[4,1024,512,8]{2,1,3,0:T(8,128)}) fusion(pred[512,1024]{0,1:T(8,128)(4,1)S(1)} %pad_add_fusion, bf16[1024,4,128,1]{0,2,3,1:T(8,128)(2,1)S(1)} %bitcast.175, bf16[512,4,8,128]{3,2,1,0:T(8,128)(2,1)} %bitcast.170), kind=kOutput, calls=%fused_computation.14 | convolution fusion | flops 4345282560 | bytes 72941568 | tf_op jit(solution)/shard_map/rkgd,skd->rkgs/dot_general | solution.py:35
  265.7 22.9 %convert_reduce_fusion = f32[512,4,8]{0,2,1:T(8,128)S(1)} fusion(f32[512,4,8]{0,2,1:T(8,128)S(1)} %get-tuple-element.227, f32[4,1024,512,8]{2,1,3,0:T(8,128)} %get-tuple-element.228, pred[512,1024]{0,1:T(8,128)(4,1)S(1)} %pad_add_fusion), kind=kLoop, calls=%fused_computation.12 | loop fusion | flops 100646912 | bytes 67764224 | tf_op jit(solution)/shard_map/reduce_sum | solution.py:41
  289.0 30.2 %fusion.19 = f32[4,128,512,8]{2,1,3,0:T(8,128)} fusion(bf16[1024,4,128,1]{0,2,3,1:T(8,128)(2,1)S(1)} %bitcast.183, f32[4,1024,512,8]{2,1,3,0:T(8,128)} %get-tuple-element.228, f32[512,4,8]{0,2,1:T(8,128)S(1)} %get-tuple-element.227, pred[512,1024]{0,1:T(8,128)(4,1)S(1)} %pad_add_fusion), kind=kOutput, calls=%fused_computation.44 | convolution fusion | flops 4362076160 | bytes 77135872 | tf_op jit(solution)/shard_map/rkgs,skd->rkgd/dot_general | solution.py:42
  319.1 9.0 %copy.60 = f32[512,4096]{1,0:T(8,128)} copy(f32[512,4096]{0,1:T(8,128)} %bitcast.172) | data formatting | bytes 16777216 | tf_op jit(solution)/shard_map/reshape;reshape | solution.py:48
  328.1 5.2 convert_reduce_fusion.2
  333.3 150.9 %all-gather.2.cloned.1.call-done = f32[16,256,4096]{2,1,0:T(8,128)} async-done(((f32[1,256,4096]{2,1,0:T(8,128)}), f32[16,256,4096]{2,1,0:T(8,128)}) %all-gather.2.cloned.1.call-update) | async-done | bytes 67108880 | tf_op jit(solution)/shard_map/all_gather | solution.py:20
  484.3 4.7 slice_bitcast_fusion
  488.9 241.4 %while.19 = (s32[]{:T(128)}, f32[256,32]{1,0:T(8,128)S(1)}, f32[256,32]{1,0:T(8,128)S(1)}, f32[256,4096]{1,0:T(8,128)}, f32[16,256,32]{1,2,0:T(8,128)}, /*index=...) while((s32[]{:T(128)}, f32[256,32]{1,0:T(8,128)S(1)}, ...), condition=%wide.region_8.9_spmd, body=%wide.region_7.8_spmd.sunk | while | flops 3194885 | bytes 63504588 | solution.py:26
  491.4 1.1 mul.143
  492.6 10.6 %fusion.51 = f32[256,4096]{1,0:T(8,128)S(1)} fusion(f32[32,8,32,128]{3,2,1,0:T(8,128)S(1)} %bitcast.167, f32[256,4096]{1,0:T(8,128)S(1)} %copy-done, f32[32,8,32,128]{3,2,1,0:T(8,128)S(1)} %bitcast.168, f32[16,256,4096]{2,1,0:T(8,128)} %get-tuple-element.318, s32[]{:T(128)S(6)} %select_n.130), kind=kLoop, calls=%fused_computation.1.clone.1 | loop fusion | flops 3145728 | bytes 20971524 | tf_op jit(solution)/shard_map/while/body/eval_jaxpr/add | solution.py:58
  503.2 2.0 copy-done.1
  507.5 1.1 mul.143
  508.6 10.6 %fusion.51 = f32[256,4096]{1,0:T(8,128)S(1)} fusion(f32[32,8,32,128]{3,2,1,0:T(8,128)S(1)} %bitcast.167, f32[256,4096]{1,0:T(8,128)S(1)} %copy-done, f32[32,8,32,128]{3,2,1,0:T(8,128)S(1)} %bitcast.168, f32[16,256,4096]{2,1,0:T(8,128)} %get-tuple-element.318, s32[]{:T(128)S(6)} %select_n.130), kind=kLoop, calls=%fused_computation.1.clone.1 | loop fusion | flops 3145728 | bytes 20971524 | tf_op jit(solution)/shard_map/while/body/eval_jaxpr/add | solution.py:58
  519.3 2.0 copy-done.1
  523.5 1.1 mul.143
  524.7 10.6 %fusion.51 = f32[256,4096]{1,0:T(8,128)S(1)} fusion(f32[32,8,32,128]{3,2,1,0:T(8,128)S(1)} %bitcast.167, f32[256,4096]{1,0:T(8,128)S(1)} %copy-done, f32[32,8,32,128]{3,2,1,0:T(8,128)S(1)} %bitcast.168, f32[16,256,4096]{2,1,0:T(8,128)} %get-tuple-element.318, s32[]{:T(128)S(6)} %select_n.130), kind=kLoop, calls=%fused_computation.1.clone.1 | loop fusion | flops 3145728 | bytes 20971524 | tf_op jit(solution)/shard_map/while/body/eval_jaxpr/add | solution.py:58
  535.3 2.0 copy-done.1
  539.6 1.1 mul.143
  540.7 10.6 %fusion.51 = f32[256,4096]{1,0:T(8,128)S(1)} fusion(f32[32,8,32,128]{3,2,1,0:T(8,128)S(1)} %bitcast.167, f32[256,4096]{1,0:T(8,128)S(1)} %copy-done, f32[32,8,32,128]{3,2,1,0:T(8,128)S(1)} %bitcast.168, f32[16,256,4096]{2,1,0:T(8,128)} %get-tuple-element.318, s32[]{:T(128)S(6)} %select_n.130), kind=kLoop, calls=%fused_computation.1.clone.1 | loop fusion | flops 3145728 | bytes 20971524 | tf_op jit(solution)/shard_map/while/body/eval_jaxpr/add | solution.py:58
  551.4 2.0 copy-done.1
  556.8 10.6 %fusion.51 = f32[256,4096]{1,0:T(8,128)S(1)} fusion(f32[32,8,32,128]{3,2,1,0:T(8,128)S(1)} %bitcast.167, f32[256,4096]{1,0:T(8,128)S(1)} %copy-done, f32[32,8,32,128]{3,2,1,0:T(8,128)S(1)} %bitcast.168, f32[16,256,4096]{2,1,0:T(8,128)} %get-tuple-element.318, s32[]{:T(128)S(6)} %select_n.130), kind=kLoop, calls=%fused_computation.1.clone.1 | loop fusion | flops 3145728 | bytes 20971524 | tf_op jit(solution)/shard_map/while/body/eval_jaxpr/add | solution.py:58
  567.5 2.0 copy-done.1
  572.9 10.6 %fusion.51 = f32[256,4096]{1,0:T(8,128)S(1)} fusion(f32[32,8,32,128]{3,2,1,0:T(8,128)S(1)} %bitcast.167, f32[256,4096]{1,0:T(8,128)S(1)} %copy-done, f32[32,8,32,128]{3,2,1,0:T(8,128)S(1)} %bitcast.168, f32[16,256,4096]{2,1,0:T(8,128)} %get-tuple-element.318, s32[]{:T(128)S(6)} %select_n.130), kind=kLoop, calls=%fused_computation.1.clone.1 | loop fusion | flops 3145728 | bytes 20971524 | tf_op jit(solution)/shard_map/while/body/eval_jaxpr/add | solution.py:58
  583.5 2.0 copy-done.1
  588.9 10.6 %fusion.51 = f32[256,4096]{1,0:T(8,128)S(1)} fusion(f32[32,8,32,128]{3,2,1,0:T(8,128)S(1)} %bitcast.167, f32[256,4096]{1,0:T(8,128)S(1)} %copy-done, f32[32,8,32,128]{3,2,1,0:T(8,128)S(1)} %bitcast.168, f32[16,256,4096]{2,1,0:T(8,128)} %get-tuple-element.318, s32[]{:T(128)S(6)} %select_n.130), kind=kLoop, calls=%fused_computation.1.clone.1 | loop fusion | flops 3145728 | bytes 20971524 | tf_op jit(solution)/shard_map/while/body/eval_jaxpr/add | solution.py:58
  599.6 2.0 copy-done.1
  605.0 10.6 %fusion.51 = f32[256,4096]{1,0:T(8,128)S(1)} fusion(f32[32,8,32,128]{3,2,1,0:T(8,128)S(1)} %bitcast.167, f32[256,4096]{1,0:T(8,128)S(1)} %copy-done, f32[32,8,32,128]{3,2,1,0:T(8,128)S(1)} %bitcast.168, f32[16,256,4096]{2,1,0:T(8,128)} %get-tuple-element.318, s32[]{:T(128)S(6)} %select_n.130), kind=kLoop, calls=%fused_computation.1.clone.1 | loop fusion | flops 3145728 | bytes 20971524 | tf_op jit(solution)/shard_map/while/body/eval_jaxpr/add | solution.py:58
  615.7 2.0 copy-done.1
  621.1 10.6 %fusion.51 = f32[256,4096]{1,0:T(8,128)S(1)} fusion(f32[32,8,32,128]{3,2,1,0:T(8,128)S(1)} %bitcast.167, f32[256,4096]{1,0:T(8,128)S(1)} %copy-done, f32[32,8,32,128]{3,2,1,0:T(8,128)S(1)} %bitcast.168, f32[16,256,4096]{2,1,0:T(8,128)} %get-tuple-element.318, s32[]{:T(128)S(6)} %select_n.130), kind=kLoop, calls=%fused_computation.1.clone.1 | loop fusion | flops 3145728 | bytes 20971524 | tf_op jit(solution)/shard_map/while/body/eval_jaxpr/add | solution.py:58
  631.7 2.0 copy-done.1
  636.0 1.1 mul.143
  637.1 10.6 %fusion.51 = f32[256,4096]{1,0:T(8,128)S(1)} fusion(f32[32,8,32,128]{3,2,1,0:T(8,128)S(1)} %bitcast.167, f32[256,4096]{1,0:T(8,128)S(1)} %copy-done, f32[32,8,32,128]{3,2,1,0:T(8,128)S(1)} %bitcast.168, f32[16,256,4096]{2,1,0:T(8,128)} %get-tuple-element.318, s32[]{:T(128)S(6)} %select_n.130), kind=kLoop, calls=%fused_computation.1.clone.1 | loop fusion | flops 3145728 | bytes 20971524 | tf_op jit(solution)/shard_map/while/body/eval_jaxpr/add | solution.py:58
  647.8 2.0 copy-done.1
  652.0 1.1 mul.143
  653.2 10.6 %fusion.51 = f32[256,4096]{1,0:T(8,128)S(1)} fusion(f32[32,8,32,128]{3,2,1,0:T(8,128)S(1)} %bitcast.167, f32[256,4096]{1,0:T(8,128)S(1)} %copy-done, f32[32,8,32,128]{3,2,1,0:T(8,128)S(1)} %bitcast.168, f32[16,256,4096]{2,1,0:T(8,128)} %get-tuple-element.318, s32[]{:T(128)S(6)} %select_n.130), kind=kLoop, calls=%fused_computation.1.clone.1 | loop fusion | flops 3145728 | bytes 20971524 | tf_op jit(solution)/shard_map/while/body/eval_jaxpr/add | solution.py:58
  663.9 2.0 copy-done.1
  669.3 10.6 %fusion.51 = f32[256,4096]{1,0:T(8,128)S(1)} fusion(f32[32,8,32,128]{3,2,1,0:T(8,128)S(1)} %bitcast.167, f32[256,4096]{1,0:T(8,128)S(1)} %copy-done, f32[32,8,32,128]{3,2,1,0:T(8,128)S(1)} %bitcast.168, f32[16,256,4096]{2,1,0:T(8,128)} %get-tuple-element.318, s32[]{:T(128)S(6)} %select_n.130), kind=kLoop, calls=%fused_computation.1.clone.1 | loop fusion | flops 3145728 | bytes 20971524 | tf_op jit(solution)/shard_map/while/body/eval_jaxpr/add | solution.py:58
  679.9 2.0 copy-done.1
  685.3 10.6 %fusion.51 = f32[256,4096]{1,0:T(8,128)S(1)} fusion(f32[32,8,32,128]{3,2,1,0:T(8,128)S(1)} %bitcast.167, f32[256,4096]{1,0:T(8,128)S(1)} %copy-done, f32[32,8,32,128]{3,2,1,0:T(8,128)S(1)} %bitcast.168, f32[16,256,4096]{2,1,0:T(8,128)} %get-tuple-element.318, s32[]{:T(128)S(6)} %select_n.130), kind=kLoop, calls=%fused_computation.1.clone.1 | loop fusion | flops 3145728 | bytes 20971524 | tf_op jit(solution)/shard_map/while/body/eval_jaxpr/add | solution.py:58
  696.0 2.0 copy-done.1
  701.4 10.6 %fusion.51 = f32[256,4096]{1,0:T(8,128)S(1)} fusion(f32[32,8,32,128]{3,2,1,0:T(8,128)S(1)} %bitcast.167, f32[256,4096]{1,0:T(8,128)S(1)} %copy-done, f32[32,8,32,128]{3,2,1,0:T(8,128)S(1)} %bitcast.168, f32[16,256,4096]{2,1,0:T(8,128)} %get-tuple-element.318, s32[]{:T(128)S(6)} %select_n.130), kind=kLoop, calls=%fused_computation.1.clone.1 | loop fusion | flops 3145728 | bytes 20971524 | tf_op jit(solution)/shard_map/while/body/eval_jaxpr/add | solution.py:58
  712.0 2.0 copy-done.1
  717.4 10.6 %fusion.51 = f32[256,4096]{1,0:T(8,128)S(1)} fusion(f32[32,8,32,128]{3,2,1,0:T(8,128)S(1)} %bitcast.167, f32[256,4096]{1,0:T(8,128)S(1)} %copy-done, f32[32,8,32,128]{3,2,1,0:T(8,128)S(1)} %bitcast.168, f32[16,256,4096]{2,1,0:T(8,128)} %get-tuple-element.318, s32[]{:T(128)S(6)} %select_n.130), kind=kLoop, calls=%fused_computation.1.clone.1 | loop fusion | flops 3145728 | bytes 20971524 | tf_op jit(solution)/shard_map/while/body/eval_jaxpr/add | solution.py:58
  728.1 2.0 copy-done.1
  734.3 10.4 %fusion.15 = bf16[256,512]{1,0:T(8,128)(2,1)} fusion(bf16[4096,512]{1,0:T(8,128)(2,1)} %param.19, f32[32,8,32,128]{3,2,1,0:T(8,128)S(1)} %bitcast.179, f32[256,4096]{1,0:T(8,128)S(1)} %copy-done.8, f32[32,8,32,128]{3,2,1,0:T(8,128)S(1)} %bitcast.178, f32[256,4096]{1,0:T(8,128)S(1)} %copy-done.2, f32[32,8,32,128]{3,2,1,0:T(8,128)S(1)} %bitcast.177), kind=kOutput, calls=%fused_computation.39 | convolution fusion | flops 1079115776 | bytes 25427968 | tf_op jit(solution)/shard_map/dot_general | solution.py:108
  744.7 2.3 div.50
  747.1 11.3 %fusion.7 = bf16[512,4096]{1,0:T(8,128)(2,1)} fusion(f32[512,4096]{1,0:T(8,128)} %copy.60, f32[64,8,32,128]{3,2,1,0:T(8,128)S(1)} %bitcast.169, pred[512]{0:T(512)(128)(4,1)S(1)} %copy-done.15), kind=kLoop, calls=%fused_computation.23 | loop fusion | flops 6291456 | bytes 20972032 | tf_op jit(solution)/shard_map/convert_element_type | solution.py:92
  (194 shorter events, 57.4 us)
Async XLA Ops:
  7.2 125.6 %all-reduce.3.cloned.1.call-start = ((), (), s32[]{:S(2)}) async-start(), calls=%async_computation.3 | async-start | bytes 7340032 | tf_op jit(solution)/shard_map/psum | solution.py:16
  9.7 12.1 %copy-start.6 = (bf16[512,512]{0,1:T(8,128)(2,1)}, bf16[512,512]{0,1:T(8,128)(2,1)S(1)}, u32[]{:S(2)}) copy-start(bf16[512,512]{0,1:T(8,128)(2,1)S(1)} %copy.54) | copy-start | bytes 1572868
  18.3 4.9 copy-start.16
  21.9 462.4 %all-gather.2.cloned.1.call-start = ((), (), s32[]{:S(2)}) async-start(), calls=%async_computation.1 | async-start | bytes 71303168 | tf_op jit(solution)/shard_map/all_gather | solution.py:20
  24.2 132.3 %copy-start.14 = (pred[512]{0:T(512)(128)(4,1)}, pred[512]{0:T(512)(128)(4,1)S(1)}, u32[]{:S(2)}) copy-start(pred[512]{0:T(512)(128)(4,1)S(1)} %iota_compare_fusion.3) | copy-start | bytes 1540
  136.7 7.4 copy-start.4
  149.8 608.5 %reduce-scatter.2.cloned.1.call-start = ((), (), s32[]{:S(2)}) async-start(), calls=%async_computation.2 | async-start | bytes 393216 | tf_op jit(solution)/shard_map/reduce_scatter | solution.py:109
  156.5 58.3 %copy-start.5 = (bf16[256,4,8,128]{3,0,2,1:T(8,128)(2,1)S(1)}, bf16[256,4,8,128]{3,0,2,1:T(8,128)(2,1)}, u32[]{:S(2)}) copy-start(bf16[256,4,8,128]{3,0,2,1:T(8,128)(2,1)} %get-tuple-element.213) | copy-start | bytes 6291460
  190.6 0.8 copy-start.9
  213.8 0.9 copy-start.10
  214.8 5.6 copy-start.13
  217.1 3.2 copy-start.3
  220.4 9.9 %copy-start.7 = (bf16[512,512]{0,1:T(8,128)(2,1)S(1)}, bf16[512,512]{0,1:T(8,128)(2,1)}, u32[]{:S(2)}) copy-start(bf16[512,512]{0,1:T(8,128)(2,1)} %copy-done.6) | copy-start | bytes 1572868
  220.4 9.9 %copy-start.12 = (bf16[512,512]{0,1:T(8,128)(2,1)S(1)}, bf16[512,512]{0,1:T(8,128)(2,1)}, u32[]{:S(2)}) copy-start(bf16[512,512]{0,1:T(8,128)(2,1)} %get-tuple-element.212) | copy-start | bytes 1572868
  265.7 23.1 %copy-start.11 = (bf16[512,512]{0,1:T(8,128)(2,1)S(1)}, bf16[512,512]{0,1:T(8,128)(2,1)}, u32[]{:S(2)}) copy-start(bf16[512,512]{0,1:T(8,128)(2,1)} %get-tuple-element.211) | copy-start | bytes 1572868
  490.1 2.4 copy-start
  503.2 2.0 copy-start.1
  506.2 2.4 copy-start
  519.3 2.0 copy-start.1
  522.3 2.4 copy-start
  535.3 2.0 copy-start.1
  538.3 2.4 copy-start
  551.4 2.0 copy-start.1
  554.4 2.4 copy-start
  567.5 2.0 copy-start.1
  570.5 2.4 copy-start
  583.5 2.0 copy-start.1
  586.5 2.4 copy-start
  599.6 2.0 copy-start.1
  602.6 2.4 copy-start
  615.6 2.0 copy-start.1
  618.6 2.4 copy-start
  631.7 2.0 copy-start.1
  634.7 2.4 copy-start
  647.8 2.0 copy-start.1
  650.8 2.4 copy-start
  663.8 2.0 copy-start.1
  666.8 2.4 copy-start
  679.9 2.0 copy-start.1
  682.9 2.4 copy-start
  696.0 2.0 copy-start.1
  699.0 2.4 copy-start
  712.0 2.0 copy-start.1
  715.0 2.4 copy-start
  728.1 2.0 copy-start.1
  730.8 3.5 copy-start.2
  730.8 3.5 copy-start.8
  744.7 2.3 copy-start.15
Sparse Core Ops, SparseCore 0:
  22.0 110.7 all-reduce.2
  150.0 334.2 all-gather.1
  744.9 12.4 reduce-scatter.1
where the time goes:
time: 773 us; the launch traced here: 765 us
  waiting for transfers between devices  260 us (34%)
  other arithmetic  214 us (28%)
  local copies, waits for them, and re-layouts  135 us (17%)
  matrix products  93.7 us (12%)
  blocking collectives  47.3 us (6%)
  between operations  15.2 us (2%)
    add x15, other arithmetic, combine(): first_piece[2].reshape(rows, heads, -1) * scale_one[..., None]  160 us
    all_gather x1, waiting for transfers between devices, combined_all(): everything = jax.tree.map(lambda part: lax.all_gather(part, axis), array)  151 us
    psum x1, waiting for transfers between devices, broadcast(): return lax.psum(block, axis)  109 us
    all_gather x2, blocking collectives, combined_all(): everything = jax.tree.map(lambda part: lax.all_gather(part, axis), array)  47.3 us
    dot_general x3, matrix products, partial_attend(): jnp.einsum('rkgs,skd->rkgd', weights, value_heads, preferred_element_type...  41.7 us
    dot_general x3, matrix products, partial_attend(): jnp.einsum('rkgd,skd->rkgs', query_heads, key_heads, preferred_element_ty...  41.6 us
    reduce_sum x3, other arithmetic, partial_attend(): totals = jnp.sum(weights.astype(jnp.float32), axis=-1)  37.2 us
    while x60, local copies, waits for them, and re-layouts  30.2 us
  transfers between devices with their start and end apart: 3, of which 2 were waited for; matrix products, arithmetic and copies ran while one was open for 19% of the time, Pallas kernels for 0%

commit v1 on v0

--- a/solution.py
+++ b/solution.py
@@ -1,11 +1,18 @@
+import functools
 import math
 
 import jax
 import jax.numpy as jnp
 from jax import lax
+from jax.experimental import pallas as pl
+from jax.experimental.pallas import tpu as pltpu
 from jax.sharding import PartitionSpec as P
 
 HEAD_SIZE = 128
+F32 = jnp.float32
+BF16 = jnp.bfloat16
+LOG_SCALE = math.log2(math.e) / math.sqrt(HEAD_SIZE)
+VMEM_LIMIT = 56 * 2**20
 
 
 masked_score = -1e30
@@ -61,7 +68,7 @@
     return (top, totals, outputs.reshape(rows, -1))
 
 
-def body(
+def generic_body(
     ctx_query,
     ctx_key,
     context_value,
@@ -112,6 +119,296 @@
     return (pieces, layer_out)
 
 
+def dot_t(a, b):
+    return lax.dot_general(a, b, (((1,), (1,)), ((), ())), preferred_element_type=F32)
+
+
+def swap(array, bit):
+    return lax.ppermute(array, "hst", [(i, i ^ bit) for i in range(16)])
+
+
+def call(kernel, out_shape, in_specs, out_specs, grid=(), scratch=(), prefetch=1, flops=0, data=0, aliases=None):
+    return pl.pallas_call(
+        kernel,
+        grid_spec=pltpu.PrefetchScalarGridSpec(
+            num_scalar_prefetch=prefetch, grid=grid, in_specs=in_specs, out_specs=out_specs, scratch_shapes=list(scratch)
+        ),
+        out_shape=out_shape,
+        input_output_aliases=aliases or {},
+        compiler_params=pltpu.CompilerParams(vmem_limit_bytes=VMEM_LIMIT),
+        cost_estimate=pl.CostEstimate(flops=flops, bytes_accessed=data, transcendentals=0),
+    )
+
+
+WHOLE = pl.BlockSpec(memory_space=pltpu.VMEM)
+
+
+def rows_of(ref, c):
+    parts = [ref[0, pl.ds(pl.multiple_of(x * 128 + c * 64, 64), 64), :] for x in range(2)]
+    return jnp.concatenate(parts, axis=0)
+
+
+def ask_pack_kernel(at, q_ref, k_ref, v_ref, out_ref):
+    other = 1 - at[2]
+    out_ref[:, 0:4096] = rows_of(q_ref, other)
+    out_ref[:, 4096:4608] = rows_of(k_ref, other)
+    out_ref[:, 4608:5120] = rows_of(v_ref, other)
+
+
+def kv_pack_kernel(at, k_ref, v_ref, *out_refs):
+    for s, out_ref in enumerate(out_refs):
+        head = pl.ds(pl.multiple_of((at[0] ^ s) * 128, 128), 128)
+        out_ref[0:512, :] = k_ref[:, head]
+        out_ref[512:1024, :] = v_ref[:, head]
+
+
+def x_pack_kernel(at, got_ref, q_ref, k_ref, v_ref, keep_ref, send_ref):
+    x, c, owner_c = at[1], at[2], at[6]
+
+    def write(ask_q, ask_kv):
+        for ref, row_half in ((keep_ref, x), (send_ref, 1 - x)):
+            ref[0:64, :] = ask_q(row_half)
+            for i in range(4):
+                ref[64:96, i * 1024 : (i + 1) * 1024] = ask_kv(i)
+
+    def own_kv(i):
+        rows = pl.ds(pl.multiple_of((i // 2) * 128 + c * 64 + (i % 2) * 32, 32), 32)
+        return jnp.concatenate([k_ref[0, rows, :], v_ref[0, rows, :]], axis=1)
+
+    @pl.when(owner_c == c)
+    def _():
+        write(lambda half: q_ref[0, pl.ds(pl.multiple_of(half * 128 + c * 64, 64), 64), :], own_kv)
+
+    @pl.when(owner_c != c)
+    def _():
+        write(
+            lambda half: got_ref[pl.ds(pl.multiple_of(half * 64, 64), 64), 0:4096],
+            lambda i: got_ref[i * 32 : (i + 1) * 32, 4096:5120],
+        )
+
+
+def z_pack_kernel(at, keep_ref, got_ref, *out_refs):
+    z, x, owner_x = at[0], at[1], at[5]
+
+    def write(ref):
+        for s, out_ref in enumerate(out_refs):
+            j = z ^ s
+            out_ref[0:64, :] = ref[0:64, pl.ds(pl.multiple_of(j * 1024, 1024), 1024)]
+            for i in range(4):
+                for part in range(2):
+                    lanes = pl.ds(pl.multiple_of(i * 1024 + part * 512 + j * 128, 128), 128)
+                    out_ref[64:96, i * 256 + part * 128 : i * 256 + (part + 1) * 128] = ref[64:96, lanes]
+
+    @pl.when(owner_x == x)
+    def _():
+        write(keep_ref)
+
+    @pl.when(owner_x != x)
+    def _():
+        write(got_ref)
+
+
+def pick_kernel(at, *refs):
+    out_ref = refs[-1]
+    for s in range(4):
+        @pl.when((at[0] ^ at[4]) == s)
+        def _(s=s):
+            out_ref[...] = refs[s][...]
+
+
+def ones_beside(values):
+    return jnp.concatenate([values, jnp.ones(values.shape, values.dtype)], axis=1)
+
+
+def read_kernel(at, own_ref, other_ref, *refs):
+    kv_refs, (mine_ref, send_ref, s_ref) = refs[:8], refs[8:]
+    z, x, c = at[0], at[1], at[2]
+    column = lax.broadcasted_iota(jnp.int32, (1, 512), 1)
+    step = pl.program_id(0)
+    ask_ref_is_own = step < 2
+    lane0 = pl.multiple_of((step % 2) * 512, 512)
+
+    def rows(ref):
+        q = ref[0:64, pl.ds(lane0, 512)]
+        return jnp.concatenate([q[:, h * 128 : (h + 1) * 128] for h in range(4)], axis=0)
+
+    q = jnp.where(ask_ref_is_own, rows(own_ref), rows(other_ref))
+    row_c = jnp.where(ask_ref_is_own, c, 1 - c)
+    peak = None
+    for i, kv_ref in enumerate(kv_refs):
+        xz = (x ^ (i // 4)) * 2 + (z ^ (i % 4)) * 4 + c
+        s = jnp.where(column < at[8 + xz], dot_t(q, kv_ref[0:512, :]), masked_score)
+        s_ref[:, i * 512 : (i + 1) * 512] = s
+        for k in range(4):
+            part = s[:, k * 128 : (k + 1) * 128]
+            peak = part if peak is None else jnp.maximum(peak, part)
+    ask_k = jnp.concatenate([own_ref[64:96, i * 256 : i * 256 + 128] for i in range(4)], axis=0)
+    ask_v = jnp.concatenate([own_ref[64:96, i * 256 + 128 : (i + 1) * 256] for i in range(4)], axis=0)
+    key_at = lax.broadcasted_iota(jnp.int32, (256, 128), 1)
+    key_at = (key_at // 64) * 128 + c * 64 + key_at % 64
+    row_at = lax.broadcasted_iota(jnp.int32, (256, 128), 0) % 64 + x * 128 + row_c * 64
+    s_self = jnp.where(key_at <= row_at, dot_t(q, ask_k), masked_score)
+    peak = jnp.max(jnp.maximum(peak, s_self), axis=1, keepdims=True) * LOG_SCALE
+    total = jnp.dot(
+        jnp.exp2(s_self * LOG_SCALE - peak).astype(BF16), ones_beside(ask_v), preferred_element_type=F32
+    )
+    for i, kv_ref in enumerate(kv_refs):
+        w = jnp.exp2(s_ref[:, i * 512 : (i + 1) * 512] * LOG_SCALE - peak).astype(BF16)
+        total = total + jnp.dot(w, ones_beside(kv_ref[512:1024, :]), preferred_element_type=F32)
+    weight = total[:, 128:]
+    result = jnp.concatenate([total[:, :128] / weight, peak + jnp.log2(weight)], axis=1)
+    at_row = pl.ds(pl.multiple_of((step % 2) * 256, 256), 256)
+
+    @pl.when(ask_ref_is_own)
+    def _():
+        mine_ref[at_row, :] = result
+
+    @pl.when(jnp.logical_not(ask_ref_is_own))
+    def _():
+        send_ref[at_row, :] = result
+
+
+def merge_kernel(at, mine_ref, got_ref, out_ref):
+    top = jnp.maximum(mine_ref[:, 128:], got_ref[:, 128:])
+    one, two = jnp.exp2(mine_ref[:, 128:] - top), jnp.exp2(got_ref[:, 128:] - top)
+    answer = ((one * mine_ref[:, :128] + two * got_ref[:, :128]) / (one + two)).astype(BF16)
+    for h in range(8):
+        out_ref[:, h * 128 : (h + 1) * 128] = answer[h * 64 : (h + 1) * 64, :]
+
+
+def project_kernel(at, *refs):
+    parts, w_ref, keep_ref, send_ref, sum_ref = refs[:16], refs[16], refs[17], refs[18], refs[19]
+    z, x, c, t = at[0], at[1], at[2], at[3]
+    for s in range(4):
+        w = w_ref[pl.ds(pl.multiple_of((z ^ s) * 1024, 1024), 1024), :]
+        a = jnp.concatenate([parts[s * 4 + r][...] for r in range(4)], axis=0)
+        product = jnp.dot(a, w, preferred_element_type=F32)
+        if s == 0:
+            sum_ref[...] = product
+        else:
+            sum_ref[...] += product
+    for r in range(4):
+        half, core = x ^ (r // 2), c ^ (r % 2)
+        at_row = pl.ds(pl.multiple_of(core * 64, 64), 64)
+        quarter = sum_ref[r * 64 : (r + 1) * 64, :]
+
+        @pl.when(half == t)
+        def _(quarter=quarter, at_row=at_row):
+            keep_ref[at_row, :] = quarter
+
+        @pl.when(half != t)
+        def _(quarter=quarter, at_row=at_row):
+            send_ref[at_row, :] = quarter.astype(BF16)
+
+
+def encode_kernel(at, q_ref, k_ref, v_ref, ak_ref, av_ref, *rest):
+    o_ref = rest[-1]
+    row = lax.broadcasted_iota(jnp.int32, (256, 256), 0)
+    column = lax.broadcasted_iota(jnp.int32, (256, 256), 1)
+    anchor_len = jnp.where(at[7] > 0, at[8], 0)
+    anchor_ok = lax.broadcasted_iota(jnp.int32, (1, 512), 1) < anchor_len
+    own_len = at[8 + at[7]]
+    anchor_v = ones_beside(av_ref[...])
+    own_v = [ones_beside(v_ref[r * 256 : (r + 1) * 256, :]) for r in range(2)]
+    for h in range(8):
+        lanes = slice(h * 128, (h + 1) * 128)
+        for r in range(2):
+            here = slice(r * 256, (r + 1) * 256)
+            q = q_ref[here, lanes]
+            scores = [jnp.where(anchor_ok, dot_t(q, ak_ref[...]), masked_score)]
+            values = [anchor_v]
+            for b in range(r + 1):
+                s = dot_t(q, k_ref[b * 256 : (b + 1) * 256, :])
+                scores.append(jnp.where(column <= row, s, masked_score) if b == r else s)
+                values.append(own_v[b])
+            peak = functools.reduce(jnp.maximum, [s.max(axis=1, keepdims=True) for s in scores]) * LOG_SCALE
+            total = 0
+            for s, v in zip(scores, values):
+                w = jnp.exp2(s * LOG_SCALE - peak).astype(BF16)
+                total = total + jnp.dot(w, v, preferred_element_type=F32)
+            valid = lax.broadcasted_iota(jnp.int32, (256, 128), 0) + r * 256 < own_len
+            o_ref[here, lanes] = jnp.where(valid, total[:, :128] / total[:, 128:], 0.0).astype(BF16)
+
+
+def anchors(key, value, at):
+    z, x, c = at[0], at[1], at[2]
+
+    def send(array, pairs):
+        return lax.ppermute(array, "hst", pairs)
+
+    got = send(value, [(0, 1)])
+    half = jnp.where(c == 0, key, got)
+    got = send(half, [(0, 2), (1, 3)])
+    half = jnp.where(x == 0, half, got)
+    got = send(half, [(i, i + 8) for i in range(4)])
+    half = jnp.where(z == 0, half, got)
+    got = send(half, [(i, i + 4) for i in (0, 1, 2, 3, 8, 9, 10, 11)])
+    half = jnp.where(z % 2 == 0, half, got)
+    got = swap(half, 1)
+    return jnp.where(c == 0, half, got), jnp.where(c == 0, got, half)
+
+
+def body(ctx_query, ctx_key, context_value, lengths, owner, ask_query, ask_key, candidate_value_rows, out_weight):
+    host, t = lax.axis_index("hst"), lax.axis_index("tensor")
+    own = owner[0]
+    at = jnp.concatenate([
+        jnp.stack([host // 4, host // 2 % 2, host % 2, t, own // 4, own // 2 % 2, own % 2, host]).astype(jnp.int32),
+        lengths,
+    ])
+    shape = jax.ShapeDtypeStruct
+
+    packed = call(ask_pack_kernel, shape((128, 5120), BF16), [WHOLE] * 3, WHOLE)(
+        at, ask_query, ask_key, candidate_value_rows
+    )
+    got = swap(packed, 1)
+    kv = call(kv_pack_kernel, [shape((1024, 128), BF16)] * 4, [WHOLE] * 2, [WHOLE] * 4)(at, ctx_key, context_value)
+    kv_z = [kv[0]] + [swap(kv[s], 4 * s) for s in (1, 2, 3)]
+    keep, send = call(x_pack_kernel, [shape((96, 4096), BF16)] * 2, [WHOLE] * 4, [WHOLE] * 2)(
+        at, got, ask_query, ask_key, candidate_value_rows
+    )
+    got = swap(send, 2)
+    asked = call(z_pack_kernel, [shape((96, 1024), BF16)] * 4, [WHOLE] * 2, [WHOLE] * 4)(at, keep, got)
+    asked = [asked[0]] + [swap(asked[s], 4 * s) for s in (1, 2, 3)]
+    asked = call(pick_kernel, shape((96, 1024), BF16), [WHOLE] * 4, WHOLE)(at, *asked)
+    asked_other = swap(asked, 1)
+    kv_x = [swap(part, 2) for part in kv_z]
+
+    anchor_key, anchor_value = anchors(ctx_key, context_value, at)
+
+    mine, send = call(
+        read_kernel, [shape((512, 256), F32)] * 2, [WHOLE] * 10, [WHOLE] * 2, grid=(4,),
+        scratch=[pltpu.VMEM((256, 4096), F32)], flops=2 * 2 * 1024 * 4096 * 256, data=2**21,
+    )(at, asked, asked_other, *kv_z, *kv_x)
+    got = swap(send, 1)
+    answer = call(merge_kernel, shape((64, 1024), BF16), [WHOLE] * 2, WHOLE)(at, mine, got)
+
+    across = [answer] + [swap(answer, 4 * s) for s in (1, 2, 3)]
+    sides = [swap(part, 2) for part in across]
+    here = [(across[s], sides[s]) for s in range(4)]
+    flat = jnp.stack([part for pair in here for part in pair])
+    there = swap(flat, 1)
+
+    ctx_out = None
+    for g in range(4):
+        block = pl.BlockSpec((512, 1024), lambda i, at, g=g: (0, g))
+        head = pl.BlockSpec((512, 128), lambda i, at, g=g: (0, g))
+        args = [ctx_query, ctx_key, context_value, anchor_key, anchor_value] + ([] if g == 0 else [ctx_out])
+        ctx_out = call(
+            encode_kernel, shape((512, 4096), BF16), [block] + [head] * 4 + ([] if g == 0 else [pl.BlockSpec(memory_space=pl.ANY)]),
+            block, grid=(1,), aliases={} if g == 0 else {6: 0}, flops=4 * 4096 * 1024 * 256, data=2**21,
+        )(at, *args)
+
+    parts = []
+    for s in range(4):
+        parts += [here[s][0], there[2 * s], here[s][1], there[2 * s + 1]]
+    keep, send = call(
+        project_kernel, [shape((128, 512), F32), shape((128, 512), BF16)], [WHOLE] * 17, [WHOLE] * 2,
+        scratch=[pltpu.VMEM((256, 512), F32)], flops=2 * 256 * 4096 * 512, data=2**22,
+    )(at, *parts, out_weight)
+    got = lax.ppermute(send, "tensor", [(0, 1), (1, 0)])
+    return ctx_out, (keep + got.astype(F32)).astype(BF16)
+
+
 def solution(mesh):
     placed = (
         P("hst", "tensor"),
@@ -124,8 +421,9 @@
         P("hst", None, "tensor"),
         P("tensor", "hst"),
     )
+    fits = dict(mesh.shape) == {"hst": 16, "tensor": 2}
     return jax.shard_map(
-        body,
+        body if fits else generic_body,
         mesh=mesh,
         in_specs=placed,
         out_specs=(P("hst", "tensor"), P("tensor", "hst")),

time: 773 us -> 186 us (0.24)
  waiting for transfers between devices: 260 us -> 45.8 us
  other arithmetic: 214 us -> 1.99 us
  local copies, waits for them, and re-layouts: 135 us -> 7.99 us
  matrix products: 93.7 us -> 0 us
  Pallas kernels: 0 us -> 76.8 us
  starting transfers between devices: 0.12 us -> 51.5 us
  blocking collectives: 47.3 us -> 0 us
  between operations: 15.2 us -> 1.68 us
    add x31 -> x0, other arithmetic: 161 us -> none  [the longest x15 160 us: combine(): first_piece[2].reshape(rows, heads, -1) * scale_one[..., None]]
    all_gather x1 -> x0, waiting for transfers between devices: 151 us -> none  [combined_all(): everything = jax.tree.map(lambda part: lax.all_gather(part, axis), array)]
    psum x1 -> x0, waiting for transfers between devices: 109 us -> none  [broadcast(): return lax.psum(block, axis)]
    dot_general x7 -> x0, matrix products: 93.7 us -> none  [the longest x3 41.7 us: partial_attend(): jnp.einsum('rkgs,skd->rkgd', weights, value_heads, preferred_element_type...]
    pallas_call x0 -> x12, Pallas kernels: none -> 76.8 us  [the longest x4 36.1 us: body(): call(encode_kernel, shape((512, 4096), BF16), [block] + [head] * 4 + ([]...]
    ppermute x0 -> x28, starting transfers between devices: none -> 51.5 us  [the longest x23 41.6 us: swap(): return lax.ppermute(array, 'hst', [(i, i ^ bit) for i in range(16)])]
    all_gather x2 -> x0, blocking collectives: 47.3 us -> none  [combined_all(): everything = jax.tree.map(lambda part: lax.all_gather(part, axis), array)]
    ppermute x0 -> x28, waiting for transfers between devices: none -> 45.8 us  [the longest x23 30.3 us: swap(): return lax.ppermute(array, 'hst', [(i, i ^ bit) for i in range(16)])]
  transfers between devices with their start and end apart: 3 -> 28, of which waited for: 2 -> 11; matrix products, arithmetic and copies ran while one was open for 19% -> 2% of each run, Pallas kernels for 0% -> 37%
where the time goes in v1:
time: 186 us
  Pallas kernels  76.8 us (41%)
  starting transfers between devices  51.5 us (28%)
  waiting for transfers between devices  45.8 us (25%)
  local copies, waits for them, and re-layouts  7.99 us (4%)
  other arithmetic  1.99 us (1%)
    ppermute x23, starting transfers between devices, swap(): return lax.ppermute(array, 'hst', [(i, i ^ bit) for i in range(16)])  41.6 us
    pallas_call x4, Pallas kernels, body(): call(encode_kernel, shape((512, 4096), BF16), [block] + [head] * 4 + ([]...  36.1 us
    ppermute x23, waiting for transfers between devices, swap(): return lax.ppermute(array, 'hst', [(i, i ^ bit) for i in range(16)])  30.3 us
    pallas_call x1, Pallas kernels, body(): call(read_kernel, [shape((512, 256), F32)] * 2, [WHOLE] * 10, [WHOLE] * 2...  16.1 us
    ppermute x4, waiting for transfers between devices, send(): return lax.ppermute(array, 'hst', pairs)  15.5 us
    ppermute x4, starting transfers between devices, send(): return lax.ppermute(array, 'hst', pairs)  8.35 us
    pallas_call x1, Pallas kernels, body(): call(project_kernel, [shape((128, 512), F32), shape((128, 512), BF16)], [...  5.9 us
    unnamed x53, local copies, waits for them, and re-layouts  5.74 us
  transfers between devices with their start and end apart: 28, of which 11 were waited for; matrix products, arithmetic and copies ran while one was open for 2% of the time, Pallas kernels for 37%

profile of v1, /device:TPU:0, one launch (start us, length us, event | category | flops | bytes accessed | tf_op | source)
XLA Modules:
  0.0 185.8 jit_solution(4377556796718113894)
XLA Ops:
  0.6 0.0 copy-start
  0.6 2.5 %collective-permute-start = (bf16[512,512]{1,0:T(8,128)(2,1)}, bf16[512,512]{1,0:T(8,128)(2,1)S(1)}, u32[]{:S(2)}, u32[]{:S(2)}) collective-permute-start(bf16[512,512]{1,0:T(8,128)(2,1)} %v_ref.13), channel_id=1, source_target_pairs={{0,2},{1,3}} | collective-permute-start | bytes 1572872 | tf_op jit(solution)/shard_map/ppermute | solution.py:337
  3.9 1.2 concatenate.3.at
  5.2 3.5 %shard_map.108 = bf16[128,5120]{1,0:T(8,128)(2,1)} custom-call(s32[24]{0:T(128)} %concatenate.3.at, bf16[1,256,4096]{2,1,0:T(8,128)(2,1)} %q_ref.11, bf16[1,256,512]{2,1,0:T(8,128)(2,1)} %k_ref.12, bf16[1,256,512]{2,1,0:T(8,128)(2,1)} %v_ref.12), custom_call_target="tpu_custom_call" | custom-call | tf_op jit(solution)/shard_map/pallas_call | solution.py:360
  8.7 0.1 broadcast_select_fusion.5
  8.7 3.2 %collective-permute-start.1 = (bf16[512,512]{1,0:T(8,128)(2,1)S(1)}, bf16[512,512]{1,0:T(8,128)(2,1)S(1)}, u32[]{:S(2)}, u32[]{:S(2)}) collective-permute-start(bf16[512,512]{1,0:T(8,128)(2,1)S(1)} %broadcast_select_fusion.5), channel_id=1, source_target_pairs={{0,4},{2,6},{1,5},{3,7}} | collective-permute-start | bytes 1572872 | tf_op jit(solution)/shard_map/ppermute | solution.py:337
  11.9 11.8 %collective-permute-done.1 = bf16[512,512]{1,0:T(8,128)(2,1)S(1)} collective-permute-done((bf16[512,512]{1,0:T(8,128)(2,1)S(1)}, bf16[512,512]{1,0:T(8,128)(2,1)S(1)}, u32[]{:S(2)}, u32[]{:S(2)}) %collective-permute-start.1) | collective-permute-done | bytes 524320 | tf_op jit(solution)/shard_map/ppermute | solution.py:337
  23.7 0.1 broadcast_select_fusion
  23.8 1.3 collective-permute-start.2
  25.1 0.0 copy-start.1
  25.1 1.0 copy-done.1
  26.2 4.0 %shard_map.109 = (bf16[96,4096]{1,0:T(8,128)(2,1)}, bf16[96,4096]{1,0:T(8,128)(2,1)}) custom-call(s32[24]{0:T(128)} %concatenate.3.at, bf16[128,5120]{1,0:T(8,128)(2,1)} %copy-done.1, bf16[1,256,4096]{2,1,0:T(8,128)(2,1)} %q_ref.11, bf16[1,256,512]{2,1,0:T(8,128)(2,1)} %k_ref.12, bf16[1,256,512]{2,1,0:T(8,128)(2,1)} %v_ref.12), custom_call_target="tpu_custom_call" | custom-call | tf_op jit(solution)/shard_map/pallas_call | solution.py:366
  30.2 2.5 %collective-permute-start.6 = (bf16[96,4096]{1,0:T(8,128)(2,1)}, bf16[96,4096]{1,0:T(8,128)(2,1)S(1)}, u32[]{:S(2)}, u32[]{:S(2)}) collective-permute-start(bf16[96,4096]{1,0:T(8,128)(2,1)} %get-tuple-element.17), channel_id=1, source_target_pairs={{0,4},{2,6},{4,0},{6,2},{8,12},{10,14},{12,8},{14,10},{16,20},{18,... | collective-permute-start | bytes 2359304 | tf_op jit(solution)/shard_map/ppermute | solution.py:127
  32.6 3.8 %collective-permute-done.2 = bf16[512,512]{1,0:T(8,128)(2,1)S(1)} collective-permute-done((bf16[512,512]{1,0:T(8,128)(2,1)S(1)}, bf16[512,512]{1,0:T(8,128)(2,1)S(1)}, u32[]{:S(2)}, u32[]{:S(2)}) %collective-permute-start.2) | collective-permute-done | bytes 524320 | tf_op jit(solution)/shard_map/ppermute | solution.py:337
  36.4 0.1 broadcast_select_fusion.1
  36.5 1.3 collective-permute-start.3
  37.8 3.0 %shard_map.112 = (bf16[1024,128]{1,0:T(8,128)(2,1)}, bf16[1024,128]{1,0:T(8,128)(2,1)}, bf16[1024,128]{1,0:T(8,128)(2,1)}, bf16[1024,128]{1,0:T(8,128)(2,1)}) custom-call(s32[24]{0:T(128)} %concatenate.3.at, bf16[512,512]{1,0:T(8,128)(2,1)} %k_ref.13, bf16[512,512]{1,0:T(8,128)(2,1)} %v_ref.13), custom_call_target="tpu_custom_call" | custom-call | tf_op jit(solution)/shard_map/pallas_call | solution.py:364
  40.8 3.4 %collective-permute-start.12 = (bf16[1024,128]{1,0:T(8,128)(2,1)}, bf16[1024,128]{1,0:T(8,128)(2,1)S(1)}, u32[]{:S(2)}, u32[]{:S(2)}) collective-permute-start(bf16[1024,128]{1,0:T(8,128)(2,1)} %get-tuple-element.24), channel_id=1, source_target_pairs={{0,16},{2,18},{4,20},{6,22},{8,24},{10,26},{12,28},{14,30},{16,0},... | collective-permute-start | bytes 786440 | tf_op jit(solution)/shard_map/ppermute | solution.py:127
  44.2 1.5 collective-permute-start.13
  45.7 4.6 %collective-permute-done.6.got_ref = bf16[96,4096]{1,0:T(8,128)(2,1)S(1)} collective-permute-done((bf16[96,4096]{1,0:T(8,128)(2,1)}, bf16[96,4096]{1,0:T(8,128)(2,1)S(1)}, u32[]{:S(2)}, u32[]{:S(2)}) %collective-permute-start.6) | collective-permute-done | bytes 786464 | tf_op jit(solution)/shard_map/ppermute | solution.py:127
  50.3 0.9 copy-done.2
  51.2 3.0 %shard_map.110 = (bf16[96,1024]{1,0:T(8,128)(2,1)}, bf16[96,1024]{1,0:T(8,128)(2,1)}, bf16[96,1024]{1,0:T(8,128)(2,1)}, bf16[96,1024]{1,0:T(8,128)(2,1)}) custom-call(s32[24]{0:T(128)} %concatenate.3.at, bf16[96,4096]{1,0:T(8,128)(2,1)} %get-tuple-element.16.keep_ref, bf16[96,4096]{1,0:T(8,128)(2,1)} %copy-done.2), custom_call_target="tpu_custom_call" | custom-call | tf_op jit(solution)/shard_map/pallas_call | solution.py:370
  54.2 0.0 collective-permute-start.7
  54.2 1.7 collective-permute-done.11.refs_1_
  55.8 16.7 %collective-permute-start.8 = (bf16[96,1024]{1,0:T(8,128)(2,1)}, bf16[96,1024]{1,0:T(8,128)(2,1)S(1)}, u32[]{:S(2)}, u32[]{:S(2)}) collective-permute-start(bf16[96,1024]{1,0:T(8,128)(2,1)} %get-tuple-element.20), channel_id=1, source_target_pairs={{0,16},{2,18},{4,20},{6,22},{8,24},{10,26},{12,28},{14,30},{16,0},... | collective-permute-start | bytes 589832 | tf_op jit(solution)/shard_map/ppermute | solution.py:127
  72.6 0.0 collective-permute-done.12.refs_2_
  72.6 1.9 %collective-permute-start.9 = (bf16[96,1024]{1,0:T(8,128)(2,1)}, bf16[96,1024]{1,0:T(8,128)(2,1)S(1)}, u32[]{:S(2)}, u32[]{:S(2)}) collective-permute-start(bf16[96,1024]{1,0:T(8,128)(2,1)} %get-tuple-element.21), channel_id=1, source_target_pairs={{0,24},{2,26},{4,28},{6,30},{8,16},{10,18},{12,20},{14,22},{16,8},... | collective-permute-start | bytes 589832 | tf_op jit(solution)/shard_map/ppermute | solution.py:127
  74.5 2.5 %collective-permute-start.14 = (bf16[1024,128]{1,0:T(8,128)(2,1)}, bf16[1024,128]{1,0:T(8,128)(2,1)S(1)}, u32[]{:S(2)}, u32[]{:S(2)}) collective-permute-start(bf16[1024,128]{1,0:T(8,128)(2,1)} %get-tuple-element.22.refs_0_), channel_id=1, source_target_pairs={{0,4},{2,6},{4,0},{6,2},{8,12},{10,14},{12,8},{14,10},{16,20},{18,... | collective-permute-start | bytes 786440 | tf_op jit(solution)/shard_map/ppermute | solution.py:127
  77.0 0.1 collective-permute-start.15
  77.0 4.7 %collective-permute-done.8.refs_2_ = bf16[96,1024]{1,0:T(8,128)(2,1)S(1)} collective-permute-done((bf16[96,1024]{1,0:T(8,128)(2,1)}, bf16[96,1024]{1,0:T(8,128)(2,1)S(1)}, u32[]{:S(2)}, u32[]{:S(2)}) %collective-permute-start.8) | collective-permute-done | bytes 196640 | tf_op jit(solution)/shard_map/ppermute | solution.py:127
  81.7 2.5 %collective-permute-start.16 = (bf16[1024,128]{1,0:T(8,128)(2,1)S(1)}, bf16[1024,128]{1,0:T(8,128)(2,1)S(1)}, u32[]{:S(2)}, u32[]{:S(2)}) collective-permute-start(bf16[1024,128]{1,0:T(8,128)(2,1)S(1)} %collective-permute-done.12.refs_2_), channel_id=1, source_target_pairs={{0,4},{2,6},{4,0},{6,2},{8,12},{10,14},{12,8},{14,10},{16,20},{18,... | collective-permute-start | bytes 786440 | tf_op jit(solution)/shard_map/ppermute | solution.py:127
  84.2 0.1 collective-permute-start.17
  84.3 0.6 copy-done.14
  84.9 2.6 %shard_map.111.own_ref = bf16[96,1024]{1,0:T(8,128)(2,1)} custom-call(s32[24]{0:T(128)} %concatenate.3.at, bf16[96,1024]{1,0:T(8,128)(2,1)} %get-tuple-element.18.refs_0_, bf16[96,1024]{1,0:T(8,128)(2,1)} %copy-done.12, bf16[96,1024]{1,0:T(8,128)(2,1)} %copy-done.13, bf16[96,1024]{1,0:T(8,128)(2,1)} %copy-done.14), custom_call_target="tpu_custom_call" | custom-call | tf_op jit(solution)/shard_map/pallas_call | solution.py:372
  87.4 0.1 broadcast_select_fusion.2
  87.5 0.6 collective-permute-start.4
  88.1 2.4 %collective-permute-done.16.refs_6_ = bf16[1024,128]{1,0:T(8,128)(2,1)S(1)} collective-permute-done((bf16[1024,128]{1,0:T(8,128)(2,1)S(1)}, bf16[1024,128]{1,0:T(8,128)(2,1)S(1)}, u32[]{:S(2)}, u32[]{:S(2)}) %collective-permute-start.16) | collective-permute-done | bytes 262176 | tf_op jit(solution)/shard_map/ppermute | solution.py:127
  90.5 2.8 %collective-permute-done.17.refs_7_ = bf16[1024,128]{1,0:T(8,128)(2,1)S(1)} collective-permute-done((bf16[1024,128]{1,0:T(8,128)(2,1)S(1)}, bf16[1024,128]{1,0:T(8,128)(2,1)S(1)}, u32[]{:S(2)}, u32[]{:S(2)}) %collective-permute-start.17) | collective-permute-done | bytes 262176 | tf_op jit(solution)/shard_map/ppermute | solution.py:127
  93.4 0.6 copy-done.21
  94.0 0.7 copy-done.22
  94.7 16.1 %shard_map.113 = (f32[512,256]{1,0:T(8,128)}, f32[512,256]{1,0:T(8,128)}) custom-call(s32[24]{0:T(128)} %concatenate.3.at, bf16[96,1024]{1,0:T(8,128)(2,1)} %shard_map.111.own_ref, bf16[96,1024]{1,0:T(8,128)(2,1)} %copy-done.22, bf16[1024,128]{1,0:T(8,128)(2,1)} %get-tuple-element.22.refs_0_, bf16[1024,128]{1,0:T(8,128)(2,1)} %copy-done.15, ...), custom_call_target="tpu_custom_call" | custom-call | flops 4294967296 | bytes 2097152 | tf_op jit(solution)/shard_map/pallas_call | solution.py:378
  110.8 1.1 broadcast_select_fusion.3
  111.9 1.0 collective-permute-done.18.got_ref
  112.9 0.8 copy-done.10
  113.7 2.6 %shard_map.114.refs_0_ = bf16[64,1024]{1,0:T(8,128)(2,1)} custom-call(s32[24]{0:T(128)} %concatenate.3.at, f32[512,256]{1,0:T(8,128)} %get-tuple-element.26.mine_ref, f32[512,256]{1,0:T(8,128)} %copy-done.10), custom_call_target="tpu_custom_call" | custom-call | tf_op jit(solution)/shard_map/pallas_call | solution.py:383
  116.3 1.7 collective-permute-start.19
  118.0 0.4 collective-permute-start.20
  118.4 5.4 %collective-permute-start.22 = (bf16[64,1024]{1,0:T(8,128)(2,1)}, bf16[64,1024]{1,0:T(8,128)(2,1)S(1)}, u32[]{:S(2)}, u32[]{:S(2)}) collective-permute-start(bf16[64,1024]{1,0:T(8,128)(2,1)} %shard_map.114.refs_0_), channel_id=1, source_target_pairs={{0,16},{2,18},{4,20},{6,22},{8,24},{10,26},{12,28},{14,30},{16,0},... | collective-permute-start | bytes 393224 | tf_op jit(solution)/shard_map/ppermute | solution.py:127
  123.8 1.0 bitcast_dynamic-update-slice_fusion.7
  124.8 0.3 collective-permute-start.21
  125.2 8.9 %collective-permute-done.22.refs_8_ = bf16[64,1024]{1,0:T(8,128)(2,1)S(1)} collective-permute-done((bf16[64,1024]{1,0:T(8,128)(2,1)}, bf16[64,1024]{1,0:T(8,128)(2,1)S(1)}, u32[]{:S(2)}, u32[]{:S(2)}) %collective-permute-start.22) | collective-permute-done | bytes 131104 | tf_op jit(solution)/shard_map/ppermute | solution.py:127
  134.0 0.3 collective-permute-start.23
  134.3 1.7 collective-permute-start.25
  136.2 2.8 %collective-permute-done.23.refs_10_ = bf16[64,1024]{1,0:T(8,128)(2,1)S(1)} collective-permute-done((bf16[64,1024]{1,0:T(8,128)(2,1)S(1)}, bf16[64,1024]{1,0:T(8,128)(2,1)S(1)}, u32[]{:S(2)}, u32[]{:S(2)}) %collective-permute-start.23) | collective-permute-done | bytes 131104 | tf_op jit(solution)/shard_map/ppermute | solution.py:127
  139.0 1.4 collective-permute-done.25.refs_14_
  140.4 0.1 collective-permute-start.26
  140.5 9.0 %shard_map.104.rest_0_ = bf16[512,4096]{1,0:T(8,128)(2,1)} custom-call(s32[24]{0:T(128)} %concatenate.3.at, bf16[512,4096]{1,0:T(8,128)(2,1)} %q_ref.9, bf16[512,512]{1,0:T(8,128)(2,1)} %k_ref.13, bf16[512,512]{1,0:T(8,128)(2,1)} %v_ref.13, bf16[512,512]{1,0:T(8,128)(2,1)} %get-tuple-element.39.ak_ref, bf16[512,512]{1,0:T(8,128)(2,1)} %get-tuple-element.38.av_ref), custom_call_target="tpu_custom_call" | custom-call | flops 4294967296 | bytes 2097152 | tf_op jit(solution)/shard_map/pallas_call | solution.py:396
  149.5 9.2 %shard_map.105.rest_0_ = bf16[512,4096]{1,0:T(8,128)(2,1)} custom-call(s32[24]{0:T(128)} %concatenate.3.at, bf16[512,4096]{1,0:T(8,128)(2,1)} %q_ref.9, bf16[512,512]{1,0:T(8,128)(2,1)} %k_ref.13, bf16[512,512]{1,0:T(8,128)(2,1)} %v_ref.13, bf16[512,512]{1,0:T(8,128)(2,1)} %get-tuple-element.39.ak_ref, ...), custom_call_target="tpu_custom_call", output_to_operand_aliasing={{}: (6, {})} | custom-call | flops 4294967296 | bytes 2097152 | tf_op jit(solution)/shard_map/pallas_call | solution.py:396
  158.7 9.0 %shard_map.106.rest_0_ = bf16[512,4096]{1,0:T(8,128)(2,1)} custom-call(s32[24]{0:T(128)} %concatenate.3.at, bf16[512,4096]{1,0:T(8,128)(2,1)} %q_ref.9, bf16[512,512]{1,0:T(8,128)(2,1)} %k_ref.13, bf16[512,512]{1,0:T(8,128)(2,1)} %v_ref.13, bf16[512,512]{1,0:T(8,128)(2,1)} %get-tuple-element.39.ak_ref, ...), custom_call_target="tpu_custom_call", output_to_operand_aliasing={{}: (6, {})} | custom-call | flops 4294967296 | bytes 2097152 | tf_op jit(solution)/shard_map/pallas_call | solution.py:396
  167.7 1.0 slice_bitcast_fusion
  168.7 5.9 %shard_map.115 = (f32[128,512]{1,0:T(8,128)}, bf16[128,512]{1,0:T(8,128)(2,1)}) custom-call(s32[24]{0:T(128)} %concatenate.3.at, bf16[64,1024]{1,0:T(8,128)(2,1)} %shard_map.114.refs_0_, bf16[64,1024]{1,0:T(8,128)(2,1)} %get-tuple-element.37.refs_1_, bf16[64,1024]{1,0:T(8,128)(2,1)} %copy-done.3, bf16[64,1024]{1,0:T(8,128)(2,1)} %get-tuple-element.36.refs_3_, ...), custom_call_target="tpu_custom_call" | custom-call | flops 1073741824 | bytes 4194304 | tf_op jit(solution)/shard_map/pallas_call | solution.py:404
  174.6 1.6 collective-permute-start.27
  176.1 9.0 %shard_map.107 = bf16[512,4096]{1,0:T(8,128)(2,1)} custom-call(s32[24]{0:T(128)} %concatenate.3.at, bf16[512,4096]{1,0:T(8,128)(2,1)} %q_ref.9, bf16[512,512]{1,0:T(8,128)(2,1)} %k_ref.13, bf16[512,512]{1,0:T(8,128)(2,1)} %v_ref.13, bf16[512,512]{1,0:T(8,128)(2,1)} %get-tuple-element.39.ak_ref, ...), custom_call_target="tpu_custom_call", output_to_operand_aliasing={{}: (6, {})} | custom-call | flops 4294967296 | bytes 2097152 | tf_op jit(solution)/shard_map/pallas_call | solution.py:396
  185.1 0.7 add_convert_fusion
  (66 shorter events, 0.2 us)
Async XLA Ops:
  0.6 8.0 %copy-start = (bf16[512,512]{1,0:T(8,128)(2,1)S(1)}, bf16[512,512]{1,0:T(8,128)(2,1)}, u32[]{:S(2)}) copy-start(bf16[512,512]{1,0:T(8,128)(2,1)} %k_ref.13) | copy-start | bytes 1572868
  0.6 8.0 %collective-permute-start = (bf16[512,512]{1,0:T(8,128)(2,1)}, bf16[512,512]{1,0:T(8,128)(2,1)S(1)}, u32[]{:S(2)}, u32[]{:S(2)}) collective-permute-start(bf16[512,512]{1,0:T(8,128)(2,1)} %v_ref.13), channel_id=1, source_target_pairs={{0,2},{1,3}} | collective-permute-start | bytes 1572872 | tf_op jit(solution)/shard_map/ppermute | solution.py:337
  8.7 16.5 %collective-permute-start.5 = (bf16[128,5120]{1,0:T(8,128)(2,1)}, bf16[128,5120]{1,0:T(8,128)(2,1)S(1)}, u32[]{:S(2)}, u32[]{:S(2)}) collective-permute-start(bf16[128,5120]{1,0:T(8,128)(2,1)} %shard_map.108), channel_id=1, source_target_pairs={{0,2},{2,0},{4,6},{6,4},{8,10},{10,8},{12,14},{14,12},{16,18},{18,... | collective-permute-start | bytes 3932168 | tf_op jit(solution)/shard_map/ppermute | solution.py:127
  8.7 15.0 %collective-permute-start.1 = (bf16[512,512]{1,0:T(8,128)(2,1)S(1)}, bf16[512,512]{1,0:T(8,128)(2,1)S(1)}, u32[]{:S(2)}, u32[]{:S(2)}) collective-permute-start(bf16[512,512]{1,0:T(8,128)(2,1)S(1)} %broadcast_select_fusion.5), channel_id=1, source_target_pairs={{0,4},{2,6},{1,5},{3,7}} | collective-permute-start | bytes 1572872 | tf_op jit(solution)/shard_map/ppermute | solution.py:337
  23.8 12.6 %collective-permute-start.2 = (bf16[512,512]{1,0:T(8,128)(2,1)S(1)}, bf16[512,512]{1,0:T(8,128)(2,1)S(1)}, u32[]{:S(2)}, u32[]{:S(2)}) collective-permute-start(bf16[512,512]{1,0:T(8,128)(2,1)S(1)} %broadcast_select_fusion), channel_id=1, source_target_pairs={{0,16},{2,18},{4,20},{6,22},{1,17},{3,19},{5,21},{7,23}} | collective-permute-start | bytes 1572872 | tf_op jit(solution)/shard_map/ppermute | solution.py:337
  25.1 1.1 copy-start.1
  30.2 20.1 %collective-permute-start.6 = (bf16[96,4096]{1,0:T(8,128)(2,1)}, bf16[96,4096]{1,0:T(8,128)(2,1)S(1)}, u32[]{:S(2)}, u32[]{:S(2)}) collective-permute-start(bf16[96,4096]{1,0:T(8,128)(2,1)} %get-tuple-element.17), channel_id=1, source_target_pairs={{0,4},{2,6},{4,0},{6,2},{8,12},{10,14},{12,8},{14,10},{16,20},{18,... | collective-permute-start | bytes 2359304 | tf_op jit(solution)/shard_map/ppermute | solution.py:127
  36.5 51.0 %collective-permute-start.3 = (bf16[512,512]{1,0:T(8,128)(2,1)S(1)}, bf16[512,512]{1,0:T(8,128)(2,1)S(1)}, u32[]{:S(2)}, u32[]{:S(2)}) collective-permute-start(bf16[512,512]{1,0:T(8,128)(2,1)S(1)} %broadcast_select_fusion.1), channel_id=1, source_target_pairs={{0,8},{2,10},{4,12},{6,14},{16,24},{18,26},{20,28},{22,30},{1,9},{... | collective-permute-start | bytes 1572872 | tf_op jit(solution)/shard_map/ppermute | solution.py:337
  40.8 15.0 %collective-permute-start.11 = (bf16[1024,128]{1,0:T(8,128)(2,1)}, bf16[1024,128]{1,0:T(8,128)(2,1)S(1)}, u32[]{:S(2)}, u32[]{:S(2)}) collective-permute-start(bf16[1024,128]{1,0:T(8,128)(2,1)} %get-tuple-element.23), channel_id=1, source_target_pairs={{0,8},{2,10},{4,12},{6,14},{8,0},{10,2},{12,4},{14,6},{16,24},{18,... | collective-permute-start | bytes 786440 | tf_op jit(solution)/shard_map/ppermute | solution.py:127
  40.8 31.8 %collective-permute-start.12 = (bf16[1024,128]{1,0:T(8,128)(2,1)}, bf16[1024,128]{1,0:T(8,128)(2,1)S(1)}, u32[]{:S(2)}, u32[]{:S(2)}) collective-permute-start(bf16[1024,128]{1,0:T(8,128)(2,1)} %get-tuple-element.24), channel_id=1, source_target_pairs={{0,16},{2,18},{4,20},{6,22},{8,24},{10,26},{12,28},{14,30},{16,0},... | collective-permute-start | bytes 786440 | tf_op jit(solution)/shard_map/ppermute | solution.py:127
  44.2 30.3 %collective-permute-start.13 = (bf16[1024,128]{1,0:T(8,128)(2,1)}, bf16[1024,128]{1,0:T(8,128)(2,1)S(1)}, u32[]{:S(2)}, u32[]{:S(2)}) collective-permute-start(bf16[1024,128]{1,0:T(8,128)(2,1)} %get-tuple-element.25), channel_id=1, source_target_pairs={{0,24},{2,26},{4,28},{6,30},{8,16},{10,18},{12,20},{14,22},{16,8},... | collective-permute-start | bytes 786440 | tf_op jit(solution)/shard_map/ppermute | solution.py:127
  50.3 0.9 copy-start.2
  54.2 22.8 %collective-permute-start.7 = (bf16[96,1024]{1,0:T(8,128)(2,1)}, bf16[96,1024]{1,0:T(8,128)(2,1)S(1)}, u32[]{:S(2)}, u32[]{:S(2)}) collective-permute-start(bf16[96,1024]{1,0:T(8,128)(2,1)} %get-tuple-element.19), channel_id=1, source_target_pairs={{0,8},{2,10},{4,12},{6,14},{8,0},{10,2},{12,4},{14,6},{16,24},{18,... | collective-permute-start | bytes 589832 | tf_op jit(solution)/shard_map/ppermute | solution.py:127
  55.8 37.5 %copy-start.15 = (bf16[1024,128]{1,0:T(8,128)(2,1)}, bf16[1024,128]{1,0:T(8,128)(2,1)S(1)}, u32[]{:S(2)}) copy-start(bf16[1024,128]{1,0:T(8,128)(2,1)S(1)} %collective-permute-done.11.refs_1_) | copy-start | bytes 786436
  55.8 25.9 %collective-permute-start.8 = (bf16[96,1024]{1,0:T(8,128)(2,1)}, bf16[96,1024]{1,0:T(8,128)(2,1)S(1)}, u32[]{:S(2)}, u32[]{:S(2)}) collective-permute-start(bf16[96,1024]{1,0:T(8,128)(2,1)} %get-tuple-element.20), channel_id=1, source_target_pairs={{0,16},{2,18},{4,20},{6,22},{8,24},{10,26},{12,28},{14,30},{16,0},... | collective-permute-start | bytes 589832 | tf_op jit(solution)/shard_map/ppermute | solution.py:127
  72.6 20.7 %copy-start.16 = (bf16[1024,128]{1,0:T(8,128)(2,1)}, bf16[1024,128]{1,0:T(8,128)(2,1)S(1)}, u32[]{:S(2)}) copy-start(bf16[1024,128]{1,0:T(8,128)(2,1)S(1)} %collective-permute-done.12.refs_2_) | copy-start | bytes 786436
  72.6 11.6 %collective-permute-start.9 = (bf16[96,1024]{1,0:T(8,128)(2,1)}, bf16[96,1024]{1,0:T(8,128)(2,1)S(1)}, u32[]{:S(2)}, u32[]{:S(2)}) collective-permute-start(bf16[96,1024]{1,0:T(8,128)(2,1)} %get-tuple-element.21), channel_id=1, source_target_pairs={{0,24},{2,26},{4,28},{6,30},{8,16},{10,18},{12,20},{14,22},{16,8},... | collective-permute-start | bytes 589832 | tf_op jit(solution)/shard_map/ppermute | solution.py:127
  74.5 18.8 %copy-start.17 = (bf16[1024,128]{1,0:T(8,128)(2,1)}, bf16[1024,128]{1,0:T(8,128)(2,1)S(1)}, u32[]{:S(2)}) copy-start(bf16[1024,128]{1,0:T(8,128)(2,1)S(1)} %collective-permute-done.13.refs_3_) | copy-start | bytes 786436
  74.5 13.0 %collective-permute-start.14 = (bf16[1024,128]{1,0:T(8,128)(2,1)}, bf16[1024,128]{1,0:T(8,128)(2,1)S(1)}, u32[]{:S(2)}, u32[]{:S(2)}) collective-permute-start(bf16[1024,128]{1,0:T(8,128)(2,1)} %get-tuple-element.22.refs_0_), channel_id=1, source_target_pairs={{0,4},{2,6},{4,0},{6,2},{8,12},{10,14},{12,8},{14,10},{16,20},{18,... | collective-permute-start | bytes 786440 | tf_op jit(solution)/shard_map/ppermute | solution.py:127
  77.0 7.3 %copy-start.12 = (bf16[96,1024]{1,0:T(8,128)(2,1)}, bf16[96,1024]{1,0:T(8,128)(2,1)S(1)}, u32[]{:S(2)}) copy-start(bf16[96,1024]{1,0:T(8,128)(2,1)S(1)} %collective-permute-done.7.refs_1_) | copy-start | bytes 589828
  77.0 11.1 %collective-permute-start.15 = (bf16[1024,128]{1,0:T(8,128)(2,1)S(1)}, bf16[1024,128]{1,0:T(8,128)(2,1)S(1)}, u32[]{:S(2)}, u32[]{:S(2)}) collective-permute-start(bf16[1024,128]{1,0:T(8,128)(2,1)S(1)} %collective-permute-done.11.refs_1_), channel_id=1, source_target_pairs={{0,4},{2,6},{4,0},{6,2},{8,12},{10,14},{12,8},{14,10},{16,20},{18,... | collective-permute-start | bytes 786440 | tf_op jit(solution)/shard_map/ppermute | solution.py:127
  81.7 2.6 %copy-start.13 = (bf16[96,1024]{1,0:T(8,128)(2,1)}, bf16[96,1024]{1,0:T(8,128)(2,1)S(1)}, u32[]{:S(2)}) copy-start(bf16[96,1024]{1,0:T(8,128)(2,1)S(1)} %collective-permute-done.8.refs_2_) | copy-start | bytes 589828
  81.7 8.8 %collective-permute-start.16 = (bf16[1024,128]{1,0:T(8,128)(2,1)S(1)}, bf16[1024,128]{1,0:T(8,128)(2,1)S(1)}, u32[]{:S(2)}, u32[]{:S(2)}) collective-permute-start(bf16[1024,128]{1,0:T(8,128)(2,1)S(1)} %collective-permute-done.12.refs_2_), channel_id=1, source_target_pairs={{0,4},{2,6},{4,0},{6,2},{8,12},{10,14},{12,8},{14,10},{16,20},{18,... | collective-permute-start | bytes 786440 | tf_op jit(solution)/shard_map/ppermute | solution.py:127
  84.2 0.7 copy-start.14
  84.2 9.1 %collective-permute-start.17 = (bf16[1024,128]{1,0:T(8,128)(2,1)S(1)}, bf16[1024,128]{1,0:T(8,128)(2,1)S(1)}, u32[]{:S(2)}, u32[]{:S(2)}) collective-permute-start(bf16[1024,128]{1,0:T(8,128)(2,1)S(1)} %collective-permute-done.13.refs_3_), channel_id=1, source_target_pairs={{0,4},{2,6},{4,0},{6,2},{8,12},{10,14},{12,8},{14,10},{16,20},{18,... | collective-permute-start | bytes 786440 | tf_op jit(solution)/shard_map/ppermute | solution.py:127
  87.4 5.9 %collective-permute-start.10 = (bf16[96,1024]{1,0:T(8,128)(2,1)}, bf16[96,1024]{1,0:T(8,128)(2,1)S(1)}, u32[]{:S(2)}, u32[]{:S(2)}) collective-permute-start(bf16[96,1024]{1,0:T(8,128)(2,1)} %shard_map.111.own_ref), channel_id=1, source_target_pairs={{0,2},{2,0},{4,6},{6,4},{8,10},{10,8},{12,14},{14,12},{16,18},{18,... | collective-permute-start | bytes 589832 | tf_op jit(solution)/shard_map/ppermute | solution.py:127
  87.5 5.8 %copy-start.18 = (bf16[1024,128]{1,0:T(8,128)(2,1)}, bf16[1024,128]{1,0:T(8,128)(2,1)S(1)}, u32[]{:S(2)}) copy-start(bf16[1024,128]{1,0:T(8,128)(2,1)S(1)} %collective-permute-done.14.refs_4_) | copy-start | bytes 786436
  87.5 23.2 %collective-permute-start.4 = (bf16[512,512]{1,0:T(8,128)(2,1)S(1)}, bf16[512,512]{1,0:T(8,128)(2,1)S(1)}, u32[]{:S(2)}, u32[]{:S(2)}) collective-permute-start(bf16[512,512]{1,0:T(8,128)(2,1)S(1)} %broadcast_select_fusion.2), channel_id=1, source_target_pairs={{0,2},{2,0},{4,6},{6,4},{8,10},{10,8},{12,14},{14,12},{16,18},{18,... | collective-permute-start | bytes 1572872 | tf_op jit(solution)/shard_map/ppermute | solution.py:127
  88.1 5.2 %copy-start.19 = (bf16[1024,128]{1,0:T(8,128)(2,1)}, bf16[1024,128]{1,0:T(8,128)(2,1)S(1)}, u32[]{:S(2)}) copy-start(bf16[1024,128]{1,0:T(8,128)(2,1)S(1)} %collective-permute-done.15.refs_5_) | copy-start | bytes 786436
  90.5 2.9 %copy-start.20 = (bf16[1024,128]{1,0:T(8,128)(2,1)}, bf16[1024,128]{1,0:T(8,128)(2,1)S(1)}, u32[]{:S(2)}) copy-start(bf16[1024,128]{1,0:T(8,128)(2,1)S(1)} %collective-permute-done.16.refs_6_) | copy-start | bytes 786436
  93.3 0.7 copy-start.21
  94.0 0.7 copy-start.22
  110.8 2.1 %collective-permute-start.18 = (f32[512,256]{1,0:T(8,128)}, f32[512,256]{1,0:T(8,128)S(1)}, u32[]{:S(2)}, u32[]{:S(2)}) collective-permute-start(f32[512,256]{1,0:T(8,128)} %get-tuple-element.27), channel_id=1, source_target_pairs={{0,2},{2,0},{4,6},{6,4},{8,10},{10,8},{12,14},{14,12},{16,18},{18,... | collective-permute-start | bytes 1572872 | tf_op jit(solution)/shard_map/ppermute | solution.py:127
  112.9 0.8 copy-start.10
  116.3 19.8 %collective-permute-start.19 = (bf16[64,1024]{1,0:T(8,128)(2,1)}, bf16[64,1024]{1,0:T(8,128)(2,1)S(1)}, u32[]{:S(2)}, u32[]{:S(2)}) collective-permute-start(bf16[64,1024]{1,0:T(8,128)(2,1)} %shard_map.114.refs_0_), channel_id=1, source_target_pairs={{0,4},{2,6},{4,0},{6,2},{8,12},{10,14},{12,8},{14,10},{16,20},{18,... | collective-permute-start | bytes 393224 | tf_op jit(solution)/shard_map/ppermute | solution.py:127
  118.0 6.8 %collective-permute-start.20 = (bf16[64,1024]{1,0:T(8,128)(2,1)}, bf16[64,1024]{1,0:T(8,128)(2,1)S(1)}, u32[]{:S(2)}, u32[]{:S(2)}) collective-permute-start(bf16[64,1024]{1,0:T(8,128)(2,1)} %shard_map.114.refs_0_), channel_id=1, source_target_pairs={{0,8},{2,10},{4,12},{6,14},{8,0},{10,2},{12,4},{14,6},{16,24},{18,... | collective-permute-start | bytes 393224 | tf_op jit(solution)/shard_map/ppermute | solution.py:127
  118.4 15.6 %collective-permute-start.22 = (bf16[64,1024]{1,0:T(8,128)(2,1)}, bf16[64,1024]{1,0:T(8,128)(2,1)S(1)}, u32[]{:S(2)}, u32[]{:S(2)}) collective-permute-start(bf16[64,1024]{1,0:T(8,128)(2,1)} %shard_map.114.refs_0_), channel_id=1, source_target_pairs={{0,16},{2,18},{4,20},{6,22},{8,24},{10,26},{12,28},{14,30},{16,0},... | collective-permute-start | bytes 393224 | tf_op jit(solution)/shard_map/ppermute | solution.py:127
  123.8 10.5 %collective-permute-start.24 = (bf16[64,1024]{1,0:T(8,128)(2,1)}, bf16[64,1024]{1,0:T(8,128)(2,1)S(1)}, u32[]{:S(2)}, u32[]{:S(2)}) collective-permute-start(bf16[64,1024]{1,0:T(8,128)(2,1)} %shard_map.114.refs_0_), channel_id=1, source_target_pairs={{0,24},{2,26},{4,28},{6,30},{8,16},{10,18},{12,20},{14,22},{16,8},... | collective-permute-start | bytes 393224 | tf_op jit(solution)/shard_map/ppermute | solution.py:127
  124.8 24.7 %copy-start.4 = (bf16[64,1024]{1,0:T(8,128)(2,1)}, bf16[64,1024]{1,0:T(8,128)(2,1)S(1)}, u32[]{:S(2)}) copy-start(bf16[64,1024]{1,0:T(8,128)(2,1)S(1)} %collective-permute-done.20.refs_4_) | copy-start | bytes 393220
  124.8 11.3 %collective-permute-start.21 = (bf16[64,1024]{1,0:T(8,128)(2,1)S(1)}, bf16[64,1024]{1,0:T(8,128)(2,1)S(1)}, u32[]{:S(2)}, u32[]{:S(2)}) collective-permute-start(bf16[64,1024]{1,0:T(8,128)(2,1)S(1)} %collective-permute-done.20.refs_4_), channel_id=1, source_target_pairs={{0,4},{2,6},{4,0},{6,2},{8,12},{10,14},{12,8},{14,10},{16,20},{18,... | collective-permute-start | bytes 393224 | tf_op jit(solution)/shard_map/ppermute | solution.py:127
  134.0 15.4 %copy-start.5 = (bf16[64,1024]{1,0:T(8,128)(2,1)}, bf16[64,1024]{1,0:T(8,128)(2,1)S(1)}, u32[]{:S(2)}) copy-start(bf16[64,1024]{1,0:T(8,128)(2,1)S(1)} %collective-permute-done.22.refs_8_) | copy-start | bytes 393220
  134.0 5.0 %collective-permute-start.23 = (bf16[64,1024]{1,0:T(8,128)(2,1)S(1)}, bf16[64,1024]{1,0:T(8,128)(2,1)S(1)}, u32[]{:S(2)}, u32[]{:S(2)}) collective-permute-start(bf16[64,1024]{1,0:T(8,128)(2,1)S(1)} %collective-permute-done.22.refs_8_), channel_id=1, source_target_pairs={{0,4},{2,6},{4,0},{6,2},{8,12},{10,14},{12,8},{14,10},{16,20},{18,... | collective-permute-start | bytes 393224 | tf_op jit(solution)/shard_map/ppermute | solution.py:127
  134.3 15.1 %copy-start.6 = (bf16[64,1024]{1,0:T(8,128)(2,1)}, bf16[64,1024]{1,0:T(8,128)(2,1)S(1)}, u32[]{:S(2)}) copy-start(bf16[64,1024]{1,0:T(8,128)(2,1)S(1)} %collective-permute-done.24.refs_12_) | copy-start | bytes 393220
  134.3 6.1 %collective-permute-start.25 = (bf16[64,1024]{1,0:T(8,128)(2,1)S(1)}, bf16[64,1024]{1,0:T(8,128)(2,1)S(1)}, u32[]{:S(2)}, u32[]{:S(2)}) collective-permute-start(bf16[64,1024]{1,0:T(8,128)(2,1)S(1)} %collective-permute-done.24.refs_12_), channel_id=1, source_target_pairs={{0,4},{2,6},{4,0},{6,2},{8,12},{10,14},{12,8},{14,10},{16,20},{18,... | collective-permute-start | bytes 393224 | tf_op jit(solution)/shard_map/ppermute | solution.py:127
  136.1 13.4 %copy-start.3 = (bf16[64,1024]{1,0:T(8,128)(2,1)}, bf16[64,1024]{1,0:T(8,128)(2,1)S(1)}, u32[]{:S(2)}) copy-start(bf16[64,1024]{1,0:T(8,128)(2,1)S(1)} %collective-permute-done.19.refs_2_) | copy-start | bytes 393220
  136.1 13.4 %copy-start.7 = (bf16[64,1024]{1,0:T(8,128)(2,1)}, bf16[64,1024]{1,0:T(8,128)(2,1)S(1)}, u32[]{:S(2)}) copy-start(bf16[64,1024]{1,0:T(8,128)(2,1)S(1)} %collective-permute-done.21.refs_6_) | copy-start | bytes 393220
  139.0 10.5 %copy-start.8 = (bf16[64,1024]{1,0:T(8,128)(2,1)}, bf16[64,1024]{1,0:T(8,128)(2,1)S(1)}, u32[]{:S(2)}) copy-start(bf16[64,1024]{1,0:T(8,128)(2,1)S(1)} %collective-permute-done.23.refs_10_) | copy-start | bytes 393220
  140.4 9.1 %copy-start.9 = (bf16[64,1024]{1,0:T(8,128)(2,1)}, bf16[64,1024]{1,0:T(8,128)(2,1)S(1)}, u32[]{:S(2)}) copy-start(bf16[64,1024]{1,0:T(8,128)(2,1)S(1)} %collective-permute-done.25.refs_14_) | copy-start | bytes 393220
  140.4 27.2 %collective-permute-start.26 = (bf16[8,64,1024]{2,1,0:T(8,128)(2,1)S(1)}, bf16[8,64,1024]{2,1,0:T(8,128)(2,1)S(1)}, u32[]{:S(2)}, u32[]{:S(2)}) collective-permute-start(bf16[8,64,1024]{2,1,0:T(8,128)(2,1)S(1)} %bitcast_dynamic-update-slice_fusion), channel_id=1, source_target_pairs={{0,2},{2,0},{4,6},{6,4},{8,10},{10,8},{12,14},{14,12},{16,18},{18,... | collective-permute-start | bytes 3145736 | tf_op jit(solution)/shard_map/ppermute | solution.py:127
  174.6 10.5 %copy-start.11 = (f32[128,512]{1,0:T(8,128)S(1)}, f32[128,512]{1,0:T(8,128)}, u32[]{:S(2)}) copy-start(f32[128,512]{1,0:T(8,128)} %get-tuple-element.28) | copy-start | bytes 786436
  174.6 10.5 %collective-permute-start.27 = (bf16[128,512]{1,0:T(8,128)(2,1)}, bf16[128,512]{1,0:T(8,128)(2,1)S(1)}, u32[]{:S(2)}, u32[]{:S(2)}) collective-permute-start(bf16[128,512]{1,0:T(8,128)(2,1)} %get-tuple-element.29), channel_id=1, source_target_pairs={{0,1},{1,0},{2,3},{3,2},{4,5},{5,4},{6,7},{7,6},{8,9},{9,8},{10,11... | collective-permute-start | bytes 393224 | tf_op jit(solution)/shard_map/ppermute | solution.py:408

commit v2 on v0

--- a/solution.py
+++ b/solution.py
@@ -1,11 +1,17 @@
+import functools
 import math
 
 import jax
 import jax.numpy as jnp
 from jax import lax
+from jax.experimental import pallas as pl
+from jax.experimental.pallas import tpu as pltpu
 from jax.sharding import PartitionSpec as P
 
 HEAD_SIZE = 128
+F32 = jnp.float32
+BF16 = jnp.bfloat16
+LOG_SCALE = math.log2(math.e) / math.sqrt(HEAD_SIZE)
 
 
 masked_score = -1e30
@@ -61,7 +67,7 @@
     return (top, totals, outputs.reshape(rows, -1))
 
 
-def body(
+def generic_body(
     ctx_query,
     ctx_key,
     context_value,
@@ -112,6 +118,416 @@
     return (pieces, layer_out)
 
 
+def dot_t(a, b):
+    return lax.dot_general(a, b, (((1,), (1,)), ((), ())), preferred_element_type=F32)
+
+
+def swap(array, bit):
+    return lax.ppermute(array, "hst", [(i, i ^ bit) for i in range(16)])
+
+
+def place():
+    host = lax.axis_index("hst")
+    return host // 4, host // 2 % 2, host % 2
+
+
+def call(
+    kernel, out_shape, in_specs, out_specs, args, scalars=(), after=(), grid=(), scratch=(), flops=0, data=0, aliases=None, vmem=8
+):
+    n, m = len(scalars), len(after)
+
+    def body(*refs):
+        kernel(*refs[:n], *refs[n + m :])
+
+    return pl.pallas_call(
+        body,
+        grid_spec=pltpu.PrefetchScalarGridSpec(
+            num_scalar_prefetch=n,
+            grid=grid,
+            in_specs=[pl.BlockSpec(memory_space=pl.ANY)] * m + in_specs,
+            out_specs=out_specs,
+            scratch_shapes=list(scratch),
+        ),
+        out_shape=out_shape,
+        input_output_aliases={n + m + i: o for i, o in (aliases or {}).items()},
+        compiler_params=pltpu.CompilerParams(vmem_limit_bytes=vmem * 2**20),
+        cost_estimate=pl.CostEstimate(flops=flops, bytes_accessed=data, transcendentals=0),
+    )(*scalars, *after, *args)
+
+
+shape = jax.ShapeDtypeStruct
+WHOLE = pl.BlockSpec(memory_space=pltpu.VMEM)
+ANY = pl.BlockSpec(memory_space=pl.ANY)
+
+
+def in_hbm(*arrays):
+    return [pltpu.with_memory_space_constraint(array, pltpu.HBM) for array in arrays]
+
+
+def in_vmem(*arrays):
+    return [pltpu.with_memory_space_constraint(array, pltpu.VMEM) for array in arrays]
+
+
+def lanes(start, size):
+    return pl.ds(pl.multiple_of(start, 128), size)
+
+
+def rows(start, size):
+    return pl.ds(pl.multiple_of(start, 64), size)
+
+
+def copy_all(pairs, sems):
+    copies = [pltpu.make_async_copy(a, b, sems.at[i]) for i, (a, b) in enumerate(pairs)]
+    for copy in copies:
+        copy.start()
+    for copy in copies:
+        copy.wait()
+
+
+def ask_pack_kernel(q_ref, k_ref, v_ref, out_ref, sems):
+    _, _, c = place()
+    pairs = []
+    for x in range(2):
+        here, there = rows(x * 128 + (1 - c) * 64, 64), slice(x * 64, (x + 1) * 64)
+        pairs += [
+            (q_ref.at[0, here], out_ref.at[there, 0:4096]),
+            (k_ref.at[0, here], out_ref.at[there, 4096:4608]),
+            (v_ref.at[0, here], out_ref.at[there, 4608:5120]),
+        ]
+    copy_all(pairs, sems)
+
+
+def kv_pack_kernel(k_ref, v_ref, *refs):
+    z, _, _ = place()
+    pairs = []
+    for s, out_ref in enumerate(refs[:4]):
+        head = lanes((z ^ s) * 128, 128)
+        pairs += [(k_ref.at[:, head], out_ref.at[0:512]), (v_ref.at[:, head], out_ref.at[512:1024])]
+    copy_all(pairs, refs[4])
+
+
+def x_pack_kernel(owner, got_ref, q_ref, k_ref, v_ref, send_ref, sems):
+    _, x, c = place()
+    owner_c = owner[0] % 2
+
+    @pl.when(owner_c == c)
+    def _():
+        pairs = [(q_ref.at[0, rows((1 - x) * 128 + c * 64, 64)], send_ref.at[:, 0:4096])]
+        for i in range(2):
+            here, to = rows(i * 128 + c * 64, 64), 4096 + i * 1024
+            pairs += [
+                (k_ref.at[0, here], send_ref.at[:, to : to + 512]),
+                (v_ref.at[0, here], send_ref.at[:, to + 512 : to + 1024]),
+            ]
+        copy_all(pairs, sems)
+
+    @pl.when(owner_c != c)
+    def _():
+        send_ref[:, 0:4096] = got_ref[rows((1 - x) * 64, 64), 0:4096]
+        for i in range(2):
+            to = 4096 + i * 1024
+            send_ref[:, to : to + 1024] = got_ref[i * 64 : (i + 1) * 64, 4096:5120]
+
+
+def z_pack_kernel(owner, c_ref, x_ref, q_ref, k_ref, v_ref, *refs):
+    z, x, c = place()
+    outs, sems = refs[:4], refs[4]
+    owner_c, owner_x = owner[0] % 2, owner[0] // 2 % 2
+
+    @pl.when(owner_x != x)
+    def _():
+        for s, out_ref in enumerate(outs):
+            j = z ^ s
+            out_ref[:, 0:1024] = x_ref[:, lanes(j * 1024, 1024)]
+            for i in range(4):
+                out_ref[:, 1024 + i * 128 : 1152 + i * 128] = x_ref[:, lanes(4096 + i * 512 + j * 128, 128)]
+
+    @pl.when((owner_x == x) & (owner_c == c))
+    def _():
+        pairs = []
+        for s, out_ref in enumerate(outs):
+            j = z ^ s
+            pairs.append((q_ref.at[0, rows(x * 128 + c * 64, 64), lanes(j * 1024, 1024)], out_ref.at[:, 0:1024]))
+            for i in range(4):
+                part = (k_ref, v_ref)[i % 2].at[0, rows(i // 2 * 128 + c * 64, 64), lanes(j * 128, 128)]
+                pairs.append((part, out_ref.at[:, 1024 + i * 128 : 1152 + i * 128]))
+        copy_all(pairs, sems)
+
+    @pl.when((owner_x == x) & (owner_c != c))
+    def _():
+        for s, out_ref in enumerate(outs):
+            j = z ^ s
+            out_ref[:, 0:1024] = c_ref[rows(x * 64, 64), lanes(j * 1024, 1024)]
+            for i in range(4):
+                part = c_ref[i // 2 * 64 : (i // 2 + 1) * 64, lanes(4096 + i % 2 * 512 + j * 128, 128)]
+                out_ref[:, 1024 + i * 128 : 1152 + i * 128] = part
+
+
+def ones_beside(values):
+    return jnp.concatenate([values, jnp.ones(values.shape, values.dtype)], axis=1)
+
+
+def read_kernel(owner, lengths, *refs):
+    asked, (own_kv, other_kv), parts, out_ref, q_ref = refs[:4], refs[4:6], refs[6:22], refs[22], refs[23]
+    z, x, c = place()
+    step = pl.program_id(0)
+    at = z ^ (owner[0] // 4)
+    for s in range(4):
+
+        @pl.when(at == s)
+        def _(s=s):
+            for h in range(4):
+                q_ref[h * 64 : (h + 1) * 64, :] = asked[s][:, lanes(step * 512 + h * 128, 128)]
+
+    q = q_ref[...]
+    column = lax.broadcasted_iota(jnp.int32, (1, 512), 1)
+    found = []
+
+    def add(scores, values):
+        peak = row_max(scores)
+        total = 0
+        for s, v in zip(scores, values):
+            total = total + jnp.dot(weights(s, peak), ones_beside(v), preferred_element_type=F32)
+        found.append((peak, total))
+
+    for pair in range(8):
+        scores, values = [], []
+        for i in (2 * pair, 2 * pair + 1):
+            block = ((z ^ (i % 4)) * 2 + (x ^ (i // 4 % 2))) * 2 + (c ^ (i // 8))
+            scores.append(jnp.where(column < lengths[block], dot_t(q, parts[i][0:512, :]), masked_score))
+            values.append(parts[i][512:1024, :])
+        add(scores, values)
+    row_at = lax.broadcasted_iota(jnp.int32, (256, 64), 0) % 64 + x * 128 + c * 64
+    column = lax.broadcasted_iota(jnp.int32, (256, 64), 1)
+    scores, values = [], []
+    for ref, core in ((own_kv, c), (other_kv, 1 - c)):
+        for i in range(2):
+            s = dot_t(q, ref[:, i * 256 : i * 256 + 128])
+            scores.append(jnp.where(column + i * 128 + core * 64 <= row_at, s, masked_score))
+            values.append(ref[:, i * 256 + 128 : (i + 1) * 256])
+    add([jnp.concatenate(scores, axis=1)], [jnp.concatenate(values, axis=0)])
+    top = functools.reduce(jnp.maximum, [peak for peak, _ in found])
+    scales = [jnp.exp2(peak - top) for peak, _ in found]
+    sums = sum(scale * part[:, :128] for scale, (_, part) in zip(scales, found))
+    total = sum(scale * part[:, 128:] for scale, (_, part) in zip(scales, found))
+    answer = (sums / total).astype(BF16)
+    for h in range(4):
+        out_ref[:, h * 128 : (h + 1) * 128] = answer[h * 64 : (h + 1) * 64, :]
+
+
+def project_kernel(*refs):
+    near, near_far, side, side_far, w_ref, keep_ref, send_ref, sum_ref = refs
+    z, x, c = place()
+    t = lax.axis_index("tensor")
+    for s in range(4):
+        w = w_ref[pl.ds(pl.multiple_of((z ^ s) * 1024, 1024), 1024), :]
+        across = [(near, s), (near_far, s), (near, 4) if s == 0 else (side, s - 1), (near_far, 4) if s == 0 else (side_far, s - 1)]
+        a = jnp.concatenate([ref[i] for ref, i in across], axis=0)
+        product = jnp.dot(a, w, preferred_element_type=F32)
+        if s == 0:
+            sum_ref[...] = product
+        else:
+            sum_ref[...] += product
+    for r in range(4):
+        half, core = x ^ (r // 2), c ^ (r % 2)
+        at_row = rows(core * 64, 64)
+        quarter = sum_ref[r * 64 : (r + 1) * 64, :]
+
+        @pl.when(half == t)
+        def _(quarter=quarter, at_row=at_row):
+            keep_ref[at_row, :] = quarter
+
+        @pl.when(half != t)
+        def _(quarter=quarter, at_row=at_row):
+            send_ref[at_row, :] = quarter.astype(BF16)
+
+
+def row_max(scores):
+    tiles = [s[:, i : i + 128] for s in scores for i in range(0, s.shape[1], 128)]
+    peak = jnp.max(functools.reduce(jnp.maximum, tiles), axis=1, keepdims=True)
+    return jnp.broadcast_to(peak * LOG_SCALE, (scores[0].shape[0], 128))
+
+
+def weights(s, peak):
+    tiles = [jnp.exp2(s[:, i : i + 128] * LOG_SCALE - peak).astype(BF16) for i in range(0, s.shape[1], 128)]
+    return jnp.concatenate(tiles, axis=1)
+
+
+def own_kernel(q_ref, k_ref, v_ref, *rest):
+    o_ref, lse_ref = rest[-2:]
+    row = lax.broadcasted_iota(jnp.int32, (256, 256), 0)
+    column = lax.broadcasted_iota(jnp.int32, (256, 256), 1)
+    lane = lax.broadcasted_iota(jnp.int32, (256, 128), 1)
+
+    def half(r):
+        own_v = [ones_beside(v_ref[b * 256 : (b + 1) * 256, :]) for b in range(r + 1)]
+        found = jnp.zeros((256, 128), F32)
+        for h in range(8):
+            q = q_ref[:, h * 128 : (h + 1) * 128]
+            scores = []
+            for b in range(r + 1):
+                s = dot_t(q, k_ref[b * 256 : (b + 1) * 256, :])
+                scores.append(jnp.where(column <= row, s, masked_score) if b == r else s)
+            peak = row_max(scores)
+            total = 0
+            for b in range(r + 1):
+                total = total + jnp.dot(weights(scores[b], peak), own_v[b], preferred_element_type=F32)
+            o_ref[:, h * 128 : (h + 1) * 128] = (total[:, :128] / total[:, 128:]).astype(BF16)
+            found = jnp.where(lane == h, peak + jnp.log2(total[:, 128:]), found)
+        lse_ref[...] = found
+
+    @pl.when(pl.program_id(0) == 0)
+    def _():
+        half(0)
+
+    @pl.when(pl.program_id(0) == 1)
+    def _():
+        half(1)
+
+
+def anchor_kernel(lengths, q_ref, own_ref, lse_ref, near_k_ref, near_v_ref, far_k_ref, far_v_ref, *rest):
+    o_ref = rest[-1]
+    host = lax.axis_index("hst")
+    anchor_len = jnp.where(host > 0, lengths[0], 0)
+    own_len = lengths[host] - pl.program_id(0) * 256
+    _, x, _ = place()
+    column = lax.broadcasted_iota(jnp.int32, (1, 256), 1)
+    parts = [
+        (near_k_ref, column + x * 256 < anchor_len, ones_beside(near_v_ref[...])),
+        (far_k_ref, column + (1 - x) * 256 < anchor_len, ones_beside(far_v_ref[...])),
+    ]
+    valid = lax.broadcasted_iota(jnp.int32, (256, 128), 0) < own_len
+    for h in range(8):
+        at = slice(h * 128, (h + 1) * 128)
+        scores = [jnp.where(ok, dot_t(q_ref[:, at], k_ref[...]), masked_score) for k_ref, ok, _ in parts]
+        lse = jnp.broadcast_to(lse_ref[:, h : h + 1], (256, 128))
+        peak = jnp.maximum(row_max(scores), lse)
+        total = 0
+        for s, (_, _, values) in zip(scores, parts):
+            total = total + jnp.dot(weights(s, peak), values, preferred_element_type=F32)
+        own = jnp.exp2(lse - peak)
+        result = (total[:, :128] + own * own_ref[:, at].astype(F32)) / (total[:, 128:] + own)
+        o_ref[:, at] = jnp.where(valid, result, 0.0).astype(BF16)
+
+
+def body(ctx_query, ctx_key, context_value, lengths, owner, ask_query, ask_key, candidate_value_rows, out_weight):
+    z, x, c = place()
+    ask = [ask_query, ask_key, candidate_value_rows]
+    dma = pltpu.SemaphoreType.DMA
+
+    def send(array, pairs):
+        return lax.ppermute(array, "hst", pairs)
+
+    def after(array, *others):
+        return lax.optimization_barrier((array, *others))[0]
+
+    own_out, lse = None, []
+
+    def own(g, *others):
+        nonlocal own_out
+        block = pl.BlockSpec((256, 1024), lambda i, g=g: (i, g))
+        head = pl.BlockSpec((512, 128), lambda i, g=g: (0, g))
+        own_out, found = call(
+            own_kernel, [pltpu.HBM((512, 4096), BF16), pltpu.HBM((512, 128), F32)],
+            [block, head, head] + ([] if g == 0 else [ANY]),
+            [block, pl.BlockSpec((256, 128), lambda i: (i, 0))],
+            in_hbm(ctx_query, ctx_key, context_value) + ([] if g == 0 else in_hbm(own_out)),
+            after=others, grid=(2,), aliases={} if g == 0 else {3: 0}, flops=4 * 4096 * 768 * 256, data=2**21, vmem=16,
+        )
+        lse.append(found)
+        return found
+
+    ctx_out = None
+
+    def encode(g, *others):
+        nonlocal ctx_out
+        block = pl.BlockSpec((256, 1024), lambda i, _, g=g: (i, g))
+        head = pl.BlockSpec((256, 128), lambda i, _, g=g: (0, g))
+        ctx_out = call(
+            anchor_kernel, pltpu.HBM((512, 4096), BF16),
+            [block, block, pl.BlockSpec((256, 128), lambda i, _: (i, 0))] + [head] * 4
+            + ([] if g == 0 else [ANY]),
+            block,
+            in_hbm(ctx_query, own_out, lse[g]) + anchor + ([] if g == 0 else in_hbm(ctx_out)),
+            scalars=[lengths], after=others, grid=(2,), aliases={} if g == 0 else {7: 0},
+            flops=4 * 4096 * 512 * 256, data=2**21, vmem=16,
+        )
+        return ctx_out
+
+    kv = call(
+        kv_pack_kernel, [pltpu.HBM((1024, 128), BF16)] + [shape((1024, 128), BF16)] * 3, [ANY] * 2, [WHOLE] * 4,
+        in_hbm(ctx_key, context_value), scratch=[dma((8,))],
+    )
+    packed = call(
+        ask_pack_kernel, shape((128, 5120), BF16), [ANY] * 3, WHOLE, in_hbm(*ask), after=[kv[0]], scratch=[dma((6,))]
+    )
+    got_c = swap(packed, 1)
+    kv_z = [kv[0]] + [swap(kv[s], 4 * s) for s in (1, 2, 3)]
+    sent = call(
+        x_pack_kernel, shape((64, 6144), BF16), [WHOLE] + [ANY] * 3, WHOLE, in_vmem(got_c) + in_hbm(*ask),
+        scalars=[owner], scratch=[dma((5,))],
+    )
+    got_x = swap(sent, 2)
+
+    whole = jnp.where(c == 0, ctx_key, send(after(context_value, packed), [(0, 1)]))
+    got = send(after(whole[256:], sent), [(0, 2), (1, 3)])
+    quarter = jnp.where(x == 0, whole[:256], got)
+    tick = own(0, sent)
+    got = send(after(quarter, tick), [(i, i + 8) for i in range(4)])
+    quarter = jnp.where(z == 0, quarter, got)
+    own(1, kv_z[1])
+    tick = own(2, kv_z[2])
+    parts = call(
+        z_pack_kernel, [pltpu.HBM((64, 1536), BF16)] + [shape((64, 1536), BF16)] * 3, [WHOLE] * 2 + [ANY] * 3, [WHOLE] * 4,
+        in_vmem(got_c, got_x) + in_hbm(*ask), scalars=[owner], after=[tick], scratch=[dma((20,))],
+    )
+    asked = [parts[0]] + [swap(parts[s], 4 * s) for s in (1, 2, 3)]
+    tick = own(3, parts[0])
+    kv_x = [swap(after(part, parts[0]), 2) for part in kv_z]
+    kv_near = kv_z + kv_x
+    kv_far = [swap(after(part, parts[0]), 1) for part in kv_near]
+
+    level = z ^ (owner[0] // 4)
+    own_kv = asked[0][:, 1024:]
+    for s in (1, 2, 3):
+        own_kv = jnp.where(level == s, asked[s][:, 1024:], own_kv)
+    other_kv = swap(own_kv, 1)
+    answer = call(
+        read_kernel, shape((64, 1024), BF16), [WHOLE] * 22, pl.BlockSpec((64, 512), lambda i, *_: (0, i)),
+        [asked[0]] + in_vmem(*asked[1:], own_kv, other_kv) + kv_near[:1] + in_vmem(*kv_near[1:], *kv_far),
+        scalars=[owner, lengths], grid=(2,),
+        scratch=[pltpu.VMEM((256, 128), BF16)], flops=4 * 512 * 8192 * 256, data=2**22, vmem=20,
+    )
+
+    got = send(after(quarter, tick), [(i, i + 4) for i in (0, 1, 2, 3, 8, 9, 10, 11)])
+    near = jnp.where(z % 2 == 0, quarter, got)
+    far = swap(near, 2)
+    anchor = []
+    for half in (near, far):
+        got = swap(half, 1)
+        anchor += [jnp.where(c == 0, half, got), jnp.where(c == 0, got, half)]
+
+    across = [swap(answer, 4 * s) for s in (1, 2, 3)]
+    side = swap(answer, 2)
+    encode(0, answer)
+    tick = encode(1)
+    across = [after(part, tick) for part in across]
+    sides = [swap(part, 2) for part in across]
+    near = jnp.stack([answer] + across + [after(side, tick)])
+    near_far = swap(near, 1)
+    tick = encode(2)
+    side = jnp.stack([after(part, tick) for part in sides])
+    side_far = swap(side, 1)
+    keep, sent = call(
+        project_kernel, [shape((128, 512), F32), shape((128, 512), BF16)], [WHOLE] * 5, [WHOLE] * 2,
+        in_vmem(near, near_far, side, side_far, out_weight), scratch=[pltpu.VMEM((256, 512), F32)],
+        flops=2 * 256 * 4096 * 512, data=2**22, vmem=16,
+    )
+    got = lax.ppermute(sent, "tensor", [(0, 1), (1, 0)])
+    tick = encode(3, sent)
+    return ctx_out, (keep + after(got, tick).astype(F32)).astype(BF16)
+
+
 def solution(mesh):
     placed = (
         P("hst", "tensor"),
@@ -124,8 +540,9 @@
         P("hst", None, "tensor"),
         P("tensor", "hst"),
     )
+    fits = dict(mesh.shape) == {"hst": 16, "tensor": 2}
     return jax.shard_map(
-        body,
+        body if fits else generic_body,
         mesh=mesh,
         in_specs=placed,
         out_specs=(P("hst", "tensor"), P("tensor", "hst")),

time: 773 us -> 132 us (0.17)
  waiting for transfers between devices: 260 us -> 23.1 us
  other arithmetic: 214 us -> 3.69 us
  local copies, waits for them, and re-layouts: 135 us -> 2.91 us
  matrix products: 93.7 us -> 0 us
  Pallas kernels: 0 us -> 61.8 us
  blocking collectives: 47.3 us -> 0 us
  starting transfers between devices: 0.12 us -> 38.7 us
  between operations: 15.2 us -> 1.6 us
    add x31 -> x0, other arithmetic: 161 us -> none  [the longest x15 160 us: combine(): first_piece[2].reshape(rows, heads, -1) * scale_one[..., None]]
    all_gather x1 -> x0, waiting for transfers between devices: 151 us -> none  [combined_all(): everything = jax.tree.map(lambda part: lax.all_gather(part, axis), array)]
    psum x1 -> x0, waiting for transfers between devices: 109 us -> none  [broadcast(): return lax.psum(block, axis)]
    dot_general x7 -> x0, matrix products: 93.7 us -> none  [the longest x3 41.7 us: partial_attend(): jnp.einsum('rkgs,skd->rkgd', weights, value_heads, preferred_element_type...]
    pallas_call x0 -> x14, Pallas kernels: none -> 61.8 us  [call(): pl.pallas_call(body, grid_spec=pltpu.PrefetchScalarGridSpec(num_scalar_pr...]
    all_gather x2 -> x0, blocking collectives: 47.3 us -> none  [combined_all(): everything = jax.tree.map(lambda part: lax.all_gather(part, axis), array)]
    ppermute x0 -> x38, starting transfers between devices: none -> 38.7 us  [the longest x33 28.6 us: swap(): return lax.ppermute(array, 'hst', [(i, i ^ bit) for i in range(16)])]
    reduce_sum x3 -> x0, other arithmetic: 37.2 us -> none  [partial_attend(): totals = jnp.sum(weights.astype(jnp.float32), axis=-1)]
  transfers between devices with their start and end apart: 3 -> 38, of which waited for: 2 -> 9; matrix products, arithmetic and copies ran while one was open for 19% -> 2% of each run, Pallas kernels for 0% -> 43%
where the time goes in v2:
time: 132 us
  Pallas kernels  61.8 us (47%)
  starting transfers between devices  38.7 us (29%)
  waiting for transfers between devices  23.1 us (18%)
  other arithmetic  3.69 us (3%)
  local copies, waits for them, and re-layouts  2.91 us (2%)
  between operations  1.6 us (1%)
    pallas_call x14, Pallas kernels, call(): pl.pallas_call(body, grid_spec=pltpu.PrefetchScalarGridSpec(num_scalar_pr...  61.8 us
    ppermute x33, starting transfers between devices, swap(): return lax.ppermute(array, 'hst', [(i, i ^ bit) for i in range(16)])  28.6 us
    ppermute x33, waiting for transfers between devices, swap(): return lax.ppermute(array, 'hst', [(i, i ^ bit) for i in range(16)])  12.8 us
    ppermute x4, waiting for transfers between devices, send(): return lax.ppermute(array, 'hst', pairs)  10.3 us
    ppermute x4, starting transfers between devices, send(): return lax.ppermute(array, 'hst', pairs)  8.78 us
    unnamed x18, local copies, waits for them, and re-layouts  2.88 us
  transfers between devices with their start and end apart: 38, of which 9 were waited for; matrix products, arithmetic and copies ran while one was open for 2% of the time, Pallas kernels for 43%

profile of v2, /device:TPU:0, one launch (start us, length us, event | category | flops | bytes accessed | tf_op | source)
XLA Modules:
  0.0 131.8 jit_solution(16960488216073404870)
XLA Ops:
  0.6 2.4 %shard_map.104 = (bf16[1024,128]{1,0:T(8,128)(2,1)}, bf16[1024,128]{1,0:T(8,128)(2,1)}, bf16[1024,128]{1,0:T(8,128)(2,1)}, bf16[1024,128]{1,0:T(8,128)(2,1)}) custom-call(bf16[512,512]{1,0:T(8,128)(2,1)} %refs_2_.13, bf16[512,512]{1,0:T(8,128)(2,1)} %refs_3_.11), custom_call_target="tpu_custom_call" | custom-call | tf_op jit(solution)/shard_map/pallas_call | solution.py:142
  3.0 0.9 copy-done.2
  3.9 1.3 shard_map.105
  5.2 0.5 collective-permute-start.2
  5.8 2.7 %collective-permute-start.22 = (bf16[512,512]{1,0:T(8,128)(2,1)}, bf16[512,512]{1,0:T(8,128)(2,1)}, u32[]{:S(2)}, u32[]{:S(2)}) collective-permute-start(bf16[512,512]{1,0:T(8,128)(2,1)} %refs_3_.11), channel_id=1, source_target_pairs={{0,2},{1,3}} | collective-permute-start | bytes 1572872 | tf_op jit(solution)/shard_map/ppermute | solution.py:419
  8.5 1.3 collective-permute-start.1
  9.8 2.6 %collective-permute-start = (bf16[1024,128]{1,0:T(8,128)(2,1)}, bf16[1024,128]{1,0:T(8,128)(2,1)S(1)}, u32[]{:S(2)}, u32[]{:S(2)}) collective-permute-start(bf16[1024,128]{1,0:T(8,128)(2,1)} %get-tuple-element.40), channel_id=1, source_target_pairs={{0,16},{2,18},{4,20},{6,22},{8,24},{10,26},{12,28},{14,30},{16,0},... | collective-permute-start | bytes 786440 | tf_op jit(solution)/shard_map/ppermute | solution.py:126
  12.4 0.5 collective-permute-start.8
  13.6 1.1 broadcast_select_fusion
  14.7 1.1 shard_map.106.refs_0_
  15.9 1.3 collective-permute-start.3
  17.1 2.7 %collective-permute-start.23 = (bf16[256,512]{1,0:T(8,128)(2,1)S(1)}, bf16[256,512]{1,0:T(8,128)(2,1)S(1)}, u32[]{:S(2)}, u32[]{:S(2)}) collective-permute-start(bf16[256,512]{1,0:T(8,128)(2,1)S(1)} %slice.28), channel_id=1, source_target_pairs={{0,4},{2,6},{1,5},{3,7}} | collective-permute-start | bytes 786440 | tf_op jit(solution)/shard_map/ppermute | solution.py:419
  19.9 4.7 %shard_map.107 = (bf16[512,4096]{1,0:T(8,128)(2,1)}, f32[512,128]{1,0:T(8,128)}) custom-call(bf16[64,6144]{1,0:T(8,128)(2,1)S(1)} %shard_map.106.refs_0_, bf16[512,4096]{1,0:T(8,128)(2,1)} %refs_2_.15, bf16[512,512]{1,0:T(8,128)(2,1)} %refs_2_.13, bf16[512,512]{1,0:T(8,128)(2,1)} %refs_3_.11), custom_call_target="tpu_custom_call" | custom-call | flops 3221225472 | bytes 2097152 | tf_op jit(solution)/shard_map/pallas_call | solution.py:142
  24.5 4.7 %shard_map.108 = (bf16[512,4096]{1,0:T(8,128)(2,1)}, f32[512,128]{1,0:T(8,128)}) custom-call(bf16[1024,128]{1,0:T(8,128)(2,1)S(1)} %collective-permute-done.1.refs_0_.refs_9_, bf16[512,4096]{1,0:T(8,128)(2,1)} %refs_2_.15, bf16[512,512]{1,0:T(8,128)(2,1)} %refs_2_.13, bf16[512,512]{1,0:T(8,128)(2,1)} %refs_3_.11, ...), custom_call_target="tpu_custom_call", output_to_operand_aliasing={{0}: (4, {})} | custom-call | flops 3221225472 | bytes 2097152 | tf_op jit(solution)/shard_map/pallas_call | solution.py:142
  29.2 9.2 %collective-permute-done.23 = bf16[256,512]{1,0:T(8,128)(2,1)S(1)} collective-permute-done((bf16[256,512]{1,0:T(8,128)(2,1)S(1)}, bf16[256,512]{1,0:T(8,128)(2,1)S(1)}, u32[]{:S(2)}, u32[]{:S(2)}) %collective-permute-start.23) | collective-permute-done | bytes 262176 | tf_op jit(solution)/shard_map/ppermute | solution.py:419
  38.5 1.3 collective-permute-start.24
  39.8 4.7 %shard_map.109 = (bf16[512,4096]{1,0:T(8,128)(2,1)}, f32[512,128]{1,0:T(8,128)}) custom-call(bf16[1024,128]{1,0:T(8,128)(2,1)S(1)} %collective-permute-done.refs_0_.refs_10_, bf16[512,4096]{1,0:T(8,128)(2,1)} %refs_2_.15, bf16[512,512]{1,0:T(8,128)(2,1)} %refs_2_.13, bf16[512,512]{1,0:T(8,128)(2,1)} %refs_3_.11, ...), custom_call_target="tpu_custom_call", output_to_operand_aliasing={{0}: (4, {})} | custom-call | flops 3221225472 | bytes 2097152 | tf_op jit(solution)/shard_map/pallas_call | solution.py:142
  44.5 0.9 copy-done.1
  45.4 2.2 %shard_map.110 = (bf16[64,1536]{1,0:T(8,128)(2,1)}, bf16[64,1536]{1,0:T(8,128)(2,1)S(1)}, bf16[64,1536]{1,0:T(8,128)(2,1)S(1)}, bf16[64,1536]{1,0:T(8,128)(2,1)S(1)}) custom-call(s32[1]{0:T(128)} %copy.27.refs_0_, f32[512,128]{1,0:T(8,128)S(1)} %copy-done.1, bf16[128,5120]{1,0:T(8,128)(2,1)S(1)} %collective-permute-done.2.refs_1_.refs_2_, ...), custom_call_target="tpu_custom_call" | custom-call | tf_op jit(solution)/shard_map/pallas_call | solution.py:142
  47.6 0.1 collective-permute-start.4
  47.7 0.1 collective-permute-start.5
  47.8 0.7 broadcast_select_fusion.1
  48.5 4.3 %collective-permute-start.6 = (bf16[64,1536]{1,0:T(8,128)(2,1)S(1)}, bf16[64,1536]{1,0:T(8,128)(2,1)S(1)}, u32[]{:S(2)}, u32[]{:S(2)}) collective-permute-start(bf16[64,1536]{1,0:T(8,128)(2,1)S(1)} %get-tuple-element.49), channel_id=1, source_target_pairs={{0,24},{2,26},{4,28},{6,30},{8,16},{10,18},{12,20},{14,22},{16,8},... | collective-permute-start | bytes 589832 | tf_op jit(solution)/shard_map/ppermute | solution.py:126
  52.8 1.4 %collective-permute-start.11 = (bf16[1024,128]{1,0:T(8,128)(2,1)S(1)}, bf16[1024,128]{1,0:T(8,128)(2,1)S(1)}, u32[]{:S(2)}, u32[]{:S(2)}) collective-permute-start(bf16[1024,128]{1,0:T(8,128)(2,1)S(1)} %collective-permute-done.refs_0_.refs_10_), channel_id=1, source_target_pairs={{0,4},{2,6},{4,0},{6,2},{8,12},{10,14},{12,8},{14,10},{16,20},{18,... | collective-permute-start | bytes 786440 | tf_op jit(solution)/shard_map/ppermute | solution.py:126
  54.3 0.6 collective-permute-start.10
  54.8 0.8 collective-permute-done.4.refs_3_
  55.6 1.4 %collective-permute-start.9 = (bf16[1024,128]{1,0:T(8,128)(2,1)S(1)}, bf16[1024,128]{1,0:T(8,128)(2,1)S(1)}, u32[]{:S(2)}, u32[]{:S(2)}) collective-permute-start(bf16[1024,128]{1,0:T(8,128)(2,1)S(1)} %copy-done.3), channel_id=1, source_target_pairs={{0,4},{2,6},{4,0},{6,2},{8,12},{10,14},{12,8},{14,10},{16,20},{18,... | collective-permute-start | bytes 786440 | tf_op jit(solution)/shard_map/ppermute | solution.py:126
  57.0 5.0 %collective-permute-done.5.refs_4_ = bf16[64,1536]{1,0:T(8,128)(2,1)S(1)} collective-permute-done((bf16[64,1536]{1,0:T(8,128)(2,1)S(1)}, bf16[64,1536]{1,0:T(8,128)(2,1)S(1)}, u32[]{:S(2)}, u32[]{:S(2)}) %collective-permute-start.5) | collective-permute-done | bytes 196640 | tf_op jit(solution)/shard_map/ppermute | solution.py:126
  62.0 2.5 %collective-permute-start.12 = (bf16[1024,128]{1,0:T(8,128)(2,1)S(1)}, bf16[1024,128]{1,0:T(8,128)(2,1)S(1)}, u32[]{:S(2)}, u32[]{:S(2)}) collective-permute-start(bf16[1024,128]{1,0:T(8,128)(2,1)S(1)} %collective-permute-done.8.refs_11_), channel_id=1, source_target_pairs={{0,4},{2,6},{4,0},{6,2},{8,12},{10,14},{12,8},{14,10},{16,20},{18,... | collective-permute-start | bytes 786440 | tf_op jit(solution)/shard_map/ppermute | solution.py:126
  64.5 0.9 copy-done.4
  65.4 4.7 %shard_map.112 = (bf16[512,4096]{1,0:T(8,128)(2,1)}, f32[512,128]{1,0:T(8,128)}) custom-call(bf16[64,1536]{1,0:T(8,128)(2,1)S(1)} %copy-done.4, bf16[512,4096]{1,0:T(8,128)(2,1)} %refs_2_.15, bf16[512,512]{1,0:T(8,128)(2,1)} %refs_2_.13, bf16[512,512]{1,0:T(8,128)(2,1)} %refs_3_.11, ...), custom_call_target="tpu_custom_call", output_to_operand_aliasing={{0}: (4, {})} | custom-call | flops 3221225472 | bytes 2097152 | tf_op jit(solution)/shard_map/pallas_call | solution.py:142
  70.1 2.0 %collective-permute-start.25 = (bf16[256,512]{1,0:T(8,128)(2,1)}, bf16[256,512]{1,0:T(8,128)(2,1)}, u32[]{:S(2)}, u32[]{:S(2)}) collective-permute-start(bf16[256,512]{1,0:T(8,128)(2,1)} %broadcast_select_fusion.1), channel_id=1, source_target_pairs={{0,8},{2,10},{4,12},{6,14},{16,24},{18,26},{20,28},{22,30},{1,9},{... | collective-permute-start | bytes 786440 | tf_op jit(solution)/shard_map/ppermute | solution.py:419
  72.1 0.5 collective-permute-start.14
  72.6 0.1 collective-permute-start.13
  72.7 1.8 %collective-permute-done.12.refs_15_ = bf16[1024,128]{1,0:T(8,128)(2,1)S(1)} collective-permute-done((bf16[1024,128]{1,0:T(8,128)(2,1)S(1)}, bf16[1024,128]{1,0:T(8,128)(2,1)S(1)}, u32[]{:S(2)}, u32[]{:S(2)}) %collective-permute-start.12) | collective-permute-done | bytes 262176 | tf_op jit(solution)/shard_map/ppermute | solution.py:126
  74.5 1.0 collective-permute-done.25
  75.6 0.5 collective-permute-start.18
  76.1 0.1 collective-permute-start.17
  76.2 0.4 collective-permute-start.20
  76.6 0.1 collective-permute-start.7
  76.8 1.0 broadcast_select_fusion.2
  77.8 0.6 collective-permute-done.7.refs_7_
  78.3 1.2 collective-permute-start.27
  79.5 0.0 collective-permute-start.26
  79.6 8.6 %shard_map.111.refs_1_ = bf16[64,1024]{1,0:T(8,128)(2,1)S(1)} custom-call(s32[1]{0:T(128)} %copy.27.refs_0_, s32[16]{0:T(128)S(1)} %copy-done.6, bf16[64,1536]{1,0:T(8,128)(2,1)S(1)} %copy-done.5, bf16[64,1536]{1,0:T(8,128)(2,1)S(1)} %collective-permute-done.4.refs_3_, bf16[64,1536]{1,0:T(8,128)(2,1)S(1)} %collective-permute-done.5.refs_4_, ...), custom_call_target="tpu_custom_call" | custom-call | flops 4294967296 | bytes 4194304 | tf_op jit(solution)/shard_map/pallas_call | solution.py:142
  88.2 0.9 collective-permute-start.31
  89.1 5.3 %collective-permute-start.30 = (bf16[64,1024]{1,0:T(8,128)(2,1)S(1)}, bf16[64,1024]{1,0:T(8,128)(2,1)S(1)}, u32[]{:S(2)}, u32[]{:S(2)}) collective-permute-start(bf16[64,1024]{1,0:T(8,128)(2,1)S(1)} %shard_map.111.refs_1_), channel_id=1, source_target_pairs={{0,24},{2,26},{4,28},{6,30},{8,16},{10,18},{12,20},{14,22},{16,8},... | collective-permute-start | bytes 393224 | tf_op jit(solution)/shard_map/ppermute | solution.py:126
  94.4 0.6 collective-permute-start.21
  95.0 0.1 broadcast_select_fusion.5
  95.1 0.8 collective-permute-done.28
  96.0 6.5 %shard_map.113.refs_8_ = bf16[512,4096]{1,0:T(8,128)(2,1)} custom-call(s32[16]{0:T(128)S(1)} %copy-done.6, bf16[64,1024]{1,0:T(8,128)(2,1)S(1)} %shard_map.111.refs_1_, bf16[512,4096]{1,0:T(8,128)(2,1)} %refs_2_.15, bf16[512,4096]{1,0:T(8,128)(2,1)} %get-tuple-element.60.refs_3_.refs_2_, f32[512,128]{1,0:T(8,128)} %get-tuple-element.64.refs_4_, ...), custom_call_target="tpu_custom_call" | custom-call | flops 2147483648 | bytes 2097152 | tf_op jit(solution)/shard_map/pallas_call | solution.py:142
  102.4 6.5 %shard_map.114.refs_8_ = bf16[512,4096]{1,0:T(8,128)(2,1)} custom-call(s32[16]{0:T(128)S(1)} %copy-done.6, bf16[512,4096]{1,0:T(8,128)(2,1)} %refs_2_.15, bf16[512,4096]{1,0:T(8,128)(2,1)} %get-tuple-element.60.refs_3_.refs_2_, f32[512,128]{1,0:T(8,128)} %get-tuple-element.61.refs_3_, ...), custom_call_target="tpu_custom_call", output_to_operand_aliasing={{}: (8, {})} | custom-call | flops 2147483648 | bytes 2097152 | tf_op jit(solution)/shard_map/pallas_call | solution.py:142
  108.9 0.2 collective-permute-start.33
  109.1 1.9 %collective-permute-start.34 = (bf16[64,1024]{1,0:T(8,128)(2,1)S(1)}, bf16[64,1024]{1,0:T(8,128)(2,1)S(1)}, u32[]{:S(2)}, u32[]{:S(2)}) collective-permute-start(bf16[64,1024]{1,0:T(8,128)(2,1)S(1)} %collective-permute-done.29), channel_id=1, source_target_pairs={{0,4},{2,6},{4,0},{6,2},{8,12},{10,14},{12,8},{14,10},{16,20},{18,... | collective-permute-start | bytes 393224 | tf_op jit(solution)/shard_map/ppermute | solution.py:126
  111.0 0.1 collective-permute-start.35
  111.2 0.1 collective-permute-start.32
  111.3 6.8 %shard_map.115.refs_9_ = bf16[512,4096]{1,0:T(8,128)(2,1)} custom-call(s32[16]{0:T(128)S(1)} %copy-done.6, bf16[512,4096]{1,0:T(8,128)(2,1)} %refs_2_.15, bf16[512,4096]{1,0:T(8,128)(2,1)} %get-tuple-element.60.refs_3_.refs_2_, f32[512,128]{1,0:T(8,128)} %get-tuple-element.45.refs_1_.refs_3_, ...), custom_call_target="tpu_custom_call", output_to_operand_aliasing={{}: (8, {})} | custom-call | flops 2147483648 | bytes 2097152 | tf_op jit(solution)/shard_map/pallas_call | solution.py:142
  118.1 2.0 %collective-permute-done.35 = bf16[64,1024]{1,0:T(8,128)(2,1)S(1)} collective-permute-done((bf16[64,1024]{1,0:T(8,128)(2,1)S(1)}, bf16[64,1024]{1,0:T(8,128)(2,1)S(1)}, u32[]{:S(2)}, u32[]{:S(2)}) %collective-permute-start.35) | collective-permute-done | bytes 131104 | tf_op jit(solution)/shard_map/ppermute | solution.py:126
  120.2 0.1 collective-permute-start.36
  120.3 1.7 %collective-permute-done.36.refs_3_ = bf16[3,64,1024]{2,1,0:T(8,128)(2,1)S(1)} collective-permute-done((bf16[3,64,1024]{2,1,0:T(8,128)(2,1)S(1)}, bf16[3,64,1024]{2,1,0:T(8,128)(2,1)S(1)}, u32[]{:S(2)}, u32[]{:S(2)}) %collective-permute-start.36) | collective-permute-done | bytes 393248 | tf_op jit(solution)/shard_map/ppermute | solution.py:126
  122.0 1.3 shard_map.116
  123.3 1.4 %collective-permute-start.37 = (bf16[128,512]{1,0:T(8,128)(2,1)S(1)}, bf16[128,512]{1,0:T(8,128)(2,1)S(1)}, u32[]{:S(2)}, u32[]{:S(2)}) collective-permute-start(bf16[128,512]{1,0:T(8,128)(2,1)S(1)} %get-tuple-element.75.refs_1_), channel_id=1, source_target_pairs={{0,1},{1,0},{2,3},{3,2},{4,5},{5,4},{6,7},{7,6},{8,9},{9,8},{10,11... | collective-permute-start | bytes 393224 | tf_op jit(solution)/shard_map/ppermute | solution.py:526
  124.7 6.5 %shard_map.117 = bf16[512,4096]{1,0:T(8,128)(2,1)} custom-call(s32[16]{0:T(128)S(1)} %copy-done.6, bf16[128,512]{1,0:T(8,128)(2,1)S(1)} %get-tuple-element.75.refs_1_, bf16[512,4096]{1,0:T(8,128)(2,1)} %refs_2_.15, bf16[512,4096]{1,0:T(8,128)(2,1)} %get-tuple-element.60.refs_3_.refs_2_, ...), custom_call_target="tpu_custom_call", output_to_operand_aliasing={{}: (9, {})} | custom-call | flops 2147483648 | bytes 2097152 | tf_op jit(solution)/shard_map/pallas_call | solution.py:142
  131.1 0.7 add_convert_fusion
  (55 shorter events, 0.3 us)
Async XLA Ops:
  3.0 1.0 copy-start.2
  5.2 9.5 %collective-permute-start.2 = (bf16[128,5120]{1,0:T(8,128)(2,1)S(1)}, bf16[128,5120]{1,0:T(8,128)(2,1)S(1)}, u32[]{:S(2)}, u32[]{:S(2)}) collective-permute-start(bf16[128,5120]{1,0:T(8,128)(2,1)S(1)} %shard_map.105), channel_id=1, source_target_pairs={{0,2},{2,0},{4,6},{6,4},{8,10},{10,8},{12,14},{14,12},{16,18},{18,... | collective-permute-start | bytes 3932168 | tf_op jit(solution)/shard_map/ppermute | solution.py:126
  5.8 7.8 %collective-permute-start.22 = (bf16[512,512]{1,0:T(8,128)(2,1)}, bf16[512,512]{1,0:T(8,128)(2,1)}, u32[]{:S(2)}, u32[]{:S(2)}) collective-permute-start(bf16[512,512]{1,0:T(8,128)(2,1)} %refs_3_.11), channel_id=1, source_target_pairs={{0,2},{1,3}} | collective-permute-start | bytes 1572872 | tf_op jit(solution)/shard_map/ppermute | solution.py:419
  8.5 16.0 %collective-permute-start.1 = (bf16[1024,128]{1,0:T(8,128)(2,1)}, bf16[1024,128]{1,0:T(8,128)(2,1)S(1)}, u32[]{:S(2)}, u32[]{:S(2)}) collective-permute-start(bf16[1024,128]{1,0:T(8,128)(2,1)} %get-tuple-element.41), channel_id=1, source_target_pairs={{0,8},{2,10},{4,12},{6,14},{8,0},{10,2},{12,4},{14,6},{16,24},{18,... | collective-permute-start | bytes 786440 | tf_op jit(solution)/shard_map/ppermute | solution.py:126
  9.8 30.0 %collective-permute-start = (bf16[1024,128]{1,0:T(8,128)(2,1)}, bf16[1024,128]{1,0:T(8,128)(2,1)S(1)}, u32[]{:S(2)}, u32[]{:S(2)}) collective-permute-start(bf16[1024,128]{1,0:T(8,128)(2,1)} %get-tuple-element.40), channel_id=1, source_target_pairs={{0,16},{2,18},{4,20},{6,22},{8,24},{10,26},{12,28},{14,30},{16,0},... | collective-permute-start | bytes 786440 | tf_op jit(solution)/shard_map/ppermute | solution.py:126
  12.4 41.9 %collective-permute-start.8 = (bf16[1024,128]{1,0:T(8,128)(2,1)}, bf16[1024,128]{1,0:T(8,128)(2,1)S(1)}, u32[]{:S(2)}, u32[]{:S(2)}) collective-permute-start(bf16[1024,128]{1,0:T(8,128)(2,1)} %get-tuple-element.50), channel_id=1, source_target_pairs={{0,24},{2,26},{4,28},{6,30},{8,16},{10,18},{12,20},{14,22},{16,8},... | collective-permute-start | bytes 786440 | tf_op jit(solution)/shard_map/ppermute | solution.py:126
  15.9 28.6 %collective-permute-start.3 = (bf16[64,6144]{1,0:T(8,128)(2,1)S(1)}, bf16[64,6144]{1,0:T(8,128)(2,1)S(1)}, u32[]{:S(2)}, u32[]{:S(2)}) collective-permute-start(bf16[64,6144]{1,0:T(8,128)(2,1)S(1)} %shard_map.106.refs_0_), channel_id=1, source_target_pairs={{0,4},{2,6},{4,0},{6,2},{8,12},{10,14},{12,8},{14,10},{16,20},{18,... | collective-permute-start | bytes 2359304 | tf_op jit(solution)/shard_map/ppermute | solution.py:126
  17.1 21.3 %collective-permute-start.23 = (bf16[256,512]{1,0:T(8,128)(2,1)S(1)}, bf16[256,512]{1,0:T(8,128)(2,1)S(1)}, u32[]{:S(2)}, u32[]{:S(2)}) collective-permute-start(bf16[256,512]{1,0:T(8,128)(2,1)S(1)} %slice.28), channel_id=1, source_target_pairs={{0,4},{2,6},{1,5},{3,7}} | collective-permute-start | bytes 786440 | tf_op jit(solution)/shard_map/ppermute | solution.py:419
  38.5 9.3 %collective-permute-start.24 = (bf16[256,512]{1,0:T(8,128)(2,1)S(1)}, bf16[256,512]{1,0:T(8,128)(2,1)S(1)}, u32[]{:S(2)}, u32[]{:S(2)}) collective-permute-start(bf16[256,512]{1,0:T(8,128)(2,1)S(1)} %slice_select_fusion), channel_id=1, source_target_pairs={{0,16},{2,18},{4,20},{6,22},{1,17},{3,19},{5,21},{7,23}} | collective-permute-start | bytes 786440 | tf_op jit(solution)/shard_map/ppermute | solution.py:419
  39.8 15.9 %copy-start.3 = (bf16[1024,128]{1,0:T(8,128)(2,1)S(1)}, bf16[1024,128]{1,0:T(8,128)(2,1)}, u32[]{:S(2)}) copy-start(bf16[1024,128]{1,0:T(8,128)(2,1)} %get-tuple-element.51.refs_0_.refs_8_) | copy-start | bytes 786436
  44.5 1.0 copy-start.1
  47.6 8.0 %collective-permute-start.4 = (bf16[64,1536]{1,0:T(8,128)(2,1)S(1)}, bf16[64,1536]{1,0:T(8,128)(2,1)S(1)}, u32[]{:S(2)}, u32[]{:S(2)}) collective-permute-start(bf16[64,1536]{1,0:T(8,128)(2,1)S(1)} %get-tuple-element.47), channel_id=1, source_target_pairs={{0,8},{2,10},{4,12},{6,14},{8,0},{10,2},{12,4},{14,6},{16,24},{18,... | collective-permute-start | bytes 589832 | tf_op jit(solution)/shard_map/ppermute | solution.py:126
  47.7 14.2 %collective-permute-start.5 = (bf16[64,1536]{1,0:T(8,128)(2,1)S(1)}, bf16[64,1536]{1,0:T(8,128)(2,1)S(1)}, u32[]{:S(2)}, u32[]{:S(2)}) collective-permute-start(bf16[64,1536]{1,0:T(8,128)(2,1)S(1)} %get-tuple-element.48), channel_id=1, source_target_pairs={{0,16},{2,18},{4,20},{6,22},{8,24},{10,26},{12,28},{14,30},{16,0},... | collective-permute-start | bytes 589832 | tf_op jit(solution)/shard_map/ppermute | solution.py:126
  48.5 21.6 %collective-permute-start.6 = (bf16[64,1536]{1,0:T(8,128)(2,1)S(1)}, bf16[64,1536]{1,0:T(8,128)(2,1)S(1)}, u32[]{:S(2)}, u32[]{:S(2)}) collective-permute-start(bf16[64,1536]{1,0:T(8,128)(2,1)S(1)} %get-tuple-element.49), channel_id=1, source_target_pairs={{0,24},{2,26},{4,28},{6,30},{8,16},{10,18},{12,20},{14,22},{16,8},... | collective-permute-start | bytes 589832 | tf_op jit(solution)/shard_map/ppermute | solution.py:126
  52.8 19.3 %collective-permute-start.11 = (bf16[1024,128]{1,0:T(8,128)(2,1)S(1)}, bf16[1024,128]{1,0:T(8,128)(2,1)S(1)}, u32[]{:S(2)}, u32[]{:S(2)}) collective-permute-start(bf16[1024,128]{1,0:T(8,128)(2,1)S(1)} %collective-permute-done.refs_0_.refs_10_), channel_id=1, source_target_pairs={{0,4},{2,6},{4,0},{6,2},{8,12},{10,14},{12,8},{14,10},{16,20},{18,... | collective-permute-start | bytes 786440 | tf_op jit(solution)/shard_map/ppermute | solution.py:126
  54.3 17.8 %collective-permute-start.10 = (bf16[1024,128]{1,0:T(8,128)(2,1)S(1)}, bf16[1024,128]{1,0:T(8,128)(2,1)S(1)}, u32[]{:S(2)}, u32[]{:S(2)}) collective-permute-start(bf16[1024,128]{1,0:T(8,128)(2,1)S(1)} %collective-permute-done.1.refs_0_.refs_9_), channel_id=1, source_target_pairs={{0,4},{2,6},{4,0},{6,2},{8,12},{10,14},{12,8},{14,10},{16,20},{18,... | collective-permute-start | bytes 786440 | tf_op jit(solution)/shard_map/ppermute | solution.py:126
  55.6 17.0 %collective-permute-start.9 = (bf16[1024,128]{1,0:T(8,128)(2,1)S(1)}, bf16[1024,128]{1,0:T(8,128)(2,1)S(1)}, u32[]{:S(2)}, u32[]{:S(2)}) collective-permute-start(bf16[1024,128]{1,0:T(8,128)(2,1)S(1)} %copy-done.3), channel_id=1, source_target_pairs={{0,4},{2,6},{4,0},{6,2},{8,12},{10,14},{12,8},{14,10},{16,20},{18,... | collective-permute-start | bytes 786440 | tf_op jit(solution)/shard_map/ppermute | solution.py:126
  62.0 12.6 %collective-permute-start.12 = (bf16[1024,128]{1,0:T(8,128)(2,1)S(1)}, bf16[1024,128]{1,0:T(8,128)(2,1)S(1)}, u32[]{:S(2)}, u32[]{:S(2)}) collective-permute-start(bf16[1024,128]{1,0:T(8,128)(2,1)S(1)} %collective-permute-done.8.refs_11_), channel_id=1, source_target_pairs={{0,4},{2,6},{4,0},{6,2},{8,12},{10,14},{12,8},{14,10},{16,20},{18,... | collective-permute-start | bytes 786440 | tf_op jit(solution)/shard_map/ppermute | solution.py:126
  64.5 0.9 copy-start.4
  65.4 11.2 %copy-start.5 = (bf16[64,1536]{1,0:T(8,128)(2,1)S(1)}, bf16[64,1536]{1,0:T(8,128)(2,1)}, u32[]{:S(2)}) copy-start(bf16[64,1536]{1,0:T(8,128)(2,1)} %get-tuple-element.46.refs_2_.refs_0_) | copy-start | bytes 589828
  65.4 14.2 %copy-start.6 = (s32[16]{0:T(128)S(1)}, s32[16]{0:T(128)}, u32[]{:S(2)}) copy-start(s32[16]{0:T(128)} %refs_0_.12) | copy-start | bytes 196
  70.1 5.5 %collective-permute-start.25 = (bf16[256,512]{1,0:T(8,128)(2,1)}, bf16[256,512]{1,0:T(8,128)(2,1)}, u32[]{:S(2)}, u32[]{:S(2)}) collective-permute-start(bf16[256,512]{1,0:T(8,128)(2,1)} %broadcast_select_fusion.1), channel_id=1, source_target_pairs={{0,8},{2,10},{4,12},{6,14},{16,24},{18,26},{20,28},{22,30},{1,9},{... | collective-permute-start | bytes 786440 | tf_op jit(solution)/shard_map/ppermute | solution.py:419
  72.1 3.5 %collective-permute-start.15 = (bf16[1024,128]{1,0:T(8,128)(2,1)S(1)}, bf16[1024,128]{1,0:T(8,128)(2,1)S(1)}, u32[]{:S(2)}, u32[]{:S(2)}) collective-permute-start(bf16[1024,128]{1,0:T(8,128)(2,1)S(1)} %collective-permute-done.refs_0_.refs_10_), channel_id=1, source_target_pairs={{0,2},{2,0},{4,6},{6,4},{8,10},{10,8},{12,14},{14,12},{16,18},{18,... | collective-permute-start | bytes 786440 | tf_op jit(solution)/shard_map/ppermute | solution.py:126
  72.1 4.0 %collective-permute-start.14 = (bf16[1024,128]{1,0:T(8,128)(2,1)S(1)}, bf16[1024,128]{1,0:T(8,128)(2,1)}, u32[]{:S(2)}, u32[]{:S(2)}) collective-permute-start(bf16[1024,128]{1,0:T(8,128)(2,1)S(1)} %collective-permute-done.1.refs_0_.refs_9_), channel_id=1, source_target_pairs={{0,2},{2,0},{4,6},{6,4},{8,10},{10,8},{12,14},{14,12},{16,18},{18,... | collective-permute-start | bytes 786440 | tf_op jit(solution)/shard_map/ppermute | solution.py:126
  72.6 3.6 %collective-permute-start.13 = (bf16[1024,128]{1,0:T(8,128)(2,1)S(1)}, bf16[1024,128]{1,0:T(8,128)(2,1)}, u32[]{:S(2)}, u32[]{:S(2)}) collective-permute-start(bf16[1024,128]{1,0:T(8,128)(2,1)S(1)} %copy-done.3), channel_id=1, source_target_pairs={{0,2},{2,0},{4,6},{6,4},{8,10},{10,8},{12,14},{14,12},{16,18},{18,... | collective-permute-start | bytes 786440 | tf_op jit(solution)/shard_map/ppermute | solution.py:126
  74.5 2.1 %collective-permute-start.16 = (bf16[1024,128]{1,0:T(8,128)(2,1)S(1)}, bf16[1024,128]{1,0:T(8,128)(2,1)}, u32[]{:S(2)}, u32[]{:S(2)}) collective-permute-start(bf16[1024,128]{1,0:T(8,128)(2,1)S(1)} %collective-permute-done.8.refs_11_), channel_id=1, source_target_pairs={{0,2},{2,0},{4,6},{6,4},{8,10},{10,8},{12,14},{14,12},{16,18},{18,... | collective-permute-start | bytes 786440 | tf_op jit(solution)/shard_map/ppermute | solution.py:126
  75.6 3.9 %collective-permute-start.19 = (bf16[1024,128]{1,0:T(8,128)(2,1)S(1)}, bf16[1024,128]{1,0:T(8,128)(2,1)S(1)}, u32[]{:S(2)}, u32[]{:S(2)}) collective-permute-start(bf16[1024,128]{1,0:T(8,128)(2,1)S(1)} %collective-permute-done.11.refs_14_), channel_id=1, source_target_pairs={{0,2},{2,0},{4,6},{6,4},{8,10},{10,8},{12,14},{14,12},{16,18},{18,... | collective-permute-start | bytes 786440 | tf_op jit(solution)/shard_map/ppermute | solution.py:126
  75.6 4.0 %collective-permute-start.18 = (bf16[1024,128]{1,0:T(8,128)(2,1)S(1)}, bf16[1024,128]{1,0:T(8,128)(2,1)S(1)}, u32[]{:S(2)}, u32[]{:S(2)}) collective-permute-start(bf16[1024,128]{1,0:T(8,128)(2,1)S(1)} %collective-permute-done.10.refs_13_), channel_id=1, source_target_pairs={{0,2},{2,0},{4,6},{6,4},{8,10},{10,8},{12,14},{14,12},{16,18},{18,... | collective-permute-start | bytes 786440 | tf_op jit(solution)/shard_map/ppermute | solution.py:126
  76.1 3.4 %collective-permute-start.17 = (bf16[1024,128]{1,0:T(8,128)(2,1)S(1)}, bf16[1024,128]{1,0:T(8,128)(2,1)S(1)}, u32[]{:S(2)}, u32[]{:S(2)}) collective-permute-start(bf16[1024,128]{1,0:T(8,128)(2,1)S(1)} %collective-permute-done.9.refs_12_), channel_id=1, source_target_pairs={{0,2},{2,0},{4,6},{6,4},{8,10},{10,8},{12,14},{14,12},{16,18},{18,... | collective-permute-start | bytes 786440 | tf_op jit(solution)/shard_map/ppermute | solution.py:126
  76.2 3.4 %collective-permute-start.20 = (bf16[1024,128]{1,0:T(8,128)(2,1)S(1)}, bf16[1024,128]{1,0:T(8,128)(2,1)S(1)}, u32[]{:S(2)}, u32[]{:S(2)}) collective-permute-start(bf16[1024,128]{1,0:T(8,128)(2,1)S(1)} %collective-permute-done.12.refs_15_), channel_id=1, source_target_pairs={{0,2},{2,0},{4,6},{6,4},{8,10},{10,8},{12,14},{14,12},{16,18},{18,... | collective-permute-start | bytes 786440 | tf_op jit(solution)/shard_map/ppermute | solution.py:126
  76.6 1.7 %collective-permute-start.7 = (bf16[64,512]{1,0:T(8,128)(2,1)S(1)}, bf16[64,512]{1,0:T(8,128)(2,1)S(1)}, u32[]{:S(2)}, u32[]{:S(2)}) collective-permute-start(bf16[64,512]{1,0:T(8,128)(2,1)S(1)} %fusion.1.refs_6_), channel_id=1, source_target_pairs={{0,2},{2,0},{4,6},{6,4},{8,10},{10,8},{12,14},{14,12},{16,18},{18,... | collective-permute-start | bytes 196616 | tf_op jit(solution)/shard_map/ppermute | solution.py:126
  78.3 16.1 %collective-permute-start.27 = (bf16[256,512]{1,0:T(8,128)(2,1)S(1)}, bf16[256,512]{1,0:T(8,128)(2,1)S(1)}, u32[]{:S(2)}, u32[]{:S(2)}) collective-permute-start(bf16[256,512]{1,0:T(8,128)(2,1)S(1)} %broadcast_select_fusion.2), channel_id=1, source_target_pairs={{0,4},{2,6},{4,0},{6,2},{8,12},{10,14},{12,8},{14,10},{16,20},{18,... | collective-permute-start | bytes 786440 | tf_op jit(solution)/shard_map/ppermute | solution.py:126
  79.5 14.9 %collective-permute-start.26 = (bf16[256,512]{1,0:T(8,128)(2,1)S(1)}, bf16[256,512]{1,0:T(8,128)(2,1)S(1)}, u32[]{:S(2)}, u32[]{:S(2)}) collective-permute-start(bf16[256,512]{1,0:T(8,128)(2,1)S(1)} %broadcast_select_fusion.2), channel_id=1, source_target_pairs={{0,2},{2,0},{4,6},{6,4},{8,10},{10,8},{12,14},{14,12},{16,18},{18,... | collective-permute-start | bytes 786440 | tf_op jit(solution)/shard_map/ppermute | solution.py:126
  88.2 20.7 %collective-permute-start.31 = (bf16[64,1024]{1,0:T(8,128)(2,1)S(1)}, bf16[64,1024]{1,0:T(8,128)(2,1)S(1)}, u32[]{:S(2)}, u32[]{:S(2)}) collective-permute-start(bf16[64,1024]{1,0:T(8,128)(2,1)S(1)} %shard_map.111.refs_1_), channel_id=1, source_target_pairs={{0,4},{2,6},{4,0},{6,2},{8,12},{10,14},{12,8},{14,10},{16,20},{18,... | collective-permute-start | bytes 393224 | tf_op jit(solution)/shard_map/ppermute | solution.py:126
  89.1 19.8 %collective-permute-start.30 = (bf16[64,1024]{1,0:T(8,128)(2,1)S(1)}, bf16[64,1024]{1,0:T(8,128)(2,1)S(1)}, u32[]{:S(2)}, u32[]{:S(2)}) collective-permute-start(bf16[64,1024]{1,0:T(8,128)(2,1)S(1)} %shard_map.111.refs_1_), channel_id=1, source_target_pairs={{0,24},{2,26},{4,28},{6,30},{8,16},{10,18},{12,20},{14,22},{16,8},... | collective-permute-start | bytes 393224 | tf_op jit(solution)/shard_map/ppermute | solution.py:126
  94.4 14.5 %collective-permute-start.29 = (bf16[64,1024]{1,0:T(8,128)(2,1)S(1)}, bf16[64,1024]{1,0:T(8,128)(2,1)S(1)}, u32[]{:S(2)}, u32[]{:S(2)}) collective-permute-start(bf16[64,1024]{1,0:T(8,128)(2,1)S(1)} %shard_map.111.refs_1_), channel_id=1, source_target_pairs={{0,16},{2,18},{4,20},{6,22},{8,24},{10,26},{12,28},{14,30},{16,0},... | collective-permute-start | bytes 393224 | tf_op jit(solution)/shard_map/ppermute | solution.py:126
  94.4 1.5 %collective-permute-start.28 = (bf16[256,512]{1,0:T(8,128)(2,1)S(1)}, bf16[256,512]{1,0:T(8,128)(2,1)S(1)}, u32[]{:S(2)}, u32[]{:S(2)}) collective-permute-start(bf16[256,512]{1,0:T(8,128)(2,1)S(1)} %collective-permute-done.27), channel_id=1, source_target_pairs={{0,2},{2,0},{4,6},{6,4},{8,10},{10,8},{12,14},{14,12},{16,18},{18,... | collective-permute-start | bytes 786440 | tf_op jit(solution)/shard_map/ppermute | solution.py:126
  94.4 14.5 %collective-permute-start.21 = (bf16[64,1024]{1,0:T(8,128)(2,1)S(1)}, bf16[64,1024]{1,0:T(8,128)(2,1)S(1)}, u32[]{:S(2)}, u32[]{:S(2)}) collective-permute-start(bf16[64,1024]{1,0:T(8,128)(2,1)S(1)} %shard_map.111.refs_1_), channel_id=1, source_target_pairs={{0,8},{2,10},{4,12},{6,14},{8,0},{10,2},{12,4},{14,6},{16,24},{18,... | collective-permute-start | bytes 393224 | tf_op jit(solution)/shard_map/ppermute | solution.py:126
  108.9 9.2 %collective-permute-start.33 = (bf16[64,1024]{1,0:T(8,128)(2,1)S(1)}, bf16[64,1024]{1,0:T(8,128)(2,1)S(1)}, u32[]{:S(2)}, u32[]{:S(2)}) collective-permute-start(bf16[64,1024]{1,0:T(8,128)(2,1)S(1)} %collective-permute-done.21), channel_id=1, source_target_pairs={{0,4},{2,6},{4,0},{6,2},{8,12},{10,14},{12,8},{14,10},{16,20},{18,... | collective-permute-start | bytes 393224 | tf_op jit(solution)/shard_map/ppermute | solution.py:126
  109.1 9.0 %collective-permute-start.34 = (bf16[64,1024]{1,0:T(8,128)(2,1)S(1)}, bf16[64,1024]{1,0:T(8,128)(2,1)S(1)}, u32[]{:S(2)}, u32[]{:S(2)}) collective-permute-start(bf16[64,1024]{1,0:T(8,128)(2,1)S(1)} %collective-permute-done.29), channel_id=1, source_target_pairs={{0,4},{2,6},{4,0},{6,2},{8,12},{10,14},{12,8},{14,10},{16,20},{18,... | collective-permute-start | bytes 393224 | tf_op jit(solution)/shard_map/ppermute | solution.py:126
  111.0 9.1 %collective-permute-start.35 = (bf16[64,1024]{1,0:T(8,128)(2,1)S(1)}, bf16[64,1024]{1,0:T(8,128)(2,1)S(1)}, u32[]{:S(2)}, u32[]{:S(2)}) collective-permute-start(bf16[64,1024]{1,0:T(8,128)(2,1)S(1)} %collective-permute-done.30), channel_id=1, source_target_pairs={{0,4},{2,6},{4,0},{6,2},{8,12},{10,14},{12,8},{14,10},{16,20},{18,... | collective-permute-start | bytes 393224 | tf_op jit(solution)/shard_map/ppermute | solution.py:126
  111.2 10.8 %copy-start = (bf16[4096,512]{1,0:T(8,128)(2,1)S(1)}, bf16[4096,512]{1,0:T(8,128)(2,1)}, u32[]{:S(2)}) copy-start(bf16[4096,512]{1,0:T(8,128)(2,1)} %refs_4_.5) | copy-start | bytes 12582916
  111.2 10.8 %collective-permute-start.32 = (bf16[5,64,1024]{2,1,0:T(8,128)(2,1)S(1)}, bf16[5,64,1024]{2,1,0:T(8,128)(2,1)S(1)}, u32[]{:S(2)}, u32[]{:S(2)}) collective-permute-start(bf16[5,64,1024]{2,1,0:T(8,128)(2,1)S(1)} %bitcast_dynamic-update-slice_fusion.refs_0_), channel_id=1, source_target_pairs={{0,2},{2,0},{4,6},{6,4},{8,10},{10,8},{12,14},{14,12},{16,18},{18,... | collective-permute-start | bytes 1966088 | tf_op jit(solution)/shard_map/ppermute | solution.py:126
  120.2 1.8 %collective-permute-start.36 = (bf16[3,64,1024]{2,1,0:T(8,128)(2,1)S(1)}, bf16[3,64,1024]{2,1,0:T(8,128)(2,1)S(1)}, u32[]{:S(2)}, u32[]{:S(2)}) collective-permute-start(bf16[3,64,1024]{2,1,0:T(8,128)(2,1)S(1)} %pad_maximum_fusion.refs_2_), channel_id=1, source_target_pairs={{0,2},{2,0},{4,6},{6,4},{8,10},{10,8},{12,14},{14,12},{16,18},{18,... | collective-permute-start | bytes 1179656 | tf_op jit(solution)/shard_map/ppermute | solution.py:126
  123.3 7.8 %collective-permute-start.37 = (bf16[128,512]{1,0:T(8,128)(2,1)S(1)}, bf16[128,512]{1,0:T(8,128)(2,1)S(1)}, u32[]{:S(2)}, u32[]{:S(2)}) collective-permute-start(bf16[128,512]{1,0:T(8,128)(2,1)S(1)} %get-tuple-element.75.refs_1_), channel_id=1, source_target_pairs={{0,1},{1,0},{2,3},{3,2},{4,5},{5,4},{6,7},{7,6},{8,9},{9,8},{10,11... | collective-permute-start | bytes 393224 | tf_op jit(solution)/shard_map/ppermute | solution.py:526

commit v3 on v2

--- a/solution.py
+++ b/solution.py
@@ -199,11 +199,14 @@
 
 def kv_pack_kernel(k_ref, v_ref, *refs):
     z, _, _ = place()
-    pairs = []
+    sems, pairs = refs[6], []
     for s, out_ref in enumerate(refs[:4]):
         head = lanes((z ^ s) * 128, 128)
         pairs += [(k_ref.at[:, head], out_ref.at[0:512]), (v_ref.at[:, head], out_ref.at[512:1024])]
-    copy_all(pairs, refs[4])
+    for i, out_ref in enumerate(refs[4:6]):
+        here = slice(i * 256, (i + 1) * 256)
+        pairs += [(k_ref.at[here], out_ref.at[0:256]), (v_ref.at[here], out_ref.at[256:512])]
+    copy_all(pairs, sems)
 
 
 def x_pack_kernel(owner, got_ref, q_ref, k_ref, v_ref, send_ref, sems):
@@ -223,10 +226,11 @@
 
     @pl.when(owner_c != c)
     def _():
-        send_ref[:, 0:4096] = got_ref[rows((1 - x) * 64, 64), 0:4096]
+        pairs = [(got_ref.at[rows((1 - x) * 64, 64), 0:4096], send_ref.at[:, 0:4096])]
         for i in range(2):
             to = 4096 + i * 1024
-            send_ref[:, to : to + 1024] = got_ref[i * 64 : (i + 1) * 64, 4096:5120]
+            pairs += [(got_ref.at[i * 64 : (i + 1) * 64, 4096:5120], send_ref.at[:, to : to + 1024])]
+        copy_all(pairs, sems)
 
 
 def z_pack_kernel(owner, c_ref, x_ref, q_ref, k_ref, v_ref, *refs):
@@ -255,12 +259,14 @@
 
     @pl.when((owner_x == x) & (owner_c != c))
     def _():
+        pairs = []
         for s, out_ref in enumerate(outs):
             j = z ^ s
-            out_ref[:, 0:1024] = c_ref[rows(x * 64, 64), lanes(j * 1024, 1024)]
+            pairs.append((c_ref.at[rows(x * 64, 64), lanes(j * 1024, 1024)], out_ref.at[:, 0:1024]))
             for i in range(4):
-                part = c_ref[i // 2 * 64 : (i // 2 + 1) * 64, lanes(4096 + i % 2 * 512 + j * 128, 128)]
-                out_ref[:, 1024 + i * 128 : 1152 + i * 128] = part
+                part = c_ref.at[i // 2 * 64 : (i // 2 + 1) * 64, lanes(4096 + i % 2 * 512 + j * 128, 128)]
+                pairs.append((part, out_ref.at[:, 1024 + i * 128 : 1152 + i * 128]))
+        copy_all(pairs, sems)
 
 
 def ones_beside(values):
@@ -268,7 +274,7 @@
 
 
 def read_kernel(owner, lengths, *refs):
-    asked, (own_kv, other_kv), parts, out_ref, q_ref = refs[:4], refs[4:6], refs[6:22], refs[22], refs[23]
+    asked, (own_kv, other_kv), pairs, (out_ref, q_ref) = refs[:4], refs[4:6], refs[6:14], refs[14:]
     z, x, c = place()
     step = pl.program_id(0)
     at = z ^ (owner[0] // 4)
@@ -290,12 +296,13 @@
             total = total + jnp.dot(weights(s, peak), ones_beside(v), preferred_element_type=F32)
         found.append((peak, total))
 
-    for pair in range(8):
+    for pair, ref in enumerate(pairs):
         scores, values = [], []
-        for i in (2 * pair, 2 * pair + 1):
-            block = ((z ^ (i % 4)) * 2 + (x ^ (i // 4 % 2))) * 2 + (c ^ (i // 8))
-            scores.append(jnp.where(column < lengths[block], dot_t(q, parts[i][0:512, :]), masked_score))
-            values.append(parts[i][512:1024, :])
+        for i in range(2):
+            block = ((z ^ (pair % 2 * 2 + i)) * 2 + (x ^ (pair // 2 % 2))) * 2 + (c ^ (pair // 4))
+            k, v = ref[i * 1024 : i * 1024 + 512, :], ref[i * 1024 + 512 : (i + 1) * 1024, :]
+            scores.append(jnp.where(column < lengths[block], dot_t(q, k), masked_score))
+            values.append(v)
         add(scores, values)
     row_at = lax.broadcasted_iota(jnp.int32, (256, 64), 0) % 64 + x * 128 + c * 64
     column = lax.broadcasted_iota(jnp.int32, (256, 64), 1)
@@ -376,35 +383,34 @@
             found = jnp.where(lane == h, peak + jnp.log2(total[:, 128:]), found)
         lse_ref[...] = found
 
-    @pl.when(pl.program_id(0) == 0)
+    @pl.when(pl.program_id(1) == 0)
     def _():
         half(0)
 
-    @pl.when(pl.program_id(0) == 1)
+    @pl.when(pl.program_id(1) == 1)
     def _():
         half(1)
 
 
-def anchor_kernel(lengths, q_ref, own_ref, lse_ref, near_k_ref, near_v_ref, far_k_ref, far_v_ref, *rest):
+def anchor_kernel(lengths, q_ref, own_ref, lse_ref, near_ref, far_ref, *rest):
     o_ref = rest[-1]
     host = lax.axis_index("hst")
+    _, x, _ = place()
     anchor_len = jnp.where(host > 0, lengths[0], 0)
-    own_len = lengths[host] - pl.program_id(0) * 256
-    _, x, _ = place()
+    own_len = lengths[host] - pl.program_id(1) * 256
+    valid = lax.broadcasted_iota(jnp.int32, (256, 128), 0) < own_len
     column = lax.broadcasted_iota(jnp.int32, (1, 256), 1)
-    parts = [
-        (near_k_ref, column + x * 256 < anchor_len, ones_beside(near_v_ref[...])),
-        (far_k_ref, column + (1 - x) * 256 < anchor_len, ones_beside(far_v_ref[...])),
-    ]
-    valid = lax.broadcasted_iota(jnp.int32, (256, 128), 0) < own_len
+    values = ones_beside(jnp.concatenate([near_ref[256:512, :], far_ref[256:512, :]], axis=0))
+    near_ok, far_ok = column + x * 256 < anchor_len, column + (1 - x) * 256 < anchor_len
     for h in range(8):
         at = slice(h * 128, (h + 1) * 128)
-        scores = [jnp.where(ok, dot_t(q_ref[:, at], k_ref[...]), masked_score) for k_ref, ok, _ in parts]
+        q = q_ref[:, at]
+        near = jnp.where(near_ok, dot_t(q, near_ref[0:256, :]), masked_score)
+        far = jnp.where(far_ok, dot_t(q, far_ref[0:256, :]), masked_score)
         lse = jnp.broadcast_to(lse_ref[:, h : h + 1], (256, 128))
-        peak = jnp.maximum(row_max(scores), lse)
-        total = 0
-        for s, (_, _, values) in zip(scores, parts):
-            total = total + jnp.dot(weights(s, peak), values, preferred_element_type=F32)
+        peak = jnp.maximum(row_max([near, far]), lse)
+        w = jnp.concatenate([weights(near, peak), weights(far, peak)], axis=1)
+        total = jnp.dot(w, values, preferred_element_type=F32)
         own = jnp.exp2(lse - peak)
         result = (total[:, :128] + own * own_ref[:, at].astype(F32)) / (total[:, 128:] + own)
         o_ref[:, at] = jnp.where(valid, result, 0.0).astype(BF16)
@@ -425,97 +431,97 @@
 
     def own(g, *others):
         nonlocal own_out
-        block = pl.BlockSpec((256, 1024), lambda i, g=g: (i, g))
-        head = pl.BlockSpec((512, 128), lambda i, g=g: (0, g))
+        block = pl.BlockSpec((256, 1024), lambda j, i, g=g: (i, 2 * g + j))
+        head = pl.BlockSpec((512, 128), lambda j, i, g=g: (0, 2 * g + j))
         own_out, found = call(
-            own_kernel, [pltpu.HBM((512, 4096), BF16), pltpu.HBM((512, 128), F32)],
+            own_kernel, [pltpu.HBM((512, 4096), BF16), pltpu.HBM((1024, 128), F32)],
             [block, head, head] + ([] if g == 0 else [ANY]),
-            [block, pl.BlockSpec((256, 128), lambda i: (i, 0))],
+            [block, pl.BlockSpec((256, 128), lambda j, i: (2 * j + i, 0))],
             in_hbm(ctx_query, ctx_key, context_value) + ([] if g == 0 else in_hbm(own_out)),
-            after=others, grid=(2,), aliases={} if g == 0 else {3: 0}, flops=4 * 4096 * 768 * 256, data=2**21, vmem=16,
+            after=others, grid=(2, 2), aliases={} if g == 0 else {3: 0}, flops=8 * 4096 * 768 * 256, data=2**22, vmem=16,
         )
         lse.append(found)
         return found
 
     ctx_out = None
 
-    def encode(g, *others):
+    def encode(g, n, *others):
         nonlocal ctx_out
-        block = pl.BlockSpec((256, 1024), lambda i, _, g=g: (i, g))
-        head = pl.BlockSpec((256, 128), lambda i, _, g=g: (0, g))
+        block = pl.BlockSpec((256, 1024), lambda j, i, _, g=g: (i, g + j))
+        half = pl.BlockSpec((512, 128), lambda j, i, _, g=g: (0, g + j))
+        logs = pl.BlockSpec((256, 128), lambda j, i, _, g=g: ((g % 2 + j) * 2 + i, 0))
         ctx_out = call(
             anchor_kernel, pltpu.HBM((512, 4096), BF16),
-            [block, block, pl.BlockSpec((256, 128), lambda i, _: (i, 0))] + [head] * 4
-            + ([] if g == 0 else [ANY]),
+            [block, block, logs, half, half] + ([] if g == 0 else [ANY]),
             block,
-            in_hbm(ctx_query, own_out, lse[g]) + anchor + ([] if g == 0 else in_hbm(ctx_out)),
-            scalars=[lengths], after=others, grid=(2,), aliases={} if g == 0 else {7: 0},
-            flops=4 * 4096 * 512 * 256, data=2**21, vmem=16,
+            in_hbm(ctx_query, own_out, lse[g // 2]) + halves + ([] if g == 0 else in_hbm(ctx_out)),
+            scalars=[lengths], after=others, grid=(n, 2), aliases={} if g == 0 else {5: 0},
+            flops=n * 4 * 4096 * 512 * 256, data=2**21, vmem=16,
         )
         return ctx_out
 
     kv = call(
-        kv_pack_kernel, [pltpu.HBM((1024, 128), BF16)] + [shape((1024, 128), BF16)] * 3, [ANY] * 2, [WHOLE] * 4,
-        in_hbm(ctx_key, context_value), scratch=[dma((8,))],
+        kv_pack_kernel,
+        [pltpu.HBM((1024, 128), BF16)] + [shape((1024, 128), BF16)] * 3 + [pltpu.HBM((512, 512), BF16)] * 2,
+        [ANY] * 2, [WHOLE] * 6, in_hbm(ctx_key, context_value), scratch=[dma((12,))],
     )
     packed = call(
         ask_pack_kernel, shape((128, 5120), BF16), [ANY] * 3, WHOLE, in_hbm(*ask), after=[kv[0]], scratch=[dma((6,))]
     )
-    got_c = swap(packed, 1)
+    got_c = in_hbm(swap(packed, 1))
     kv_z = [kv[0]] + [swap(kv[s], 4 * s) for s in (1, 2, 3)]
+    got = send(after(kv[5], packed), [(0, 2)])
     sent = call(
-        x_pack_kernel, shape((64, 6144), BF16), [WHOLE] + [ANY] * 3, WHOLE, in_vmem(got_c) + in_hbm(*ask),
-        scalars=[owner], scratch=[dma((5,))],
+        x_pack_kernel, shape((64, 6144), BF16), [ANY] * 4, WHOLE, got_c + in_hbm(*ask), scalars=[owner],
+        scratch=[dma((5,))],
     )
     got_x = swap(sent, 2)
 
-    whole = jnp.where(c == 0, ctx_key, send(after(context_value, packed), [(0, 1)]))
-    got = send(after(whole[256:], sent), [(0, 2), (1, 3)])
-    quarter = jnp.where(x == 0, whole[:256], got)
     tick = own(0, sent)
-    got = send(after(quarter, tick), [(i, i + 8) for i in range(4)])
-    quarter = jnp.where(z == 0, quarter, got)
-    own(1, kv_z[1])
-    tick = own(2, kv_z[2])
+    near = jnp.where(x == 0, kv[4], after(got, tick))
+    got = send(near, [(i, i + 8) for i in (0, 2)])
+    first = jnp.concatenate([kv[0], after(kv_z[1], tick)], axis=0)
+    first_x = swap(first, 2)
+    tick = own(1, near, kv_z[1])
     parts = call(
-        z_pack_kernel, [pltpu.HBM((64, 1536), BF16)] + [shape((64, 1536), BF16)] * 3, [WHOLE] * 2 + [ANY] * 3, [WHOLE] * 4,
-        in_vmem(got_c, got_x) + in_hbm(*ask), scalars=[owner], after=[tick], scratch=[dma((20,))],
+        z_pack_kernel, [pltpu.HBM((64, 1536), BF16)] + [shape((64, 1536), BF16)] * 3, [ANY, WHOLE] + [ANY] * 3,
+        [WHOLE] * 4, got_c + in_vmem(got_x) + in_hbm(*ask), scalars=[owner], after=[tick], scratch=[dma((20,))],
     )
     asked = [parts[0]] + [swap(parts[s], 4 * s) for s in (1, 2, 3)]
-    tick = own(3, parts[0])
-    kv_x = [swap(after(part, parts[0]), 2) for part in kv_z]
-    kv_near = kv_z + kv_x
-    kv_far = [swap(after(part, parts[0]), 1) for part in kv_near]
+    near = jnp.where(z == 0, near, after(got, parts[0]))
+    got = send(near, [(i, i + 4) for i in (0, 2, 8, 10)])
+    second = jnp.concatenate([after(kv_z[2], parts[0]), kv_z[3]], axis=0)
+    second_x = swap(second, 2)
 
     level = z ^ (owner[0] // 4)
     own_kv = asked[0][:, 1024:]
     for s in (1, 2, 3):
         own_kv = jnp.where(level == s, asked[s][:, 1024:], own_kv)
     other_kv = swap(own_kv, 1)
+    pairs = [first, second, first_x, second_x]
+    pairs += [swap(after(part, own_kv), 1) for part in pairs]
+    near = jnp.where(z % 2 == 0, near, after(got, own_kv))
+    far = swap(near, 2)
+    near_c = send(near, [(i, i + 1) for i in range(0, 16, 2)])
     answer = call(
-        read_kernel, shape((64, 1024), BF16), [WHOLE] * 22, pl.BlockSpec((64, 512), lambda i, *_: (0, i)),
-        [asked[0]] + in_vmem(*asked[1:], own_kv, other_kv) + kv_near[:1] + in_vmem(*kv_near[1:], *kv_far),
+        read_kernel, shape((64, 1024), BF16), [WHOLE] * 14, pl.BlockSpec((64, 512), lambda i, *_: (0, i)),
+        [asked[0]] + in_vmem(*asked[1:], own_kv, other_kv, *pairs),
         scalars=[owner, lengths], grid=(2,),
         scratch=[pltpu.VMEM((256, 128), BF16)], flops=4 * 512 * 8192 * 256, data=2**22, vmem=20,
     )
 
-    got = send(after(quarter, tick), [(i, i + 4) for i in (0, 1, 2, 3, 8, 9, 10, 11)])
-    near = jnp.where(z % 2 == 0, quarter, got)
-    far = swap(near, 2)
-    anchor = []
-    for half in (near, far):
-        got = swap(half, 1)
-        anchor += [jnp.where(c == 0, half, got), jnp.where(c == 0, got, half)]
+    far = after(far, answer)
+    halves = [jnp.where(c == 0, near, after(near_c, answer))]
+    halves.append(jnp.where(c == 0, far, send(far, [(i, i + 1) for i in range(0, 16, 2)])))
 
     across = [swap(answer, 4 * s) for s in (1, 2, 3)]
     side = swap(answer, 2)
-    encode(0, answer)
-    tick = encode(1)
+    tick = encode(0, 2, answer)
     across = [after(part, tick) for part in across]
     sides = [swap(part, 2) for part in across]
     near = jnp.stack([answer] + across + [after(side, tick)])
     near_far = swap(near, 1)
-    tick = encode(2)
+    tick = encode(2, 1)
     side = jnp.stack([after(part, tick) for part in sides])
     side_far = swap(side, 1)
     keep, sent = call(
@@ -524,7 +530,7 @@
         flops=2 * 256 * 4096 * 512, data=2**22, vmem=16,
     )
     got = lax.ppermute(sent, "tensor", [(0, 1), (1, 0)])
-    tick = encode(3, sent)
+    tick = encode(3, 1, sent)
     return ctx_out, (keep + after(got, tick).astype(F32)).astype(BF16)
 
 

time: 132 us -> 119 us (0.902)
  waiting for transfers between devices: 23.1 us -> 8.03 us
  Pallas kernels: 61.8 us -> 56.9 us
  other arithmetic: 3.69 us -> 6.61 us
  starting transfers between devices: 38.7 us -> 41.3 us
    ppermute x4 -> x5, waiting for transfers between devices: 10.3 us -> 0.24 us  [send(): return lax.ppermute(array, 'hst', pairs)]
    ppermute x4 -> x5, starting transfers between devices: 8.78 us -> 15.1 us  [send(): return lax.ppermute(array, 'hst', pairs)]
    ppermute x33 -> x25, waiting for transfers between devices: 12.8 us -> 7.79 us  [swap(): return lax.ppermute(array, 'hst', [(i, i ^ bit) for i in range(16)])]
    pallas_call x14 -> x11, Pallas kernels: 61.8 us -> 56.9 us  [call(): pl.pallas_call(body, grid_spec=pltpu.PrefetchScalarGridSpec(num_scalar_pr...]
    ppermute x33 -> x25, starting transfers between devices: 28.6 us -> 24.5 us  [swap(): return lax.ppermute(array, 'hst', [(i, i ^ bit) for i in range(16)])]
    select_n x6 -> x5, other arithmetic: 2.94 us -> 5.03 us  [the longest x1 1.89 us: body(): near = jnp.where(z % 2 == 0, near, after(got, own_kv))]
    unnamed x18 -> x20, local copies, waits for them, and re-layouts: 2.88 us -> 3.04 us
  transfers between devices with their start and end apart: 38 -> 31, of which waited for: 9 -> 5; matrix products, arithmetic and copies ran while one was open for 2% -> 7% of each run, Pallas kernels for 43% -> 43%
where the time goes in v3:
time: 119 us
  Pallas kernels  56.9 us (48%)
  starting transfers between devices  41.3 us (35%)
  waiting for transfers between devices  8.03 us (7%)
  other arithmetic  6.61 us (6%)
  local copies, waits for them, and re-layouts  4.07 us (3%)
  between operations  1.65 us (1%)
    pallas_call x11, Pallas kernels, call(): pl.pallas_call(body, grid_spec=pltpu.PrefetchScalarGridSpec(num_scalar_pr...  56.9 us
    ppermute x25, starting transfers between devices, swap(): return lax.ppermute(array, 'hst', [(i, i ^ bit) for i in range(16)])  24.5 us
    ppermute x5, starting transfers between devices, send(): return lax.ppermute(array, 'hst', pairs)  15.1 us
    ppermute x25, waiting for transfers between devices, swap(): return lax.ppermute(array, 'hst', [(i, i ^ bit) for i in range(16)])  7.79 us
    unnamed x20, local copies, waits for them, and re-layouts  3.04 us
  transfers between devices with their start and end apart: 31, of which 5 were waited for; matrix products, arithmetic and copies ran while one was open for 7% of the time, Pallas kernels for 43%

profile of v3, /device:TPU:0, one launch (start us, length us, event | category | flops | bytes accessed | tf_op | source)
XLA Modules:
  0.0 118.6 jit_solution(15570839094059459764)
XLA Ops:
  0.6 2.8 %shard_map.104 = (bf16[1024,128]{1,0:T(8,128)(2,1)}, bf16[1024,128]{1,0:T(8,128)(2,1)S(1)}, bf16[1024,128]{1,0:T(8,128)(2,1)S(1)}, bf16[1024,128]{1,0:T(8,128)(2...) custom-call(bf16[512,512]{1,0:T(8,128)(2,1)} %refs_3_.7, bf16[512,512]{1,0:T(8,128)(2,1)} %refs_4_.5), custom_call_target="tpu_custom_call" | custom-call | tf_op jit(solution)/shard_map/pallas_call | solution.py:142
  3.4 0.9 copy-done.2
  4.4 1.3 %shard_map.105 = bf16[128,5120]{1,0:T(8,128)(2,1)S(1)} custom-call(bf16[1024,128]{1,0:T(8,128)(2,1)S(1)} %copy-done.2, bf16[1,256,4096]{2,1,0:T(8,128)(2,1)} %refs_4_.6, bf16[1,256,512]{2,1,0:T(8,128)(2,1)} %refs_5_.1, bf16[1,256,512]{2,1,0:T(8,128)(2,1)} %refs_6_.1), custom_call_target="tpu_custom_call" | custom-call | tf_op jit(solution)/shard_map/pallas_call | solution.py:142
  5.7 0.5 collective-permute-start.1
  6.3 5.2 %collective-permute-start = (bf16[512,512]{1,0:T(8,128)(2,1)}, bf16[512,512]{1,0:T(8,128)(2,1)}, u32[]{:S(2)}, u32[]{:S(2)}) collective-permute-start(bf16[512,512]{1,0:T(8,128)(2,1)} %get-tuple-element.41), channel_id=1, source_target_pairs={{0,4},{1,5}} | collective-permute-start | bytes 1572872 | tf_op jit(solution)/shard_map/ppermute | solution.py:425
  11.5 0.0 collective-permute-start.2
  11.5 1.4 %collective-permute-start.8 = (bf16[1024,128]{1,0:T(8,128)(2,1)S(1)}, bf16[1024,128]{1,0:T(8,128)(2,1)}, u32[]{:S(2)}, u32[]{:S(2)}) collective-permute-start(bf16[1024,128]{1,0:T(8,128)(2,1)S(1)} %get-tuple-element.52), channel_id=1, source_target_pairs={{0,16},{2,18},{4,20},{6,22},{8,24},{10,26},{12,28},{14,30},{16,0},... | collective-permute-start | bytes 786440 | tf_op jit(solution)/shard_map/ppermute | solution.py:126
  12.9 3.0 %collective-permute-start.9 = (bf16[1024,128]{1,0:T(8,128)(2,1)S(1)}, bf16[1024,128]{1,0:T(8,128)(2,1)}, u32[]{:S(2)}, u32[]{:S(2)}) collective-permute-start(bf16[1024,128]{1,0:T(8,128)(2,1)S(1)} %get-tuple-element.54), channel_id=1, source_target_pairs={{0,24},{2,26},{4,28},{6,30},{8,16},{10,18},{12,20},{14,22},{16,8},... | collective-permute-start | bytes 786440 | tf_op jit(solution)/shard_map/ppermute | solution.py:126
  16.6 0.0 collective-permute-done.1.refs_1_.refs_2_
  16.6 1.2 shard_map.106.refs_0_
  17.8 0.0 copy-start.6
  17.8 0.1 collective-permute-start.3
  17.8 7.7 %shard_map.107 = (bf16[512,4096]{1,0:T(8,128)(2,1)}, f32[1024,128]{1,0:T(8,128)}) custom-call(bf16[64,6144]{1,0:T(8,128)(2,1)S(1)} %shard_map.106.refs_0_, bf16[512,4096]{1,0:T(8,128)(2,1)} %refs_2_.11, bf16[512,512]{1,0:T(8,128)(2,1)} %refs_3_.7, bf16[512,512]{1,0:T(8,128)(2,1)} %refs_4_.5), custom_call_target="tpu_custom_call" | custom-call | flops 6442450944 | bytes 4194304 | tf_op jit(solution)/shard_map/pallas_call | solution.py:142
  25.6 0.1 broadcast_select_fusion.4.refs_0_
  25.6 2.3 %collective-permute-start.17 = (bf16[512,512]{1,0:T(8,128)(2,1)S(1)}, bf16[512,512]{1,0:T(8,128)(2,1)S(1)}, u32[]{:S(2)}, u32[]{:S(2)}) collective-permute-start(bf16[512,512]{1,0:T(8,128)(2,1)S(1)} %broadcast_select_fusion.4.refs_0_), channel_id=1, source_target_pairs={{0,16},{4,20},{1,17},{5,21}} | collective-permute-start | bytes 1572872 | tf_op jit(solution)/shard_map/ppermute | solution.py:425
  28.0 0.0 collective-permute-done.2.refs_1_
  28.0 2.1 %collective-permute-start.10 = (bf16[2048,128]{1,0:T(8,128)(2,1)S(1)}, bf16[2048,128]{1,0:T(8,128)(2,1)S(1)}, u32[]{:S(2)}, u32[]{:S(2)}) collective-permute-start(bf16[2048,128]{1,0:T(8,128)(2,1)S(1)} %constant_dynamic-update-slice_fusion.refs_8_), channel_id=1, source_target_pairs={{0,4},{2,6},{4,0},{6,2},{8,12},{10,14},{12,8},{14,10},{16,20},{18,... | collective-permute-start | bytes 1572872 | tf_op jit(solution)/shard_map/ppermute | solution.py:126
  30.1 7.6 %shard_map.108 = (bf16[512,4096]{1,0:T(8,128)(2,1)}, f32[1024,128]{1,0:T(8,128)}) custom-call(bf16[512,512]{1,0:T(8,128)(2,1)S(1)} %broadcast_select_fusion.4.refs_0_, bf16[1024,128]{1,0:T(8,128)(2,1)S(1)} %collective-permute-done.2.refs_1_, bf16[512,4096]{1,0:T(8,128)(2,1)} %refs_2_.11, bf16[512,512]{1,0:T(8,128)(2,1)} %refs_3_.7, ...), custom_call_target="tpu_custom_call", output_to_operand_aliasing={{0}: (5, {})} | custom-call | flops 6442450944 | bytes 4194304 | tf_op jit(solution)/shard_map/pallas_call | solution.py:142
  37.7 0.6 collective-permute-done.3.refs_3_
  38.3 1.0 copy-done
  39.4 2.1 %shard_map.109 = (bf16[64,1536]{1,0:T(8,128)(2,1)}, bf16[64,1536]{1,0:T(8,128)(2,1)S(1)}, bf16[64,1536]{1,0:T(8,128)(2,1)S(1)}, bf16[64,1536]{1,0:T(8,128)(2,1)S(1)}) custom-call(s32[1]{0:T(128)} %copy.23.refs_0_, f32[1024,128]{1,0:T(8,128)S(1)} %copy-done, bf16[128,5120]{1,0:T(8,128)(2,1)} %collective-permute-done.1.refs_1_.refs_2_, ...), custom_call_target="tpu_custom_call" | custom-call | tf_op jit(solution)/shard_map/pallas_call | solution.py:142
  41.5 0.0 collective-permute-done.17
  41.5 0.1 collective-permute-start.4
  41.6 1.4 %collective-permute-start.5 = (bf16[64,1536]{1,0:T(8,128)(2,1)S(1)}, bf16[64,1536]{1,0:T(8,128)(2,1)S(1)}, u32[]{:S(2)}, u32[]{:S(2)}) collective-permute-start(bf16[64,1536]{1,0:T(8,128)(2,1)S(1)} %get-tuple-element.49), channel_id=1, source_target_pairs={{0,16},{2,18},{4,20},{6,22},{8,24},{10,26},{12,28},{14,30},{16,0},... | collective-permute-start | bytes 589832 | tf_op jit(solution)/shard_map/ppermute | solution.py:126
  43.0 0.0 collective-permute-done.8
  43.0 3.0 %collective-permute-start.6 = (bf16[64,1536]{1,0:T(8,128)(2,1)S(1)}, bf16[64,1536]{1,0:T(8,128)(2,1)S(1)}, u32[]{:S(2)}, u32[]{:S(2)}) collective-permute-start(bf16[64,1536]{1,0:T(8,128)(2,1)S(1)} %get-tuple-element.50), channel_id=1, source_target_pairs={{0,24},{2,26},{4,28},{6,30},{8,16},{10,18},{12,20},{14,22},{16,8},... | collective-permute-start | bytes 589832 | tf_op jit(solution)/shard_map/ppermute | solution.py:126
  45.9 1.0 constant_dynamic-update-slice_fusion.3
  46.9 1.0 constant_dynamic-update-slice_fusion.2.refs_9_
  47.9 0.1 collective-permute-start.11
  48.0 0.9 broadcast_select_fusion
  48.8 0.0 collective-permute-done.4.refs_3_
  48.9 3.3 %collective-permute-start.18 = (bf16[512,512]{1,0:T(8,128)(2,1)}, bf16[512,512]{1,0:T(8,128)(2,1)}, u32[]{:S(2)}, u32[]{:S(2)}) collective-permute-start(bf16[512,512]{1,0:T(8,128)(2,1)} %broadcast_select_fusion), channel_id=1, source_target_pairs={{0,8},{4,12},{16,24},{20,28},{1,9},{5,13},{17,25},{21,29}} | collective-permute-start | bytes 1572872 | tf_op jit(solution)/shard_map/ppermute | solution.py:425
  52.2 3.9 %collective-permute-done.5.refs_4_ = bf16[64,1536]{1,0:T(8,128)(2,1)S(1)} collective-permute-done((bf16[64,1536]{1,0:T(8,128)(2,1)S(1)}, bf16[64,1536]{1,0:T(8,128)(2,1)S(1)}, u32[]{:S(2)}, u32[]{:S(2)}) %collective-permute-start.5) | collective-permute-done | bytes 196640 | tf_op jit(solution)/shard_map/ppermute | solution.py:126
  56.1 0.0 collective-permute-done.6.refs_5_
  56.1 0.9 fusion.1.refs_6_
  57.0 0.1 collective-permute-start.14
  57.1 0.5 collective-permute-start.13
  57.6 0.1 collective-permute-start.12
  57.6 0.4 collective-permute-start.15
  58.1 0.2 collective-permute-done.18
  58.3 1.9 %broadcast_select_fusion.1 = bf16[512,512]{1,0:T(8,128)(2,1)} fusion(bf16[512,512]{1,0:T(8,128)(2,1)} %broadcast_select_fusion, bf16[512,512]{1,0:T(8,128)(2,1)} %collective-permute-done.18, pred[]{:T(512)S(6)} %eq.31), kind=kLoop, calls=%fused_computation.1 | loop fusion | flops 262144 | bytes 1572865 | tf_op jit(solution)/shard_map/jit(_where)/select_n | solution.py:503
  60.2 1.6 %collective-permute-start.20 = (bf16[512,512]{1,0:T(8,128)(2,1)}, bf16[512,512]{1,0:T(8,128)(2,1)}, u32[]{:S(2)}, u32[]{:S(2)}) collective-permute-start(bf16[512,512]{1,0:T(8,128)(2,1)} %broadcast_select_fusion.1), channel_id=1, source_target_pairs={{0,4},{2,6},{4,0},{6,2},{8,12},{10,14},{12,8},{14,10},{16,20},{18,... | collective-permute-start | bytes 1572872 | tf_op jit(solution)/shard_map/ppermute | solution.py:126
  61.8 2.5 %collective-permute-start.19 = (bf16[512,512]{1,0:T(8,128)(2,1)}, bf16[512,512]{1,0:T(8,128)(2,1)}, u32[]{:S(2)}, u32[]{:S(2)}) collective-permute-start(bf16[512,512]{1,0:T(8,128)(2,1)} %broadcast_select_fusion.1), channel_id=1, source_target_pairs={{0,2},{4,6},{8,10},{12,14},{16,18},{20,22},{24,26},{28,30},{1,3},{... | collective-permute-start | bytes 1572872 | tf_op jit(solution)/shard_map/ppermute | solution.py:425
  64.3 8.9 %shard_map.110.refs_1_ = bf16[64,1024]{1,0:T(8,128)(2,1)S(1)} custom-call(s32[1]{0:T(128)} %copy.23.refs_0_, s32[16]{0:T(128)S(1)} %copy-done.5, bf16[64,1536]{1,0:T(8,128)(2,1)S(1)} %copy-done.4, bf16[64,1536]{1,0:T(8,128)(2,1)S(1)} %collective-permute-done.4.refs_3_, bf16[64,1536]{1,0:T(8,128)(2,1)S(1)} %collective-permute-done.5.refs_4_, ...), custom_call_target="tpu_custom_call" | custom-call | flops 4294967296 | bytes 4194304 | tf_op jit(solution)/shard_map/pallas_call | solution.py:142
  73.2 1.6 %collective-permute-done.20 = bf16[512,512]{1,0:T(8,128)(2,1)} collective-permute-done((bf16[512,512]{1,0:T(8,128)(2,1)}, bf16[512,512]{1,0:T(8,128)(2,1)}, u32[]{:S(2)}, u32[]{:S(2)}) %collective-permute-start.20) | collective-permute-done | bytes 524320 | tf_op jit(solution)/shard_map/ppermute | solution.py:126
  74.9 1.8 %collective-permute-start.21 = (bf16[512,512]{1,0:T(8,128)(2,1)}, bf16[512,512]{1,0:T(8,128)(2,1)S(1)}, u32[]{:S(2)}, u32[]{:S(2)}) collective-permute-start(bf16[512,512]{1,0:T(8,128)(2,1)} %collective-permute-done.20), channel_id=1, source_target_pairs={{0,2},{4,6},{8,10},{12,14},{16,18},{20,22},{24,26},{28,30},{1,3},{... | collective-permute-start | bytes 1572872 | tf_op jit(solution)/shard_map/ppermute | solution.py:425
  76.7 0.8 collective-permute-start.24
  77.5 5.4 %collective-permute-start.23 = (bf16[64,1024]{1,0:T(8,128)(2,1)S(1)}, bf16[64,1024]{1,0:T(8,128)(2,1)S(1)}, u32[]{:S(2)}, u32[]{:S(2)}) collective-permute-start(bf16[64,1024]{1,0:T(8,128)(2,1)S(1)} %shard_map.110.refs_1_), channel_id=1, source_target_pairs={{0,24},{2,26},{4,28},{6,30},{8,16},{10,18},{12,20},{14,22},{16,8},... | collective-permute-start | bytes 393224 | tf_op jit(solution)/shard_map/ppermute | solution.py:126
  82.9 0.6 collective-permute-start.16
  83.5 1.1 broadcast_select_fusion.3.refs_5_.refs_4_
  84.6 1.1 broadcast_select_fusion.2.refs_6_.refs_5_
  85.7 10.6 %shard_map.111.refs_6_ = bf16[512,4096]{1,0:T(8,128)(2,1)} custom-call(s32[16]{0:T(128)S(1)} %copy-done.5, bf16[64,1024]{1,0:T(8,128)(2,1)S(1)} %shard_map.110.refs_1_, bf16[512,4096]{1,0:T(8,128)(2,1)} %refs_2_.11, bf16[512,4096]{1,0:T(8,128)(2,1)} %get-tuple-element.59.refs_3_.refs_2_, f32[1024,128]{1,0:T(8,128)} %get-tuple-element.42.refs_4_, ...), custom_call_target="tpu_custom_call" | custom-call | flops 4294967296 | bytes 2097152 | tf_op jit(solution)/shard_map/pallas_call | solution.py:142
  96.4 1.2 %collective-permute-start.26 = (bf16[64,1024]{1,0:T(8,128)(2,1)S(1)}, bf16[64,1024]{1,0:T(8,128)(2,1)S(1)}, u32[]{:S(2)}, u32[]{:S(2)}) collective-permute-start(bf16[64,1024]{1,0:T(8,128)(2,1)S(1)} %collective-permute-done.16), channel_id=1, source_target_pairs={{0,4},{2,6},{4,0},{6,2},{8,12},{10,14},{12,8},{14,10},{16,20},{18,... | collective-permute-start | bytes 393224 | tf_op jit(solution)/shard_map/ppermute | solution.py:126
  97.6 0.9 collective-permute-start.27
  98.5 1.1 collective-permute-start.28
  99.7 0.0 copy-start.1
  99.7 0.1 collective-permute-start.25
  99.8 6.8 %shard_map.112.refs_7_ = bf16[512,4096]{1,0:T(8,128)(2,1)} custom-call(s32[16]{0:T(128)S(1)} %copy-done.5, bf16[512,4096]{1,0:T(8,128)(2,1)} %refs_2_.11, bf16[512,4096]{1,0:T(8,128)(2,1)} %get-tuple-element.59.refs_3_.refs_2_, f32[1024,128]{1,0:T(8,128)} %get-tuple-element.46.refs_1_.refs_3_.refs_4_, ...), custom_call_target="tpu_custom_call", output_to_operand_aliasing={{}: (6, {})} | custom-call | flops 2147483648 | bytes 2097152 | tf_op jit(solution)/shard_map/pallas_call | solution.py:142
  106.7 0.2 collective-permute-start.29
  106.9 1.6 %collective-permute-done.29.refs_3_ = bf16[3,64,1024]{2,1,0:T(8,128)(2,1)S(1)} collective-permute-done((bf16[3,64,1024]{2,1,0:T(8,128)(2,1)S(1)}, bf16[3,64,1024]{2,1,0:T(8,128)(2,1)S(1)}, u32[]{:S(2)}, u32[]{:S(2)}) %collective-permute-start.29) | collective-permute-done | bytes 393248 | tf_op jit(solution)/shard_map/ppermute | solution.py:126
  108.5 1.3 %shard_map.113 = (f32[128,512]{1,0:T(8,128)S(1)}, bf16[128,512]{1,0:T(8,128)(2,1)S(1)}) custom-call(bf16[5,64,1024]{2,1,0:T(8,128)(2,1)S(1)} %bitcast_dynamic-update-slice_fusion.refs_0_, bf16[5,64,1024]{2,1,0:T(8,128)(2,1)S(1)} %collective-permute-done.25.refs_1_, bf16[3,64,1024]{2,1,0:T(8,128)(2,1)S(1)} %pad_maximum_fusion.refs_2_, ...), custom_call_target="tpu_custom_call" | custom-call | flops 1073741824 | bytes 4194304 | tf_op jit(solution)/shard_map/pallas_call | solution.py:142
  109.8 1.6 %collective-permute-start.30 = (bf16[128,512]{1,0:T(8,128)(2,1)S(1)}, bf16[128,512]{1,0:T(8,128)(2,1)S(1)}, u32[]{:S(2)}, u32[]{:S(2)}) collective-permute-start(bf16[128,512]{1,0:T(8,128)(2,1)S(1)} %get-tuple-element.71.refs_1_), channel_id=1, source_target_pairs={{0,1},{1,0},{2,3},{3,2},{4,5},{5,4},{6,7},{7,6},{8,9},{9,8},{10,11... | collective-permute-start | bytes 393224 | tf_op jit(solution)/shard_map/ppermute | solution.py:532
  111.4 6.5 %shard_map.114 = bf16[512,4096]{1,0:T(8,128)(2,1)} custom-call(s32[16]{0:T(128)S(1)} %copy-done.5, bf16[128,512]{1,0:T(8,128)(2,1)S(1)} %get-tuple-element.71.refs_1_, bf16[512,4096]{1,0:T(8,128)(2,1)} %refs_2_.11, bf16[512,4096]{1,0:T(8,128)(2,1)} %get-tuple-element.59.refs_3_.refs_2_, ...), custom_call_target="tpu_custom_call", output_to_operand_aliasing={{}: (7, {})} | custom-call | flops 2147483648 | bytes 2097152 | tf_op jit(solution)/shard_map/pallas_call | solution.py:142
  117.9 0.7 add_convert_fusion
  (40 shorter events, 0.2 us)
Async XLA Ops:
  3.4 1.0 copy-start.2
  4.4 12.1 %copy-start.3 = (bf16[1024,128]{1,0:T(8,128)(2,1)S(1)}, bf16[1024,128]{1,0:T(8,128)(2,1)}, u32[]{:S(2)}) copy-start(bf16[1024,128]{1,0:T(8,128)(2,1)} %get-tuple-element.40.refs_0_) | copy-start | bytes 786436
  5.7 10.8 %collective-permute-start.1 = (bf16[128,5120]{1,0:T(8,128)(2,1)S(1)}, bf16[128,5120]{1,0:T(8,128)(2,1)}, u32[]{:S(2)}, u32[]{:S(2)}) collective-permute-start(bf16[128,5120]{1,0:T(8,128)(2,1)S(1)} %shard_map.105), channel_id=1, source_target_pairs={{0,2},{2,0},{4,6},{6,4},{8,10},{10,8},{12,14},{14,12},{16,18},{18,... | collective-permute-start | bytes 3932168 | tf_op jit(solution)/shard_map/ppermute | solution.py:126
  6.3 19.3 %collective-permute-start = (bf16[512,512]{1,0:T(8,128)(2,1)}, bf16[512,512]{1,0:T(8,128)(2,1)}, u32[]{:S(2)}, u32[]{:S(2)}) collective-permute-start(bf16[512,512]{1,0:T(8,128)(2,1)} %get-tuple-element.41), channel_id=1, source_target_pairs={{0,4},{1,5}} | collective-permute-start | bytes 1572872 | tf_op jit(solution)/shard_map/ppermute | solution.py:425
  11.5 16.5 %collective-permute-start.2 = (bf16[1024,128]{1,0:T(8,128)(2,1)S(1)}, bf16[1024,128]{1,0:T(8,128)(2,1)S(1)}, u32[]{:S(2)}, u32[]{:S(2)}) collective-permute-start(bf16[1024,128]{1,0:T(8,128)(2,1)S(1)} %get-tuple-element.44), channel_id=1, source_target_pairs={{0,8},{2,10},{4,12},{6,14},{8,0},{10,2},{12,4},{14,6},{16,24},{18,... | collective-permute-start | bytes 786440 | tf_op jit(solution)/shard_map/ppermute | solution.py:126
  11.5 31.5 %collective-permute-start.8 = (bf16[1024,128]{1,0:T(8,128)(2,1)S(1)}, bf16[1024,128]{1,0:T(8,128)(2,1)}, u32[]{:S(2)}, u32[]{:S(2)}) collective-permute-start(bf16[1024,128]{1,0:T(8,128)(2,1)S(1)} %get-tuple-element.52), channel_id=1, source_target_pairs={{0,16},{2,18},{4,20},{6,22},{8,24},{10,26},{12,28},{14,30},{16,0},... | collective-permute-start | bytes 786440 | tf_op jit(solution)/shard_map/ppermute | solution.py:126
  12.9 34.0 %collective-permute-start.9 = (bf16[1024,128]{1,0:T(8,128)(2,1)S(1)}, bf16[1024,128]{1,0:T(8,128)(2,1)}, u32[]{:S(2)}, u32[]{:S(2)}) collective-permute-start(bf16[1024,128]{1,0:T(8,128)(2,1)S(1)} %get-tuple-element.54), channel_id=1, source_target_pairs={{0,24},{2,26},{4,28},{6,30},{8,16},{10,18},{12,20},{14,22},{16,8},... | collective-permute-start | bytes 786440 | tf_op jit(solution)/shard_map/ppermute | solution.py:126
  17.8 7.8 %copy-start.6 = (bf16[512,512]{1,0:T(8,128)(2,1)S(1)}, bf16[512,512]{1,0:T(8,128)(2,1)}, u32[]{:S(2)}) copy-start(bf16[512,512]{1,0:T(8,128)(2,1)} %get-tuple-element.38) | copy-start | bytes 1572868
  17.8 20.5 %collective-permute-start.3 = (bf16[64,6144]{1,0:T(8,128)(2,1)S(1)}, bf16[64,6144]{1,0:T(8,128)(2,1)S(1)}, u32[]{:S(2)}, u32[]{:S(2)}) collective-permute-start(bf16[64,6144]{1,0:T(8,128)(2,1)S(1)} %shard_map.106.refs_0_), channel_id=1, source_target_pairs={{0,4},{2,6},{4,0},{6,2},{8,12},{10,14},{12,8},{14,10},{16,20},{18,... | collective-permute-start | bytes 2359304 | tf_op jit(solution)/shard_map/ppermute | solution.py:126
  25.6 15.8 %collective-permute-start.17 = (bf16[512,512]{1,0:T(8,128)(2,1)S(1)}, bf16[512,512]{1,0:T(8,128)(2,1)S(1)}, u32[]{:S(2)}, u32[]{:S(2)}) collective-permute-start(bf16[512,512]{1,0:T(8,128)(2,1)S(1)} %broadcast_select_fusion.4.refs_0_), channel_id=1, source_target_pairs={{0,16},{4,20},{1,17},{5,21}} | collective-permute-start | bytes 1572872 | tf_op jit(solution)/shard_map/ppermute | solution.py:425
  28.0 29.0 %collective-permute-start.10 = (bf16[2048,128]{1,0:T(8,128)(2,1)S(1)}, bf16[2048,128]{1,0:T(8,128)(2,1)S(1)}, u32[]{:S(2)}, u32[]{:S(2)}) collective-permute-start(bf16[2048,128]{1,0:T(8,128)(2,1)S(1)} %constant_dynamic-update-slice_fusion.refs_8_), channel_id=1, source_target_pairs={{0,4},{2,6},{4,0},{6,2},{8,12},{10,14},{12,8},{14,10},{16,20},{18,... | collective-permute-start | bytes 1572872 | tf_op jit(solution)/shard_map/ppermute | solution.py:126
  38.3 1.0 copy-start
  39.4 24.9 %copy-start.5 = (s32[16]{0:T(128)S(1)}, s32[16]{0:T(128)}, u32[]{:S(2)}) copy-start(s32[16]{0:T(128)} %refs_0_.10) | copy-start | bytes 196
  41.5 22.8 %copy-start.4 = (bf16[64,1536]{1,0:T(8,128)(2,1)S(1)}, bf16[64,1536]{1,0:T(8,128)(2,1)}, u32[]{:S(2)}) copy-start(bf16[64,1536]{1,0:T(8,128)(2,1)} %get-tuple-element.47.refs_2_) | copy-start | bytes 589828
  41.5 7.4 %collective-permute-start.4 = (bf16[64,1536]{1,0:T(8,128)(2,1)S(1)}, bf16[64,1536]{1,0:T(8,128)(2,1)S(1)}, u32[]{:S(2)}, u32[]{:S(2)}) collective-permute-start(bf16[64,1536]{1,0:T(8,128)(2,1)S(1)} %get-tuple-element.48), channel_id=1, source_target_pairs={{0,8},{2,10},{4,12},{6,14},{8,0},{10,2},{12,4},{14,6},{16,24},{18,... | collective-permute-start | bytes 589832 | tf_op jit(solution)/shard_map/ppermute | solution.py:126
  41.6 14.5 %collective-permute-start.5 = (bf16[64,1536]{1,0:T(8,128)(2,1)S(1)}, bf16[64,1536]{1,0:T(8,128)(2,1)S(1)}, u32[]{:S(2)}, u32[]{:S(2)}) collective-permute-start(bf16[64,1536]{1,0:T(8,128)(2,1)S(1)} %get-tuple-element.49), channel_id=1, source_target_pairs={{0,16},{2,18},{4,20},{6,22},{8,24},{10,26},{12,28},{14,30},{16,0},... | collective-permute-start | bytes 589832 | tf_op jit(solution)/shard_map/ppermute | solution.py:126
  43.0 13.1 %collective-permute-start.6 = (bf16[64,1536]{1,0:T(8,128)(2,1)S(1)}, bf16[64,1536]{1,0:T(8,128)(2,1)S(1)}, u32[]{:S(2)}, u32[]{:S(2)}) collective-permute-start(bf16[64,1536]{1,0:T(8,128)(2,1)S(1)} %get-tuple-element.50), channel_id=1, source_target_pairs={{0,24},{2,26},{4,28},{6,30},{8,16},{10,18},{12,20},{14,22},{16,8},... | collective-permute-start | bytes 589832 | tf_op jit(solution)/shard_map/ppermute | solution.py:126
  47.9 9.7 %collective-permute-start.11 = (bf16[2048,128]{1,0:T(8,128)(2,1)S(1)}, bf16[2048,128]{1,0:T(8,128)(2,1)S(1)}, u32[]{:S(2)}, u32[]{:S(2)}) collective-permute-start(bf16[2048,128]{1,0:T(8,128)(2,1)S(1)} %constant_dynamic-update-slice_fusion.2.refs_9_), channel_id=1, source_target_pairs={{0,4},{2,6},{4,0},{6,2},{8,12},{10,14},{12,8},{14,10},{16,20},{18,... | collective-permute-start | bytes 1572872 | tf_op jit(solution)/shard_map/ppermute | solution.py:126
  48.9 9.4 %collective-permute-start.18 = (bf16[512,512]{1,0:T(8,128)(2,1)}, bf16[512,512]{1,0:T(8,128)(2,1)}, u32[]{:S(2)}, u32[]{:S(2)}) collective-permute-start(bf16[512,512]{1,0:T(8,128)(2,1)} %broadcast_select_fusion), channel_id=1, source_target_pairs={{0,8},{4,12},{16,24},{20,28},{1,9},{5,13},{17,25},{21,29}} | collective-permute-start | bytes 1572872 | tf_op jit(solution)/shard_map/ppermute | solution.py:425
  57.0 4.8 %collective-permute-start.14 = (bf16[2048,128]{1,0:T(8,128)(2,1)S(1)}, bf16[2048,128]{1,0:T(8,128)(2,1)}, u32[]{:S(2)}, u32[]{:S(2)}) collective-permute-start(bf16[2048,128]{1,0:T(8,128)(2,1)S(1)} %collective-permute-done.10.refs_10_), channel_id=1, source_target_pairs={{0,2},{2,0},{4,6},{6,4},{8,10},{10,8},{12,14},{14,12},{16,18},{18,... | collective-permute-start | bytes 1572872 | tf_op jit(solution)/shard_map/ppermute | solution.py:126
  57.1 7.2 %collective-permute-start.13 = (bf16[2048,128]{1,0:T(8,128)(2,1)S(1)}, bf16[2048,128]{1,0:T(8,128)(2,1)}, u32[]{:S(2)}, u32[]{:S(2)}) collective-permute-start(bf16[2048,128]{1,0:T(8,128)(2,1)S(1)} %constant_dynamic-update-slice_fusion.2.refs_9_), channel_id=1, source_target_pairs={{0,2},{2,0},{4,6},{6,4},{8,10},{10,8},{12,14},{14,12},{16,18},{18,... | collective-permute-start | bytes 1572872 | tf_op jit(solution)/shard_map/ppermute | solution.py:126
  57.6 6.7 %collective-permute-start.12 = (bf16[2048,128]{1,0:T(8,128)(2,1)S(1)}, bf16[2048,128]{1,0:T(8,128)(2,1)}, u32[]{:S(2)}, u32[]{:S(2)}) collective-permute-start(bf16[2048,128]{1,0:T(8,128)(2,1)S(1)} %constant_dynamic-update-slice_fusion.refs_8_), channel_id=1, source_target_pairs={{0,2},{2,0},{4,6},{6,4},{8,10},{10,8},{12,14},{14,12},{16,18},{18,... | collective-permute-start | bytes 1572872 | tf_op jit(solution)/shard_map/ppermute | solution.py:126
  57.6 6.6 %collective-permute-start.15 = (bf16[2048,128]{1,0:T(8,128)(2,1)S(1)}, bf16[2048,128]{1,0:T(8,128)(2,1)}, u32[]{:S(2)}, u32[]{:S(2)}) collective-permute-start(bf16[2048,128]{1,0:T(8,128)(2,1)S(1)} %collective-permute-done.11.refs_11_), channel_id=1, source_target_pairs={{0,2},{2,0},{4,6},{6,4},{8,10},{10,8},{12,14},{14,12},{16,18},{18,... | collective-permute-start | bytes 1572872 | tf_op jit(solution)/shard_map/ppermute | solution.py:126
  58.3 1.9 %collective-permute-start.7 = (bf16[64,512]{1,0:T(8,128)(2,1)S(1)}, bf16[64,512]{1,0:T(8,128)(2,1)S(1)}, u32[]{:S(2)}, u32[]{:S(2)}) collective-permute-start(bf16[64,512]{1,0:T(8,128)(2,1)S(1)} %fusion.1.refs_6_), channel_id=1, source_target_pairs={{0,2},{2,0},{4,6},{6,4},{8,10},{10,8},{12,14},{14,12},{16,18},{18,... | collective-permute-start | bytes 196616 | tf_op jit(solution)/shard_map/ppermute | solution.py:126
  60.2 14.7 %collective-permute-start.20 = (bf16[512,512]{1,0:T(8,128)(2,1)}, bf16[512,512]{1,0:T(8,128)(2,1)}, u32[]{:S(2)}, u32[]{:S(2)}) collective-permute-start(bf16[512,512]{1,0:T(8,128)(2,1)} %broadcast_select_fusion.1), channel_id=1, source_target_pairs={{0,4},{2,6},{4,0},{6,2},{8,12},{10,14},{12,8},{14,10},{16,20},{18,... | collective-permute-start | bytes 1572872 | tf_op jit(solution)/shard_map/ppermute | solution.py:126
  61.8 21.2 %collective-permute-start.19 = (bf16[512,512]{1,0:T(8,128)(2,1)}, bf16[512,512]{1,0:T(8,128)(2,1)}, u32[]{:S(2)}, u32[]{:S(2)}) collective-permute-start(bf16[512,512]{1,0:T(8,128)(2,1)} %broadcast_select_fusion.1), channel_id=1, source_target_pairs={{0,2},{4,6},{8,10},{12,14},{16,18},{20,22},{24,26},{28,30},{1,3},{... | collective-permute-start | bytes 1572872 | tf_op jit(solution)/shard_map/ppermute | solution.py:425
  74.9 9.8 %collective-permute-start.21 = (bf16[512,512]{1,0:T(8,128)(2,1)}, bf16[512,512]{1,0:T(8,128)(2,1)S(1)}, u32[]{:S(2)}, u32[]{:S(2)}) collective-permute-start(bf16[512,512]{1,0:T(8,128)(2,1)} %collective-permute-done.20), channel_id=1, source_target_pairs={{0,2},{4,6},{8,10},{12,14},{16,18},{20,22},{24,26},{28,30},{1,3},{... | collective-permute-start | bytes 1572872 | tf_op jit(solution)/shard_map/ppermute | solution.py:425
  76.7 19.6 %collective-permute-start.24 = (bf16[64,1024]{1,0:T(8,128)(2,1)S(1)}, bf16[64,1024]{1,0:T(8,128)(2,1)S(1)}, u32[]{:S(2)}, u32[]{:S(2)}) collective-permute-start(bf16[64,1024]{1,0:T(8,128)(2,1)S(1)} %shard_map.110.refs_1_), channel_id=1, source_target_pairs={{0,4},{2,6},{4,0},{6,2},{8,12},{10,14},{12,8},{14,10},{16,20},{18,... | collective-permute-start | bytes 393224 | tf_op jit(solution)/shard_map/ppermute | solution.py:126
  77.5 18.8 %collective-permute-start.23 = (bf16[64,1024]{1,0:T(8,128)(2,1)S(1)}, bf16[64,1024]{1,0:T(8,128)(2,1)S(1)}, u32[]{:S(2)}, u32[]{:S(2)}) collective-permute-start(bf16[64,1024]{1,0:T(8,128)(2,1)S(1)} %shard_map.110.refs_1_), channel_id=1, source_target_pairs={{0,24},{2,26},{4,28},{6,30},{8,16},{10,18},{12,20},{14,22},{16,8},... | collective-permute-start | bytes 393224 | tf_op jit(solution)/shard_map/ppermute | solution.py:126
  82.9 13.4 %collective-permute-start.22 = (bf16[64,1024]{1,0:T(8,128)(2,1)S(1)}, bf16[64,1024]{1,0:T(8,128)(2,1)S(1)}, u32[]{:S(2)}, u32[]{:S(2)}) collective-permute-start(bf16[64,1024]{1,0:T(8,128)(2,1)S(1)} %shard_map.110.refs_1_), channel_id=1, source_target_pairs={{0,16},{2,18},{4,20},{6,22},{8,24},{10,26},{12,28},{14,30},{16,0},... | collective-permute-start | bytes 393224 | tf_op jit(solution)/shard_map/ppermute | solution.py:126
  82.9 13.4 %collective-permute-start.16 = (bf16[64,1024]{1,0:T(8,128)(2,1)S(1)}, bf16[64,1024]{1,0:T(8,128)(2,1)S(1)}, u32[]{:S(2)}, u32[]{:S(2)}) collective-permute-start(bf16[64,1024]{1,0:T(8,128)(2,1)S(1)} %shard_map.110.refs_1_), channel_id=1, source_target_pairs={{0,8},{2,10},{4,12},{6,14},{8,0},{10,2},{12,4},{14,6},{16,24},{18,... | collective-permute-start | bytes 393224 | tf_op jit(solution)/shard_map/ppermute | solution.py:126
  96.4 10.2 %collective-permute-start.26 = (bf16[64,1024]{1,0:T(8,128)(2,1)S(1)}, bf16[64,1024]{1,0:T(8,128)(2,1)S(1)}, u32[]{:S(2)}, u32[]{:S(2)}) collective-permute-start(bf16[64,1024]{1,0:T(8,128)(2,1)S(1)} %collective-permute-done.16), channel_id=1, source_target_pairs={{0,4},{2,6},{4,0},{6,2},{8,12},{10,14},{12,8},{14,10},{16,20},{18,... | collective-permute-start | bytes 393224 | tf_op jit(solution)/shard_map/ppermute | solution.py:126
  97.6 9.0 %collective-permute-start.27 = (bf16[64,1024]{1,0:T(8,128)(2,1)S(1)}, bf16[64,1024]{1,0:T(8,128)(2,1)S(1)}, u32[]{:S(2)}, u32[]{:S(2)}) collective-permute-start(bf16[64,1024]{1,0:T(8,128)(2,1)S(1)} %collective-permute-done.22), channel_id=1, source_target_pairs={{0,4},{2,6},{4,0},{6,2},{8,12},{10,14},{12,8},{14,10},{16,20},{18,... | collective-permute-start | bytes 393224 | tf_op jit(solution)/shard_map/ppermute | solution.py:126
  98.5 8.1 %collective-permute-start.28 = (bf16[64,1024]{1,0:T(8,128)(2,1)S(1)}, bf16[64,1024]{1,0:T(8,128)(2,1)S(1)}, u32[]{:S(2)}, u32[]{:S(2)}) collective-permute-start(bf16[64,1024]{1,0:T(8,128)(2,1)S(1)} %collective-permute-done.23), channel_id=1, source_target_pairs={{0,4},{2,6},{4,0},{6,2},{8,12},{10,14},{12,8},{14,10},{16,20},{18,... | collective-permute-start | bytes 393224 | tf_op jit(solution)/shard_map/ppermute | solution.py:126
  99.7 8.8 %copy-start.1 = (bf16[4096,512]{1,0:T(8,128)(2,1)S(1)}, bf16[4096,512]{1,0:T(8,128)(2,1)}, u32[]{:S(2)}) copy-start(bf16[4096,512]{1,0:T(8,128)(2,1)} %refs_4_.7) | copy-start | bytes 12582916
  99.7 8.8 %collective-permute-start.25 = (bf16[5,64,1024]{2,1,0:T(8,128)(2,1)S(1)}, bf16[5,64,1024]{2,1,0:T(8,128)(2,1)S(1)}, u32[]{:S(2)}, u32[]{:S(2)}) collective-permute-start(bf16[5,64,1024]{2,1,0:T(8,128)(2,1)S(1)} %bitcast_dynamic-update-slice_fusion.refs_0_), channel_id=1, source_target_pairs={{0,2},{2,0},{4,6},{6,4},{8,10},{10,8},{12,14},{14,12},{16,18},{18,... | collective-permute-start | bytes 1966088 | tf_op jit(solution)/shard_map/ppermute | solution.py:126
  106.7 1.8 %collective-permute-start.29 = (bf16[3,64,1024]{2,1,0:T(8,128)(2,1)S(1)}, bf16[3,64,1024]{2,1,0:T(8,128)(2,1)S(1)}, u32[]{:S(2)}, u32[]{:S(2)}) collective-permute-start(bf16[3,64,1024]{2,1,0:T(8,128)(2,1)S(1)} %pad_maximum_fusion.refs_2_), channel_id=1, source_target_pairs={{0,2},{2,0},{4,6},{6,4},{8,10},{10,8},{12,14},{14,12},{16,18},{18,... | collective-permute-start | bytes 1179656 | tf_op jit(solution)/shard_map/ppermute | solution.py:126
  109.8 8.1 %collective-permute-start.30 = (bf16[128,512]{1,0:T(8,128)(2,1)S(1)}, bf16[128,512]{1,0:T(8,128)(2,1)S(1)}, u32[]{:S(2)}, u32[]{:S(2)}) collective-permute-start(bf16[128,512]{1,0:T(8,128)(2,1)S(1)} %get-tuple-element.71.refs_1_), channel_id=1, source_target_pairs={{0,1},{1,0},{2,3},{3,2},{4,5},{5,4},{6,7},{7,6},{8,9},{9,8},{10,11... | collective-permute-start | bytes 393224 | tf_op jit(solution)/shard_map/ppermute | solution.py:532

commit v4 on v3

--- a/solution.py
+++ b/solution.py
@@ -392,21 +392,23 @@
         half(1)
 
 
-def anchor_kernel(lengths, q_ref, own_ref, lse_ref, near_ref, far_ref, *rest):
+def anchor_kernel(lengths, q_ref, own_ref, lse_ref, near_ref, far_ref, near_c_ref, far_c_ref, *rest):
     o_ref = rest[-1]
     host = lax.axis_index("hst")
-    _, x, _ = place()
+    _, x, c = place()
+    near_half = jnp.where(c == 0, near_ref[...], near_c_ref[...])
+    far_half = jnp.where(c == 0, far_ref[...], far_c_ref[...])
     anchor_len = jnp.where(host > 0, lengths[0], 0)
     own_len = lengths[host] - pl.program_id(1) * 256
     valid = lax.broadcasted_iota(jnp.int32, (256, 128), 0) < own_len
     column = lax.broadcasted_iota(jnp.int32, (1, 256), 1)
-    values = ones_beside(jnp.concatenate([near_ref[256:512, :], far_ref[256:512, :]], axis=0))
+    values = ones_beside(jnp.concatenate([near_half[256:512, :], far_half[256:512, :]], axis=0))
     near_ok, far_ok = column + x * 256 < anchor_len, column + (1 - x) * 256 < anchor_len
     for h in range(8):
         at = slice(h * 128, (h + 1) * 128)
         q = q_ref[:, at]
-        near = jnp.where(near_ok, dot_t(q, near_ref[0:256, :]), masked_score)
-        far = jnp.where(far_ok, dot_t(q, far_ref[0:256, :]), masked_score)
+        near = jnp.where(near_ok, dot_t(q, near_half[0:256, :]), masked_score)
+        far = jnp.where(far_ok, dot_t(q, far_half[0:256, :]), masked_score)
         lse = jnp.broadcast_to(lse_ref[:, h : h + 1], (256, 128))
         peak = jnp.maximum(row_max([near, far]), lse)
         w = jnp.concatenate([weights(near, peak), weights(far, peak)], axis=1)
@@ -452,21 +454,21 @@
         logs = pl.BlockSpec((256, 128), lambda j, i, _, g=g: ((g % 2 + j) * 2 + i, 0))
         ctx_out = call(
             anchor_kernel, pltpu.HBM((512, 4096), BF16),
-            [block, block, logs, half, half] + ([] if g == 0 else [ANY]),
+            [block, block, logs] + [half] * 4 + ([] if g == 0 else [ANY]),
             block,
             in_hbm(ctx_query, own_out, lse[g // 2]) + halves + ([] if g == 0 else in_hbm(ctx_out)),
-            scalars=[lengths], after=others, grid=(n, 2), aliases={} if g == 0 else {5: 0},
+            scalars=[lengths], after=others, grid=(n, 2), aliases={} if g == 0 else {7: 0},
             flops=n * 4 * 4096 * 512 * 256, data=2**21, vmem=16,
         )
         return ctx_out
 
+    packed = call(
+        ask_pack_kernel, shape((128, 5120), BF16), [ANY] * 3, WHOLE, in_hbm(*ask), scratch=[dma((6,))]
+    )
     kv = call(
         kv_pack_kernel,
         [pltpu.HBM((1024, 128), BF16)] + [shape((1024, 128), BF16)] * 3 + [pltpu.HBM((512, 512), BF16)] * 2,
-        [ANY] * 2, [WHOLE] * 6, in_hbm(ctx_key, context_value), scratch=[dma((12,))],
-    )
-    packed = call(
-        ask_pack_kernel, shape((128, 5120), BF16), [ANY] * 3, WHOLE, in_hbm(*ask), after=[kv[0]], scratch=[dma((6,))]
+        [ANY] * 2, [WHOLE] * 6, in_hbm(ctx_key, context_value), after=[packed], scratch=[dma((12,))],
     )
     got_c = in_hbm(swap(packed, 1))
     kv_z = [kv[0]] + [swap(kv[s], 4 * s) for s in (1, 2, 3)]
@@ -511,8 +513,7 @@
     )
 
     far = after(far, answer)
-    halves = [jnp.where(c == 0, near, after(near_c, answer))]
-    halves.append(jnp.where(c == 0, far, send(far, [(i, i + 1) for i in range(0, 16, 2)])))
+    halves = [near, far, after(near_c, answer), send(far, [(i, i + 1) for i in range(0, 16, 2)])]
 
     across = [swap(answer, 4 * s) for s in (1, 2, 3)]
     side = swap(answer, 2)

time: 119 us -> 116 us (0.975)
  other arithmetic: 6.61 us -> 3.61 us
    select_n x2 -> x0, other arithmetic: 2.22 us -> none  [the longest x1 1.11 us: body(): halves = [jnp.where(c == 0, near, after(near_c, answer))]]
    ppermute x25, starting transfers between devices: 24.5 us -> 26.5 us  [swap(): return lax.ppermute(array, 'hst', [(i, i ^ bit) for i in range(16)])]
    ppermute x5, starting transfers between devices: 15.1 us -> 13.2 us  [send(): return lax.ppermute(array, 'hst', pairs)]
    unnamed x20 -> x16, local copies, waits for them, and re-layouts: 3.04 us -> 3.04 us
  transfers between devices with their start and end apart: 31 -> 31, of which waited for: 5 -> 7; matrix products, arithmetic and copies ran while one was open for 7% -> 5% of each run, Pallas kernels for 43% -> 46%
where the time goes in v4:
time: 116 us; the launch traced here: 115 us
  Pallas kernels  55.9 us (48%)
  starting transfers between devices  41.3 us (36%)
  waiting for transfers between devices  8.5 us (7%)
  local copies, waits for them, and re-layouts  4.07 us (4%)
  other arithmetic  3.61 us (3%)
  between operations  1.63 us (1%)
    pallas_call x11, Pallas kernels, call(): pl.pallas_call(body, grid_spec=pltpu.PrefetchScalarGridSpec(num_scalar_pr...  55.9 us
    ppermute x25, starting transfers between devices, swap(): return lax.ppermute(array, 'hst', [(i, i ^ bit) for i in range(16)])  26.5 us
    ppermute x5, starting transfers between devices, send(): return lax.ppermute(array, 'hst', pairs)  13.2 us
    ppermute x25, waiting for transfers between devices, swap(): return lax.ppermute(array, 'hst', [(i, i ^ bit) for i in range(16)])  8.36 us
    unnamed x16, local copies, waits for them, and re-layouts  3.04 us
  transfers between devices with their start and end apart: 31, of which 7 were waited for; matrix products, arithmetic and copies ran while one was open for 5% of the time, Pallas kernels for 46%

profile of v4, /device:TPU:0, one launch (start us, length us, event | category | flops | bytes accessed | tf_op | source)
XLA Modules:
  0.0 115.1 jit_solution(12463015662156757369)
XLA Ops:
  0.6 1.3 %shard_map.104.refs_0_ = bf16[128,5120]{1,0:T(8,128)(2,1)S(1)} custom-call(bf16[1,256,4096]{2,1,0:T(8,128)(2,1)} %refs_4_.6, bf16[1,256,512]{2,1,0:T(8,128)(2,1)} %refs_5_.1, bf16[1,256,512]{2,1,0:T(8,128)(2,1)} %refs_6_.1), custom_call_target="tpu_custom_call" | custom-call | tf_op jit(solution)/shard_map/pallas_call | solution.py:142
  1.9 0.5 collective-permute-start.1
  2.5 2.8 %shard_map.105 = (bf16[1024,128]{1,0:T(8,128)(2,1)}, bf16[1024,128]{1,0:T(8,128)(2,1)S(1)}, bf16[1024,128]{1,0:T(8,128)(2,1)S(1)}, bf16[1024,128]{1,0:T(8,128)(2...) custom-call(bf16[128,5120]{1,0:T(8,128)(2,1)S(1)} %shard_map.104.refs_0_, bf16[512,512]{1,0:T(8,128)(2,1)} %refs_3_.5, ...), custom_call_target="tpu_custom_call" | custom-call | tf_op jit(solution)/shard_map/pallas_call | solution.py:142
  5.3 5.2 %collective-permute-start = (bf16[512,512]{1,0:T(8,128)(2,1)}, bf16[512,512]{1,0:T(8,128)(2,1)}, u32[]{:S(2)}, u32[]{:S(2)}) collective-permute-start(bf16[512,512]{1,0:T(8,128)(2,1)} %get-tuple-element.40), channel_id=1, source_target_pairs={{0,4},{1,5}} | collective-permute-start | bytes 1572872 | tf_op jit(solution)/shard_map/ppermute | solution.py:427
  10.5 0.0 collective-permute-start.2
  10.5 1.4 %collective-permute-start.8 = (bf16[1024,128]{1,0:T(8,128)(2,1)S(1)}, bf16[1024,128]{1,0:T(8,128)(2,1)}, u32[]{:S(2)}, u32[]{:S(2)}) collective-permute-start(bf16[1024,128]{1,0:T(8,128)(2,1)S(1)} %get-tuple-element.52), channel_id=1, source_target_pairs={{0,16},{2,18},{4,20},{6,22},{8,24},{10,26},{12,28},{14,30},{16,0},... | collective-permute-start | bytes 786440 | tf_op jit(solution)/shard_map/ppermute | solution.py:126
  11.9 3.0 %collective-permute-start.9 = (bf16[1024,128]{1,0:T(8,128)(2,1)S(1)}, bf16[1024,128]{1,0:T(8,128)(2,1)}, u32[]{:S(2)}, u32[]{:S(2)}) collective-permute-start(bf16[1024,128]{1,0:T(8,128)(2,1)S(1)} %get-tuple-element.54), channel_id=1, source_target_pairs={{0,24},{2,26},{4,28},{6,30},{8,16},{10,18},{12,20},{14,22},{16,8},... | collective-permute-start | bytes 786440 | tf_op jit(solution)/shard_map/ppermute | solution.py:126
  15.5 1.0 constant_dynamic-update-slice_fusion.1
  16.5 0.0 collective-permute-done.1.refs_1_.refs_2_
  16.5 1.1 shard_map.106.refs_0_
  17.6 0.0 copy-start.4
  17.7 0.1 collective-permute-start.3
  17.7 7.7 %shard_map.107 = (bf16[512,4096]{1,0:T(8,128)(2,1)}, f32[1024,128]{1,0:T(8,128)}) custom-call(bf16[64,6144]{1,0:T(8,128)(2,1)S(1)} %shard_map.106.refs_0_, bf16[512,4096]{1,0:T(8,128)(2,1)} %refs_2_.13, bf16[512,512]{1,0:T(8,128)(2,1)} %refs_3_.5, bf16[512,512]{1,0:T(8,128)(2,1)} %refs_4_.5), custom_call_target="tpu_custom_call" | custom-call | flops 6442450944 | bytes 4194304 | tf_op jit(solution)/shard_map/pallas_call | solution.py:142
  25.4 0.0 collective-permute-done
  25.4 0.1 broadcast_select_fusion.2.refs_0_
  25.5 2.3 %collective-permute-start.17 = (bf16[512,512]{1,0:T(8,128)(2,1)S(1)}, bf16[512,512]{1,0:T(8,128)(2,1)S(1)}, u32[]{:S(2)}, u32[]{:S(2)}) collective-permute-start(bf16[512,512]{1,0:T(8,128)(2,1)S(1)} %broadcast_select_fusion.2.refs_0_), channel_id=1, source_target_pairs={{0,16},{4,20},{1,17},{5,21}} | collective-permute-start | bytes 1572872 | tf_op jit(solution)/shard_map/ppermute | solution.py:427
  27.8 0.0 collective-permute-done.2.refs_1_
  27.9 2.1 %collective-permute-start.10 = (bf16[2048,128]{1,0:T(8,128)(2,1)S(1)}, bf16[2048,128]{1,0:T(8,128)(2,1)S(1)}, u32[]{:S(2)}, u32[]{:S(2)}) collective-permute-start(bf16[2048,128]{1,0:T(8,128)(2,1)S(1)} %constant_dynamic-update-slice_fusion.refs_8_), channel_id=1, source_target_pairs={{0,4},{2,6},{4,0},{6,2},{8,12},{10,14},{12,8},{14,10},{16,20},{18,... | collective-permute-start | bytes 1572872 | tf_op jit(solution)/shard_map/ppermute | solution.py:126
  30.0 7.6 %shard_map.108 = (bf16[512,4096]{1,0:T(8,128)(2,1)}, f32[1024,128]{1,0:T(8,128)}) custom-call(bf16[512,512]{1,0:T(8,128)(2,1)S(1)} %broadcast_select_fusion.2.refs_0_, bf16[1024,128]{1,0:T(8,128)(2,1)S(1)} %collective-permute-done.2.refs_1_, bf16[512,4096]{1,0:T(8,128)(2,1)} %refs_2_.13, bf16[512,512]{1,0:T(8,128)(2,1)} %refs_3_.5, ...), custom_call_target="tpu_custom_call", output_to_operand_aliasing={{0}: (5, {})} | custom-call | flops 6442450944 | bytes 4194304 | tf_op jit(solution)/shard_map/pallas_call | solution.py:142
  37.6 0.6 collective-permute-done.3.refs_3_
  38.2 1.0 copy-done
  39.2 1.0 shard_map.109
  40.2 0.0 collective-permute-done.17
  40.3 0.1 collective-permute-start.4
  40.3 1.4 %collective-permute-start.5 = (bf16[64,1536]{1,0:T(8,128)(2,1)S(1)}, bf16[64,1536]{1,0:T(8,128)(2,1)S(1)}, u32[]{:S(2)}, u32[]{:S(2)}) collective-permute-start(bf16[64,1536]{1,0:T(8,128)(2,1)S(1)} %get-tuple-element.48), channel_id=1, source_target_pairs={{0,16},{2,18},{4,20},{6,22},{8,24},{10,26},{12,28},{14,30},{16,0},... | collective-permute-start | bytes 589832 | tf_op jit(solution)/shard_map/ppermute | solution.py:126
  41.7 0.0 collective-permute-done.8
  41.7 3.0 %collective-permute-start.6 = (bf16[64,1536]{1,0:T(8,128)(2,1)S(1)}, bf16[64,1536]{1,0:T(8,128)(2,1)S(1)}, u32[]{:S(2)}, u32[]{:S(2)}) collective-permute-start(bf16[64,1536]{1,0:T(8,128)(2,1)S(1)} %get-tuple-element.49), channel_id=1, source_target_pairs={{0,24},{2,26},{4,28},{6,30},{8,16},{10,18},{12,20},{14,22},{16,8},... | collective-permute-start | bytes 589832 | tf_op jit(solution)/shard_map/ppermute | solution.py:126
  44.7 1.0 constant_dynamic-update-slice_fusion.3
  45.7 1.0 constant_dynamic-update-slice_fusion.2.refs_9_
  46.7 1.2 %collective-permute-start.11 = (bf16[2048,128]{1,0:T(8,128)(2,1)S(1)}, bf16[2048,128]{1,0:T(8,128)(2,1)S(1)}, u32[]{:S(2)}, u32[]{:S(2)}) collective-permute-start(bf16[2048,128]{1,0:T(8,128)(2,1)S(1)} %constant_dynamic-update-slice_fusion.2.refs_9_), channel_id=1, source_target_pairs={{0,4},{2,6},{4,0},{6,2},{8,12},{10,14},{12,8},{14,10},{16,20},{18,... | collective-permute-start | bytes 1572872 | tf_op jit(solution)/shard_map/ppermute | solution.py:126
  47.9 0.8 broadcast_select_fusion
  48.7 2.2 %collective-permute-start.18 = (bf16[512,512]{1,0:T(8,128)(2,1)}, bf16[512,512]{1,0:T(8,128)(2,1)}, u32[]{:S(2)}, u32[]{:S(2)}) collective-permute-start(bf16[512,512]{1,0:T(8,128)(2,1)} %broadcast_select_fusion), channel_id=1, source_target_pairs={{0,8},{4,12},{16,24},{20,28},{1,9},{5,13},{17,25},{21,29}} | collective-permute-start | bytes 1572872 | tf_op jit(solution)/shard_map/ppermute | solution.py:427
  50.9 4.1 %collective-permute-done.5.refs_4_ = bf16[64,1536]{1,0:T(8,128)(2,1)S(1)} collective-permute-done((bf16[64,1536]{1,0:T(8,128)(2,1)S(1)}, bf16[64,1536]{1,0:T(8,128)(2,1)S(1)}, u32[]{:S(2)}, u32[]{:S(2)}) %collective-permute-start.5) | collective-permute-done | bytes 196640 | tf_op jit(solution)/shard_map/ppermute | solution.py:126
  55.0 0.9 fusion.1.refs_6_
  55.8 0.1 collective-permute-start.14
  55.9 0.5 collective-permute-start.13
  56.4 0.1 collective-permute-start.12
  56.5 0.2 collective-permute-done.11.refs_11_
  56.7 0.3 collective-permute-start.15
  56.9 0.1 collective-permute-done.18
  57.1 0.1 collective-permute-start.7
  57.2 1.1 broadcast_select_fusion.1.refs_5_.refs_4_
  58.3 0.5 collective-permute-done.7.refs_7_
  58.8 2.2 %collective-permute-start.19 = (bf16[512,512]{1,0:T(8,128)(2,1)S(1)}, bf16[512,512]{1,0:T(8,128)(2,1)S(1)}, u32[]{:S(2)}, u32[]{:S(2)}) collective-permute-start(bf16[512,512]{1,0:T(8,128)(2,1)S(1)} %broadcast_select_fusion.1.refs_5_.refs_4_), channel_id=1, source_target_pairs={{0,4},{2,6},{4,0},{6,2},{8,12},{10,14},{12,8},{14,10},{16,20},{18,... | collective-permute-start | bytes 1572872 | tf_op jit(solution)/shard_map/ppermute | solution.py:126
  60.9 1.8 %collective-permute-start.20 = (bf16[512,512]{1,0:T(8,128)(2,1)S(1)}, bf16[512,512]{1,0:T(8,128)(2,1)S(1)}, u32[]{:S(2)}, u32[]{:S(2)}) collective-permute-start(bf16[512,512]{1,0:T(8,128)(2,1)S(1)} %broadcast_select_fusion.1.refs_5_.refs_4_), channel_id=1, source_target_pairs={{0,2},{4,6},{8,10},{12,14},{16,18},{20,22},{24,26},{28,30},{1,3},{... | collective-permute-start | bytes 1572872 | tf_op jit(solution)/shard_map/ppermute | solution.py:427
  62.8 8.9 %shard_map.110.refs_1_ = bf16[64,1024]{1,0:T(8,128)(2,1)S(1)} custom-call(s32[1]{0:T(128)} %copy.23.refs_0_, s32[16]{0:T(128)S(1)} %copy-done.3, bf16[64,1536]{1,0:T(8,128)(2,1)S(1)} %copy-done.2, bf16[64,1536]{1,0:T(8,128)(2,1)S(1)} %collective-permute-done.4.refs_3_, bf16[64,1536]{1,0:T(8,128)(2,1)S(1)} %collective-permute-done.5.refs_4_, ...), custom_call_target="tpu_custom_call" | custom-call | flops 4294967296 | bytes 4194304 | tf_op jit(solution)/shard_map/pallas_call | solution.py:142
  71.7 1.4 %collective-permute-done.19.refs_6_.refs_5_ = bf16[512,512]{1,0:T(8,128)(2,1)S(1)} collective-permute-done((bf16[512,512]{1,0:T(8,128)(2,1)S(1)}, bf16[512,512]{1,0:T(8,128)(2,1)S(1)}, u32[]{:S(2)}, u32[]{:S(2)}) %collective-permute-start.19) | collective-permute-done | bytes 524320 | tf_op jit(solution)/shard_map/ppermute | solution.py:126
  73.1 1.7 %collective-permute-start.21 = (bf16[512,512]{1,0:T(8,128)(2,1)S(1)}, bf16[512,512]{1,0:T(8,128)(2,1)S(1)}, u32[]{:S(2)}, u32[]{:S(2)}) collective-permute-start(bf16[512,512]{1,0:T(8,128)(2,1)S(1)} %collective-permute-done.19.refs_6_.refs_5_), channel_id=1, source_target_pairs={{0,2},{4,6},{8,10},{12,14},{16,18},{20,22},{24,26},{28,30},{1,3},{... | collective-permute-start | bytes 1572872 | tf_op jit(solution)/shard_map/ppermute | solution.py:427
  74.9 1.6 %collective-permute-start.24 = (bf16[64,1024]{1,0:T(8,128)(2,1)S(1)}, bf16[64,1024]{1,0:T(8,128)(2,1)S(1)}, u32[]{:S(2)}, u32[]{:S(2)}) collective-permute-start(bf16[64,1024]{1,0:T(8,128)(2,1)S(1)} %shard_map.110.refs_1_), channel_id=1, source_target_pairs={{0,4},{2,6},{4,0},{6,2},{8,12},{10,14},{12,8},{14,10},{16,20},{18,... | collective-permute-start | bytes 393224 | tf_op jit(solution)/shard_map/ppermute | solution.py:126
  76.5 5.6 %collective-permute-start.23 = (bf16[64,1024]{1,0:T(8,128)(2,1)S(1)}, bf16[64,1024]{1,0:T(8,128)(2,1)S(1)}, u32[]{:S(2)}, u32[]{:S(2)}) collective-permute-start(bf16[64,1024]{1,0:T(8,128)(2,1)S(1)} %shard_map.110.refs_1_), channel_id=1, source_target_pairs={{0,24},{2,26},{4,28},{6,30},{8,16},{10,18},{12,20},{14,22},{16,8},... | collective-permute-start | bytes 393224 | tf_op jit(solution)/shard_map/ppermute | solution.py:126
  82.1 0.6 collective-permute-start.16
  82.7 10.7 %shard_map.111.refs_8_ = bf16[512,4096]{1,0:T(8,128)(2,1)} custom-call(s32[16]{0:T(128)S(1)} %copy-done.3, bf16[64,1024]{1,0:T(8,128)(2,1)S(1)} %shard_map.110.refs_1_, bf16[512,4096]{1,0:T(8,128)(2,1)} %refs_2_.13, bf16[512,4096]{1,0:T(8,128)(2,1)} %get-tuple-element.59.refs_3_.refs_2_, f32[1024,128]{1,0:T(8,128)} %get-tuple-element.41.refs_4_, ...), custom_call_target="tpu_custom_call" | custom-call | flops 4294967296 | bytes 2097152 | tf_op jit(solution)/shard_map/pallas_call | solution.py:142
  93.4 0.5 collective-permute-start.26
  94.0 1.6 %collective-permute-start.27 = (bf16[64,1024]{1,0:T(8,128)(2,1)S(1)}, bf16[64,1024]{1,0:T(8,128)(2,1)S(1)}, u32[]{:S(2)}, u32[]{:S(2)}) collective-permute-start(bf16[64,1024]{1,0:T(8,128)(2,1)S(1)} %collective-permute-done.22), channel_id=1, source_target_pairs={{0,4},{2,6},{4,0},{6,2},{8,12},{10,14},{12,8},{14,10},{16,20},{18,... | collective-permute-start | bytes 393224 | tf_op jit(solution)/shard_map/ppermute | solution.py:126
  95.5 0.5 collective-permute-start.28
  96.1 0.0 copy-start.1
  96.1 0.1 collective-permute-start.25
  96.1 6.9 %shard_map.112.refs_9_ = bf16[512,4096]{1,0:T(8,128)(2,1)} custom-call(s32[16]{0:T(128)S(1)} %copy-done.3, bf16[512,4096]{1,0:T(8,128)(2,1)} %refs_2_.13, bf16[512,4096]{1,0:T(8,128)(2,1)} %get-tuple-element.59.refs_3_.refs_2_, f32[1024,128]{1,0:T(8,128)} %get-tuple-element.45.refs_1_.refs_3_.refs_4_, ...), custom_call_target="tpu_custom_call", output_to_operand_aliasing={{}: (8, {})} | custom-call | flops 2147483648 | bytes 2097152 | tf_op jit(solution)/shard_map/pallas_call | solution.py:142
  103.1 0.2 collective-permute-start.29
  103.3 1.6 %collective-permute-done.29.refs_3_ = bf16[3,64,1024]{2,1,0:T(8,128)(2,1)S(1)} collective-permute-done((bf16[3,64,1024]{2,1,0:T(8,128)(2,1)S(1)}, bf16[3,64,1024]{2,1,0:T(8,128)(2,1)S(1)}, u32[]{:S(2)}, u32[]{:S(2)}) %collective-permute-start.29) | collective-permute-done | bytes 393248 | tf_op jit(solution)/shard_map/ppermute | solution.py:126
  104.9 1.3 %shard_map.113 = (f32[128,512]{1,0:T(8,128)S(1)}, bf16[128,512]{1,0:T(8,128)(2,1)S(1)}) custom-call(bf16[5,64,1024]{2,1,0:T(8,128)(2,1)S(1)} %bitcast_dynamic-update-slice_fusion.refs_0_, bf16[5,64,1024]{2,1,0:T(8,128)(2,1)S(1)} %collective-permute-done.25.refs_1_, bf16[3,64,1024]{2,1,0:T(8,128)(2,1)S(1)} %pad_maximum_fusion.refs_2_, ...), custom_call_target="tpu_custom_call" | custom-call | flops 1073741824 | bytes 4194304 | tf_op jit(solution)/shard_map/pallas_call | solution.py:142
  106.2 1.6 %collective-permute-start.30 = (bf16[128,512]{1,0:T(8,128)(2,1)S(1)}, bf16[128,512]{1,0:T(8,128)(2,1)S(1)}, u32[]{:S(2)}, u32[]{:S(2)}) collective-permute-start(bf16[128,512]{1,0:T(8,128)(2,1)S(1)} %get-tuple-element.71.refs_1_), channel_id=1, source_target_pairs={{0,1},{1,0},{2,3},{3,2},{4,5},{5,4},{6,7},{7,6},{8,9},{9,8},{10,11... | collective-permute-start | bytes 393224 | tf_op jit(solution)/shard_map/ppermute | solution.py:533
  107.8 6.6 %shard_map.114 = bf16[512,4096]{1,0:T(8,128)(2,1)} custom-call(s32[16]{0:T(128)S(1)} %copy-done.3, bf16[128,512]{1,0:T(8,128)(2,1)S(1)} %get-tuple-element.71.refs_1_, bf16[512,4096]{1,0:T(8,128)(2,1)} %refs_2_.13, bf16[512,4096]{1,0:T(8,128)(2,1)} %get-tuple-element.59.refs_3_.refs_2_, ...), custom_call_target="tpu_custom_call", output_to_operand_aliasing={{}: (9, {})} | custom-call | flops 2147483648 | bytes 2097152 | tf_op jit(solution)/shard_map/pallas_call | solution.py:142
  114.4 0.7 add_convert_fusion
  (34 shorter events, 0.2 us)
Async XLA Ops:
  1.9 14.6 %collective-permute-start.1 = (bf16[128,5120]{1,0:T(8,128)(2,1)S(1)}, bf16[128,5120]{1,0:T(8,128)(2,1)}, u32[]{:S(2)}, u32[]{:S(2)}) collective-permute-start(bf16[128,5120]{1,0:T(8,128)(2,1)S(1)} %shard_map.104.refs_0_), channel_id=1, source_target_pairs={{0,2},{2,0},{4,6},{6,4},{8,10},{10,8},{12,14},{14,12},{16,18},{18,... | collective-permute-start | bytes 3932168 | tf_op jit(solution)/shard_map/ppermute | solution.py:126
  5.3 20.2 %collective-permute-start = (bf16[512,512]{1,0:T(8,128)(2,1)}, bf16[512,512]{1,0:T(8,128)(2,1)}, u32[]{:S(2)}, u32[]{:S(2)}) collective-permute-start(bf16[512,512]{1,0:T(8,128)(2,1)} %get-tuple-element.40), channel_id=1, source_target_pairs={{0,4},{1,5}} | collective-permute-start | bytes 1572872 | tf_op jit(solution)/shard_map/ppermute | solution.py:427
  10.5 17.4 %collective-permute-start.2 = (bf16[1024,128]{1,0:T(8,128)(2,1)S(1)}, bf16[1024,128]{1,0:T(8,128)(2,1)S(1)}, u32[]{:S(2)}, u32[]{:S(2)}) collective-permute-start(bf16[1024,128]{1,0:T(8,128)(2,1)S(1)} %get-tuple-element.43), channel_id=1, source_target_pairs={{0,8},{2,10},{4,12},{6,14},{8,0},{10,2},{12,4},{14,6},{16,24},{18,... | collective-permute-start | bytes 786440 | tf_op jit(solution)/shard_map/ppermute | solution.py:126
  10.5 31.2 %collective-permute-start.8 = (bf16[1024,128]{1,0:T(8,128)(2,1)S(1)}, bf16[1024,128]{1,0:T(8,128)(2,1)}, u32[]{:S(2)}, u32[]{:S(2)}) collective-permute-start(bf16[1024,128]{1,0:T(8,128)(2,1)S(1)} %get-tuple-element.52), channel_id=1, source_target_pairs={{0,16},{2,18},{4,20},{6,22},{8,24},{10,26},{12,28},{14,30},{16,0},... | collective-permute-start | bytes 786440 | tf_op jit(solution)/shard_map/ppermute | solution.py:126
  11.9 33.8 %collective-permute-start.9 = (bf16[1024,128]{1,0:T(8,128)(2,1)S(1)}, bf16[1024,128]{1,0:T(8,128)(2,1)}, u32[]{:S(2)}, u32[]{:S(2)}) collective-permute-start(bf16[1024,128]{1,0:T(8,128)(2,1)S(1)} %get-tuple-element.54), channel_id=1, source_target_pairs={{0,24},{2,26},{4,28},{6,30},{8,16},{10,18},{12,20},{14,22},{16,8},... | collective-permute-start | bytes 786440 | tf_op jit(solution)/shard_map/ppermute | solution.py:126
  17.6 7.8 %copy-start.4 = (bf16[512,512]{1,0:T(8,128)(2,1)S(1)}, bf16[512,512]{1,0:T(8,128)(2,1)}, u32[]{:S(2)}) copy-start(bf16[512,512]{1,0:T(8,128)(2,1)} %get-tuple-element.38) | copy-start | bytes 1572868
  17.7 20.5 %collective-permute-start.3 = (bf16[64,6144]{1,0:T(8,128)(2,1)S(1)}, bf16[64,6144]{1,0:T(8,128)(2,1)S(1)}, u32[]{:S(2)}, u32[]{:S(2)}) collective-permute-start(bf16[64,6144]{1,0:T(8,128)(2,1)S(1)} %shard_map.106.refs_0_), channel_id=1, source_target_pairs={{0,4},{2,6},{4,0},{6,2},{8,12},{10,14},{12,8},{14,10},{16,20},{18,... | collective-permute-start | bytes 2359304 | tf_op jit(solution)/shard_map/ppermute | solution.py:126
  25.5 14.7 %collective-permute-start.17 = (bf16[512,512]{1,0:T(8,128)(2,1)S(1)}, bf16[512,512]{1,0:T(8,128)(2,1)S(1)}, u32[]{:S(2)}, u32[]{:S(2)}) collective-permute-start(bf16[512,512]{1,0:T(8,128)(2,1)S(1)} %broadcast_select_fusion.2.refs_0_), channel_id=1, source_target_pairs={{0,16},{4,20},{1,17},{5,21}} | collective-permute-start | bytes 1572872 | tf_op jit(solution)/shard_map/ppermute | solution.py:427
  27.9 28.0 %collective-permute-start.10 = (bf16[2048,128]{1,0:T(8,128)(2,1)S(1)}, bf16[2048,128]{1,0:T(8,128)(2,1)S(1)}, u32[]{:S(2)}, u32[]{:S(2)}) collective-permute-start(bf16[2048,128]{1,0:T(8,128)(2,1)S(1)} %constant_dynamic-update-slice_fusion.refs_8_), channel_id=1, source_target_pairs={{0,4},{2,6},{4,0},{6,2},{8,12},{10,14},{12,8},{14,10},{16,20},{18,... | collective-permute-start | bytes 1572872 | tf_op jit(solution)/shard_map/ppermute | solution.py:126
  38.2 1.0 copy-start
  39.2 23.5 %copy-start.3 = (s32[16]{0:T(128)S(1)}, s32[16]{0:T(128)}, u32[]{:S(2)}) copy-start(s32[16]{0:T(128)} %refs_0_.10) | copy-start | bytes 196
  40.2 22.5 %copy-start.2 = (bf16[64,1536]{1,0:T(8,128)(2,1)S(1)}, bf16[64,1536]{1,0:T(8,128)(2,1)}, u32[]{:S(2)}) copy-start(bf16[64,1536]{1,0:T(8,128)(2,1)} %get-tuple-element.46.refs_2_) | copy-start | bytes 589828
  40.3 8.5 %collective-permute-start.4 = (bf16[64,1536]{1,0:T(8,128)(2,1)S(1)}, bf16[64,1536]{1,0:T(8,128)(2,1)S(1)}, u32[]{:S(2)}, u32[]{:S(2)}) collective-permute-start(bf16[64,1536]{1,0:T(8,128)(2,1)S(1)} %get-tuple-element.47), channel_id=1, source_target_pairs={{0,8},{2,10},{4,12},{6,14},{8,0},{10,2},{12,4},{14,6},{16,24},{18,... | collective-permute-start | bytes 589832 | tf_op jit(solution)/shard_map/ppermute | solution.py:126
  40.3 14.6 %collective-permute-start.5 = (bf16[64,1536]{1,0:T(8,128)(2,1)S(1)}, bf16[64,1536]{1,0:T(8,128)(2,1)S(1)}, u32[]{:S(2)}, u32[]{:S(2)}) collective-permute-start(bf16[64,1536]{1,0:T(8,128)(2,1)S(1)} %get-tuple-element.48), channel_id=1, source_target_pairs={{0,16},{2,18},{4,20},{6,22},{8,24},{10,26},{12,28},{14,30},{16,0},... | collective-permute-start | bytes 589832 | tf_op jit(solution)/shard_map/ppermute | solution.py:126
  41.7 13.2 %collective-permute-start.6 = (bf16[64,1536]{1,0:T(8,128)(2,1)S(1)}, bf16[64,1536]{1,0:T(8,128)(2,1)S(1)}, u32[]{:S(2)}, u32[]{:S(2)}) collective-permute-start(bf16[64,1536]{1,0:T(8,128)(2,1)S(1)} %get-tuple-element.49), channel_id=1, source_target_pairs={{0,24},{2,26},{4,28},{6,30},{8,16},{10,18},{12,20},{14,22},{16,8},... | collective-permute-start | bytes 589832 | tf_op jit(solution)/shard_map/ppermute | solution.py:126
  46.7 10.0 %collective-permute-start.11 = (bf16[2048,128]{1,0:T(8,128)(2,1)S(1)}, bf16[2048,128]{1,0:T(8,128)(2,1)S(1)}, u32[]{:S(2)}, u32[]{:S(2)}) collective-permute-start(bf16[2048,128]{1,0:T(8,128)(2,1)S(1)} %constant_dynamic-update-slice_fusion.2.refs_9_), channel_id=1, source_target_pairs={{0,4},{2,6},{4,0},{6,2},{8,12},{10,14},{12,8},{14,10},{16,20},{18,... | collective-permute-start | bytes 1572872 | tf_op jit(solution)/shard_map/ppermute | solution.py:126
  48.7 8.3 %collective-permute-start.18 = (bf16[512,512]{1,0:T(8,128)(2,1)}, bf16[512,512]{1,0:T(8,128)(2,1)}, u32[]{:S(2)}, u32[]{:S(2)}) collective-permute-start(bf16[512,512]{1,0:T(8,128)(2,1)} %broadcast_select_fusion), channel_id=1, source_target_pairs={{0,8},{4,12},{16,24},{20,28},{1,9},{5,13},{17,25},{21,29}} | collective-permute-start | bytes 1572872 | tf_op jit(solution)/shard_map/ppermute | solution.py:427
  55.8 5.1 %collective-permute-start.14 = (bf16[2048,128]{1,0:T(8,128)(2,1)S(1)}, bf16[2048,128]{1,0:T(8,128)(2,1)}, u32[]{:S(2)}, u32[]{:S(2)}) collective-permute-start(bf16[2048,128]{1,0:T(8,128)(2,1)S(1)} %collective-permute-done.10.refs_10_), channel_id=1, source_target_pairs={{0,2},{2,0},{4,6},{6,4},{8,10},{10,8},{12,14},{14,12},{16,18},{18,... | collective-permute-start | bytes 1572872 | tf_op jit(solution)/shard_map/ppermute | solution.py:126
  55.9 6.8 %collective-permute-start.13 = (bf16[2048,128]{1,0:T(8,128)(2,1)S(1)}, bf16[2048,128]{1,0:T(8,128)(2,1)}, u32[]{:S(2)}, u32[]{:S(2)}) collective-permute-start(bf16[2048,128]{1,0:T(8,128)(2,1)S(1)} %constant_dynamic-update-slice_fusion.2.refs_9_), channel_id=1, source_target_pairs={{0,2},{2,0},{4,6},{6,4},{8,10},{10,8},{12,14},{14,12},{16,18},{18,... | collective-permute-start | bytes 1572872 | tf_op jit(solution)/shard_map/ppermute | solution.py:126
  56.4 6.3 %collective-permute-start.12 = (bf16[2048,128]{1,0:T(8,128)(2,1)S(1)}, bf16[2048,128]{1,0:T(8,128)(2,1)}, u32[]{:S(2)}, u32[]{:S(2)}) collective-permute-start(bf16[2048,128]{1,0:T(8,128)(2,1)S(1)} %constant_dynamic-update-slice_fusion.refs_8_), channel_id=1, source_target_pairs={{0,2},{2,0},{4,6},{6,4},{8,10},{10,8},{12,14},{14,12},{16,18},{18,... | collective-permute-start | bytes 1572872 | tf_op jit(solution)/shard_map/ppermute | solution.py:126
  56.7 6.1 %collective-permute-start.15 = (bf16[2048,128]{1,0:T(8,128)(2,1)S(1)}, bf16[2048,128]{1,0:T(8,128)(2,1)}, u32[]{:S(2)}, u32[]{:S(2)}) collective-permute-start(bf16[2048,128]{1,0:T(8,128)(2,1)S(1)} %collective-permute-done.11.refs_11_), channel_id=1, source_target_pairs={{0,2},{2,0},{4,6},{6,4},{8,10},{10,8},{12,14},{14,12},{16,18},{18,... | collective-permute-start | bytes 1572872 | tf_op jit(solution)/shard_map/ppermute | solution.py:126
  57.1 1.7 %collective-permute-start.7 = (bf16[64,512]{1,0:T(8,128)(2,1)S(1)}, bf16[64,512]{1,0:T(8,128)(2,1)S(1)}, u32[]{:S(2)}, u32[]{:S(2)}) collective-permute-start(bf16[64,512]{1,0:T(8,128)(2,1)S(1)} %fusion.1.refs_6_), channel_id=1, source_target_pairs={{0,2},{2,0},{4,6},{6,4},{8,10},{10,8},{12,14},{14,12},{16,18},{18,... | collective-permute-start | bytes 196616 | tf_op jit(solution)/shard_map/ppermute | solution.py:126
  58.8 14.4 %collective-permute-start.19 = (bf16[512,512]{1,0:T(8,128)(2,1)S(1)}, bf16[512,512]{1,0:T(8,128)(2,1)S(1)}, u32[]{:S(2)}, u32[]{:S(2)}) collective-permute-start(bf16[512,512]{1,0:T(8,128)(2,1)S(1)} %broadcast_select_fusion.1.refs_5_.refs_4_), channel_id=1, source_target_pairs={{0,4},{2,6},{4,0},{6,2},{8,12},{10,14},{12,8},{14,10},{16,20},{18,... | collective-permute-start | bytes 1572872 | tf_op jit(solution)/shard_map/ppermute | solution.py:126
  60.9 21.2 %collective-permute-start.20 = (bf16[512,512]{1,0:T(8,128)(2,1)S(1)}, bf16[512,512]{1,0:T(8,128)(2,1)S(1)}, u32[]{:S(2)}, u32[]{:S(2)}) collective-permute-start(bf16[512,512]{1,0:T(8,128)(2,1)S(1)} %broadcast_select_fusion.1.refs_5_.refs_4_), channel_id=1, source_target_pairs={{0,2},{4,6},{8,10},{12,14},{16,18},{20,22},{24,26},{28,30},{1,3},{... | collective-permute-start | bytes 1572872 | tf_op jit(solution)/shard_map/ppermute | solution.py:427
  73.1 9.5 %collective-permute-start.21 = (bf16[512,512]{1,0:T(8,128)(2,1)S(1)}, bf16[512,512]{1,0:T(8,128)(2,1)S(1)}, u32[]{:S(2)}, u32[]{:S(2)}) collective-permute-start(bf16[512,512]{1,0:T(8,128)(2,1)S(1)} %collective-permute-done.19.refs_6_.refs_5_), channel_id=1, source_target_pairs={{0,2},{4,6},{8,10},{12,14},{16,18},{20,22},{24,26},{28,30},{1,3},{... | collective-permute-start | bytes 1572872 | tf_op jit(solution)/shard_map/ppermute | solution.py:427
  74.9 18.5 %collective-permute-start.24 = (bf16[64,1024]{1,0:T(8,128)(2,1)S(1)}, bf16[64,1024]{1,0:T(8,128)(2,1)S(1)}, u32[]{:S(2)}, u32[]{:S(2)}) collective-permute-start(bf16[64,1024]{1,0:T(8,128)(2,1)S(1)} %shard_map.110.refs_1_), channel_id=1, source_target_pairs={{0,4},{2,6},{4,0},{6,2},{8,12},{10,14},{12,8},{14,10},{16,20},{18,... | collective-permute-start | bytes 393224 | tf_op jit(solution)/shard_map/ppermute | solution.py:126
  76.5 16.9 %collective-permute-start.23 = (bf16[64,1024]{1,0:T(8,128)(2,1)S(1)}, bf16[64,1024]{1,0:T(8,128)(2,1)S(1)}, u32[]{:S(2)}, u32[]{:S(2)}) collective-permute-start(bf16[64,1024]{1,0:T(8,128)(2,1)S(1)} %shard_map.110.refs_1_), channel_id=1, source_target_pairs={{0,24},{2,26},{4,28},{6,30},{8,16},{10,18},{12,20},{14,22},{16,8},... | collective-permute-start | bytes 393224 | tf_op jit(solution)/shard_map/ppermute | solution.py:126
  82.1 11.3 %collective-permute-start.22 = (bf16[64,1024]{1,0:T(8,128)(2,1)S(1)}, bf16[64,1024]{1,0:T(8,128)(2,1)S(1)}, u32[]{:S(2)}, u32[]{:S(2)}) collective-permute-start(bf16[64,1024]{1,0:T(8,128)(2,1)S(1)} %shard_map.110.refs_1_), channel_id=1, source_target_pairs={{0,16},{2,18},{4,20},{6,22},{8,24},{10,26},{12,28},{14,30},{16,0},... | collective-permute-start | bytes 393224 | tf_op jit(solution)/shard_map/ppermute | solution.py:126
  82.1 11.3 %collective-permute-start.16 = (bf16[64,1024]{1,0:T(8,128)(2,1)S(1)}, bf16[64,1024]{1,0:T(8,128)(2,1)S(1)}, u32[]{:S(2)}, u32[]{:S(2)}) collective-permute-start(bf16[64,1024]{1,0:T(8,128)(2,1)S(1)} %shard_map.110.refs_1_), channel_id=1, source_target_pairs={{0,8},{2,10},{4,12},{6,14},{8,0},{10,2},{12,4},{14,6},{16,24},{18,... | collective-permute-start | bytes 393224 | tf_op jit(solution)/shard_map/ppermute | solution.py:126
  93.4 9.6 %collective-permute-start.26 = (bf16[64,1024]{1,0:T(8,128)(2,1)S(1)}, bf16[64,1024]{1,0:T(8,128)(2,1)S(1)}, u32[]{:S(2)}, u32[]{:S(2)}) collective-permute-start(bf16[64,1024]{1,0:T(8,128)(2,1)S(1)} %collective-permute-done.16), channel_id=1, source_target_pairs={{0,4},{2,6},{4,0},{6,2},{8,12},{10,14},{12,8},{14,10},{16,20},{18,... | collective-permute-start | bytes 393224 | tf_op jit(solution)/shard_map/ppermute | solution.py:126
  94.0 9.1 %collective-permute-start.27 = (bf16[64,1024]{1,0:T(8,128)(2,1)S(1)}, bf16[64,1024]{1,0:T(8,128)(2,1)S(1)}, u32[]{:S(2)}, u32[]{:S(2)}) collective-permute-start(bf16[64,1024]{1,0:T(8,128)(2,1)S(1)} %collective-permute-done.22), channel_id=1, source_target_pairs={{0,4},{2,6},{4,0},{6,2},{8,12},{10,14},{12,8},{14,10},{16,20},{18,... | collective-permute-start | bytes 393224 | tf_op jit(solution)/shard_map/ppermute | solution.py:126
  95.5 7.5 %collective-permute-start.28 = (bf16[64,1024]{1,0:T(8,128)(2,1)S(1)}, bf16[64,1024]{1,0:T(8,128)(2,1)S(1)}, u32[]{:S(2)}, u32[]{:S(2)}) collective-permute-start(bf16[64,1024]{1,0:T(8,128)(2,1)S(1)} %collective-permute-done.23), channel_id=1, source_target_pairs={{0,4},{2,6},{4,0},{6,2},{8,12},{10,14},{12,8},{14,10},{16,20},{18,... | collective-permute-start | bytes 393224 | tf_op jit(solution)/shard_map/ppermute | solution.py:126
  96.1 8.8 %copy-start.1 = (bf16[4096,512]{1,0:T(8,128)(2,1)S(1)}, bf16[4096,512]{1,0:T(8,128)(2,1)}, u32[]{:S(2)}) copy-start(bf16[4096,512]{1,0:T(8,128)(2,1)} %refs_4_.7) | copy-start | bytes 12582916
  96.1 8.8 %collective-permute-start.25 = (bf16[5,64,1024]{2,1,0:T(8,128)(2,1)S(1)}, bf16[5,64,1024]{2,1,0:T(8,128)(2,1)S(1)}, u32[]{:S(2)}, u32[]{:S(2)}) collective-permute-start(bf16[5,64,1024]{2,1,0:T(8,128)(2,1)S(1)} %bitcast_dynamic-update-slice_fusion.refs_0_), channel_id=1, source_target_pairs={{0,2},{2,0},{4,6},{6,4},{8,10},{10,8},{12,14},{14,12},{16,18},{18,... | collective-permute-start | bytes 1966088 | tf_op jit(solution)/shard_map/ppermute | solution.py:126
  103.1 1.8 %collective-permute-start.29 = (bf16[3,64,1024]{2,1,0:T(8,128)(2,1)S(1)}, bf16[3,64,1024]{2,1,0:T(8,128)(2,1)S(1)}, u32[]{:S(2)}, u32[]{:S(2)}) collective-permute-start(bf16[3,64,1024]{2,1,0:T(8,128)(2,1)S(1)} %pad_maximum_fusion.refs_2_), channel_id=1, source_target_pairs={{0,2},{2,0},{4,6},{6,4},{8,10},{10,8},{12,14},{14,12},{16,18},{18,... | collective-permute-start | bytes 1179656 | tf_op jit(solution)/shard_map/ppermute | solution.py:126
  106.2 8.1 %collective-permute-start.30 = (bf16[128,512]{1,0:T(8,128)(2,1)S(1)}, bf16[128,512]{1,0:T(8,128)(2,1)S(1)}, u32[]{:S(2)}, u32[]{:S(2)}) collective-permute-start(bf16[128,512]{1,0:T(8,128)(2,1)S(1)} %get-tuple-element.71.refs_1_), channel_id=1, source_target_pairs={{0,1},{1,0},{2,3},{3,2},{4,5},{5,4},{6,7},{7,6},{8,9},{9,8},{10,11... | collective-permute-start | bytes 393224 | tf_op jit(solution)/shard_map/ppermute | solution.py:533

commit v5 on v4

--- a/solution.py
+++ b/solution.py
@@ -486,7 +486,7 @@
     first_x = swap(first, 2)
     tick = own(1, near, kv_z[1])
     parts = call(
-        z_pack_kernel, [pltpu.HBM((64, 1536), BF16)] + [shape((64, 1536), BF16)] * 3, [ANY, WHOLE] + [ANY] * 3,
+        z_pack_kernel, [shape((64, 1536), BF16)] * 4, [ANY, WHOLE] + [ANY] * 3,
         [WHOLE] * 4, got_c + in_vmem(got_x) + in_hbm(*ask), scalars=[owner], after=[tick], scratch=[dma((20,))],
     )
     asked = [parts[0]] + [swap(parts[s], 4 * s) for s in (1, 2, 3)]
@@ -507,7 +507,7 @@
     near_c = send(near, [(i, i + 1) for i in range(0, 16, 2)])
     answer = call(
         read_kernel, shape((64, 1024), BF16), [WHOLE] * 14, pl.BlockSpec((64, 512), lambda i, *_: (0, i)),
-        [asked[0]] + in_vmem(*asked[1:], own_kv, other_kv, *pairs),
+        in_vmem(*asked, own_kv, other_kv, *pairs),
         scalars=[owner, lengths], grid=(2,),
         scratch=[pltpu.VMEM((256, 128), BF16)], flops=4 * 512 * 8192 * 256, data=2**22, vmem=20,
     )

time: 116 us -> 115 us (level)
  waiting for transfers between devices: 8.5 us -> 9.96 us
    ppermute x25, waiting for transfers between devices: 8.36 us -> 9.94 us  [swap(): return lax.ppermute(array, 'hst', [(i, i ^ bit) for i in range(16)])]
    unnamed x16 -> x14, local copies, waits for them, and re-layouts: 3.04 us -> 3.03 us
  transfers between devices with their start and end apart: 31 -> 31, of which waited for: 7 -> 7; matrix products, arithmetic and copies ran while one was open for 5% -> 4% of each run, Pallas kernels for 46% -> 46%
where the time goes in v5:
time: 115 us; the launch traced here: 114 us
  Pallas kernels  55.4 us (48%)
  starting transfers between devices  40.6 us (35%)
  waiting for transfers between devices  9.96 us (9%)
  local copies, waits for them, and re-layouts  4.07 us (4%)
  other arithmetic  2.76 us (2%)
  between operations  1.61 us (1%)
    pallas_call x11, Pallas kernels, call(): pl.pallas_call(body, grid_spec=pltpu.PrefetchScalarGridSpec(num_scalar_pr...  55.4 us
    ppermute x25, starting transfers between devices, swap(): return lax.ppermute(array, 'hst', [(i, i ^ bit) for i in range(16)])  25.8 us
    ppermute x5, starting transfers between devices, send(): return lax.ppermute(array, 'hst', pairs)  13.3 us
    ppermute x25, waiting for transfers between devices, swap(): return lax.ppermute(array, 'hst', [(i, i ^ bit) for i in range(16)])  9.94 us
    unnamed x14, local copies, waits for them, and re-layouts  3.03 us
  transfers between devices with their start and end apart: 31, of which 7 were waited for; matrix products, arithmetic and copies ran while one was open for 4% of the time, Pallas kernels for 46%

profile of v5, /device:TPU:0, one launch (start us, length us, event | category | flops | bytes accessed | tf_op | source)
XLA Modules:
  0.0 114.4 jit_solution(4802343452227329371)
XLA Ops:
  0.6 1.3 %shard_map.104.refs_0_ = bf16[128,5120]{1,0:T(8,128)(2,1)S(1)} custom-call(bf16[1,256,4096]{2,1,0:T(8,128)(2,1)} %refs_4_.6, bf16[1,256,512]{2,1,0:T(8,128)(2,1)} %refs_5_.1, bf16[1,256,512]{2,1,0:T(8,128)(2,1)} %refs_6_.1), custom_call_target="tpu_custom_call" | custom-call | tf_op jit(solution)/shard_map/pallas_call | solution.py:142
  1.9 0.5 collective-permute-start.1
  2.5 2.8 %shard_map.105 = (bf16[1024,128]{1,0:T(8,128)(2,1)}, bf16[1024,128]{1,0:T(8,128)(2,1)S(1)}, bf16[1024,128]{1,0:T(8,128)(2,1)S(1)}, bf16[1024,128]{1,0:T(8,128)(2...) custom-call(bf16[128,5120]{1,0:T(8,128)(2,1)S(1)} %shard_map.104.refs_0_, bf16[512,512]{1,0:T(8,128)(2,1)} %refs_3_.5, ...), custom_call_target="tpu_custom_call" | custom-call | tf_op jit(solution)/shard_map/pallas_call | solution.py:142
  5.3 5.2 %collective-permute-start = (bf16[512,512]{1,0:T(8,128)(2,1)}, bf16[512,512]{1,0:T(8,128)(2,1)}, u32[]{:S(2)}, u32[]{:S(2)}) collective-permute-start(bf16[512,512]{1,0:T(8,128)(2,1)} %get-tuple-element.40), channel_id=1, source_target_pairs={{0,4},{1,5}} | collective-permute-start | bytes 1572872 | tf_op jit(solution)/shard_map/ppermute | solution.py:427
  10.5 1.4 %collective-permute-start.8 = (bf16[1024,128]{1,0:T(8,128)(2,1)S(1)}, bf16[1024,128]{1,0:T(8,128)(2,1)}, u32[]{:S(2)}, u32[]{:S(2)}) collective-permute-start(bf16[1024,128]{1,0:T(8,128)(2,1)S(1)} %get-tuple-element.52), channel_id=1, source_target_pairs={{0,16},{2,18},{4,20},{6,22},{8,24},{10,26},{12,28},{14,30},{16,0},... | collective-permute-start | bytes 786440 | tf_op jit(solution)/shard_map/ppermute | solution.py:126
  11.9 3.0 %collective-permute-start.9 = (bf16[1024,128]{1,0:T(8,128)(2,1)S(1)}, bf16[1024,128]{1,0:T(8,128)(2,1)}, u32[]{:S(2)}, u32[]{:S(2)}) collective-permute-start(bf16[1024,128]{1,0:T(8,128)(2,1)S(1)} %get-tuple-element.54), channel_id=1, source_target_pairs={{0,24},{2,26},{4,28},{6,30},{8,16},{10,18},{12,20},{14,22},{16,8},... | collective-permute-start | bytes 786440 | tf_op jit(solution)/shard_map/ppermute | solution.py:126
  15.5 1.0 constant_dynamic-update-slice_fusion.1
  16.5 1.2 %shard_map.106.refs_0_ = bf16[64,6144]{1,0:T(8,128)(2,1)S(1)} custom-call(s32[1]{0:T(128)} %copy.23.refs_0_, bf16[128,5120]{1,0:T(8,128)(2,1)} %collective-permute-done.1.refs_1_.refs_2_, bf16[1,256,4096]{2,1,0:T(8,128)(2,1)} %refs_4_.6, bf16[1,256,512]{2,1,0:T(8,128)(2,1)} %refs_5_.1, bf16[1,256,512]{2,1,0:T(8,128)(2,1)} %refs_6_.1), custom_call_target="tpu_custom_call" | custom-call | tf_op jit(solution)/shard_map/pallas_call | solution.py:142
  17.7 0.0 copy-start.3
  17.7 0.1 collective-permute-start.3
  17.8 7.7 %shard_map.107 = (bf16[512,4096]{1,0:T(8,128)(2,1)}, f32[1024,128]{1,0:T(8,128)}) custom-call(bf16[64,6144]{1,0:T(8,128)(2,1)S(1)} %shard_map.106.refs_0_, bf16[512,4096]{1,0:T(8,128)(2,1)} %refs_2_.13, bf16[512,512]{1,0:T(8,128)(2,1)} %refs_3_.5, bf16[512,512]{1,0:T(8,128)(2,1)} %refs_4_.5), custom_call_target="tpu_custom_call" | custom-call | flops 6442450944 | bytes 4194304 | tf_op jit(solution)/shard_map/pallas_call | solution.py:142
  25.5 0.0 collective-permute-done
  25.5 0.1 broadcast_select_fusion.2.refs_0_
  25.6 2.3 %collective-permute-start.17 = (bf16[512,512]{1,0:T(8,128)(2,1)S(1)}, bf16[512,512]{1,0:T(8,128)(2,1)S(1)}, u32[]{:S(2)}, u32[]{:S(2)}) collective-permute-start(bf16[512,512]{1,0:T(8,128)(2,1)S(1)} %broadcast_select_fusion.2.refs_0_), channel_id=1, source_target_pairs={{0,16},{4,20},{1,17},{5,21}} | collective-permute-start | bytes 1572872 | tf_op jit(solution)/shard_map/ppermute | solution.py:427
  28.0 2.1 %collective-permute-start.10 = (bf16[2048,128]{1,0:T(8,128)(2,1)S(1)}, bf16[2048,128]{1,0:T(8,128)(2,1)S(1)}, u32[]{:S(2)}, u32[]{:S(2)}) collective-permute-start(bf16[2048,128]{1,0:T(8,128)(2,1)S(1)} %constant_dynamic-update-slice_fusion.refs_8_), channel_id=1, source_target_pairs={{0,4},{2,6},{4,0},{6,2},{8,12},{10,14},{12,8},{14,10},{16,20},{18,... | collective-permute-start | bytes 1572872 | tf_op jit(solution)/shard_map/ppermute | solution.py:126
  30.1 7.6 %shard_map.108 = (bf16[512,4096]{1,0:T(8,128)(2,1)}, f32[1024,128]{1,0:T(8,128)}) custom-call(bf16[512,512]{1,0:T(8,128)(2,1)S(1)} %broadcast_select_fusion.2.refs_0_, bf16[1024,128]{1,0:T(8,128)(2,1)S(1)} %collective-permute-done.2.refs_1_, bf16[512,4096]{1,0:T(8,128)(2,1)} %refs_2_.13, bf16[512,512]{1,0:T(8,128)(2,1)} %refs_3_.5, ...), custom_call_target="tpu_custom_call", output_to_operand_aliasing={{0}: (5, {})} | custom-call | flops 6442450944 | bytes 4194304 | tf_op jit(solution)/shard_map/pallas_call | solution.py:142
  37.7 0.6 collective-permute-done.3.refs_3_
  38.3 1.0 copy-done
  39.3 0.3 shard_map.109
  39.6 0.1 collective-permute-start.4
  39.7 1.4 %collective-permute-start.5 = (bf16[64,1536]{1,0:T(8,128)(2,1)S(1)}, bf16[64,1536]{1,0:T(8,128)(2,1)S(1)}, u32[]{:S(2)}, u32[]{:S(2)}) collective-permute-start(bf16[64,1536]{1,0:T(8,128)(2,1)S(1)} %get-tuple-element.48), channel_id=1, source_target_pairs={{0,16},{2,18},{4,20},{6,22},{8,24},{10,26},{12,28},{14,30},{16,0},... | collective-permute-start | bytes 589832 | tf_op jit(solution)/shard_map/ppermute | solution.py:126
  41.1 3.0 %collective-permute-start.6 = (bf16[64,1536]{1,0:T(8,128)(2,1)S(1)}, bf16[64,1536]{1,0:T(8,128)(2,1)S(1)}, u32[]{:S(2)}, u32[]{:S(2)}) collective-permute-start(bf16[64,1536]{1,0:T(8,128)(2,1)S(1)} %get-tuple-element.49), channel_id=1, source_target_pairs={{0,24},{2,26},{4,28},{6,30},{8,16},{10,18},{12,20},{14,22},{16,8},... | collective-permute-start | bytes 589832 | tf_op jit(solution)/shard_map/ppermute | solution.py:126
  44.1 1.0 constant_dynamic-update-slice_fusion.3
  45.0 0.0 collective-permute-done.9
  45.0 1.0 constant_dynamic-update-slice_fusion.2.refs_9_
  46.0 1.2 %collective-permute-start.11 = (bf16[2048,128]{1,0:T(8,128)(2,1)S(1)}, bf16[2048,128]{1,0:T(8,128)(2,1)S(1)}, u32[]{:S(2)}, u32[]{:S(2)}) collective-permute-start(bf16[2048,128]{1,0:T(8,128)(2,1)S(1)} %constant_dynamic-update-slice_fusion.2.refs_9_), channel_id=1, source_target_pairs={{0,4},{2,6},{4,0},{6,2},{8,12},{10,14},{12,8},{14,10},{16,20},{18,... | collective-permute-start | bytes 1572872 | tf_op jit(solution)/shard_map/ppermute | solution.py:126
  47.2 0.8 broadcast_select_fusion
  48.1 0.0 collective-permute-done.4.refs_3_
  48.1 2.2 %collective-permute-start.18 = (bf16[512,512]{1,0:T(8,128)(2,1)}, bf16[512,512]{1,0:T(8,128)(2,1)}, u32[]{:S(2)}, u32[]{:S(2)}) collective-permute-start(bf16[512,512]{1,0:T(8,128)(2,1)} %broadcast_select_fusion), channel_id=1, source_target_pairs={{0,8},{4,12},{16,24},{20,28},{1,9},{5,13},{17,25},{21,29}} | collective-permute-start | bytes 1572872 | tf_op jit(solution)/shard_map/ppermute | solution.py:427
  50.3 4.0 %collective-permute-done.5.refs_4_ = bf16[64,1536]{1,0:T(8,128)(2,1)S(1)} collective-permute-done((bf16[64,1536]{1,0:T(8,128)(2,1)S(1)}, bf16[64,1536]{1,0:T(8,128)(2,1)S(1)}, u32[]{:S(2)}, u32[]{:S(2)}) %collective-permute-start.5) | collective-permute-done | bytes 196640 | tf_op jit(solution)/shard_map/ppermute | solution.py:126
  54.3 0.0 collective-permute-done.6.refs_5_
  54.3 0.0 collective-permute-done.10.refs_10_
  54.3 0.1 collective-permute-start.14
  54.4 0.5 collective-permute-start.13
  54.9 0.1 collective-permute-start.12
  54.9 1.7 %collective-permute-done.11.refs_11_ = bf16[2048,128]{1,0:T(8,128)(2,1)S(1)} collective-permute-done((bf16[2048,128]{1,0:T(8,128)(2,1)S(1)}, bf16[2048,128]{1,0:T(8,128)(2,1)S(1)}, u32[]{:S(2)}, u32[]{:S(2)}) %collective-permute-start.11) | collective-permute-done | bytes 524320 | tf_op jit(solution)/shard_map/ppermute | solution.py:126
  56.6 0.0 collective-permute-start.15
  56.6 0.5 collective-permute-start.7
  57.1 1.1 broadcast_select_fusion.1.refs_5_.refs_4_
  58.2 0.4 collective-permute-done.7.refs_7_
  58.6 1.6 %collective-permute-start.19 = (bf16[512,512]{1,0:T(8,128)(2,1)S(1)}, bf16[512,512]{1,0:T(8,128)(2,1)S(1)}, u32[]{:S(2)}, u32[]{:S(2)}) collective-permute-start(bf16[512,512]{1,0:T(8,128)(2,1)S(1)} %broadcast_select_fusion.1.refs_5_.refs_4_), channel_id=1, source_target_pairs={{0,4},{2,6},{4,0},{6,2},{8,12},{10,14},{12,8},{14,10},{16,20},{18,... | collective-permute-start | bytes 1572872 | tf_op jit(solution)/shard_map/ppermute | solution.py:126
  60.3 2.0 %collective-permute-start.20 = (bf16[512,512]{1,0:T(8,128)(2,1)S(1)}, bf16[512,512]{1,0:T(8,128)(2,1)S(1)}, u32[]{:S(2)}, u32[]{:S(2)}) collective-permute-start(bf16[512,512]{1,0:T(8,128)(2,1)S(1)} %broadcast_select_fusion.1.refs_5_.refs_4_), channel_id=1, source_target_pairs={{0,2},{4,6},{8,10},{12,14},{16,18},{20,22},{24,26},{28,30},{1,3},{... | collective-permute-start | bytes 1572872 | tf_op jit(solution)/shard_map/ppermute | solution.py:427
  62.3 0.0 collective-permute-done.13.refs_13_
  62.3 0.0 collective-permute-done.12.refs_12_
  62.3 8.9 %shard_map.110.refs_1_ = bf16[64,1024]{1,0:T(8,128)(2,1)S(1)} custom-call(s32[1]{0:T(128)} %copy.23.refs_0_, s32[16]{0:T(128)S(1)} %copy-done.2, bf16[64,1536]{1,0:T(8,128)(2,1)S(1)} %get-tuple-element.46.refs_2_, bf16[64,1536]{1,0:T(8,128)(2,1)S(1)} %collective-permute-done.4.refs_3_, bf16[64,1536]{1,0:T(8,128)(2,1)S(1)} %collective-permute-done.5.refs_4_, ...), custom_call_target="tpu_custom_call" | custom-call | flops 4294967296 | bytes 4194304 | tf_op jit(solution)/shard_map/pallas_call | solution.py:142
  71.3 1.4 %collective-permute-done.19.refs_6_.refs_5_ = bf16[512,512]{1,0:T(8,128)(2,1)S(1)} collective-permute-done((bf16[512,512]{1,0:T(8,128)(2,1)S(1)}, bf16[512,512]{1,0:T(8,128)(2,1)S(1)}, u32[]{:S(2)}, u32[]{:S(2)}) %collective-permute-start.19) | collective-permute-done | bytes 524320 | tf_op jit(solution)/shard_map/ppermute | solution.py:126
  72.7 1.6 %collective-permute-start.21 = (bf16[512,512]{1,0:T(8,128)(2,1)S(1)}, bf16[512,512]{1,0:T(8,128)(2,1)S(1)}, u32[]{:S(2)}, u32[]{:S(2)}) collective-permute-start(bf16[512,512]{1,0:T(8,128)(2,1)S(1)} %collective-permute-done.19.refs_6_.refs_5_), channel_id=1, source_target_pairs={{0,2},{4,6},{8,10},{12,14},{16,18},{20,22},{24,26},{28,30},{1,3},{... | collective-permute-start | bytes 1572872 | tf_op jit(solution)/shard_map/ppermute | solution.py:427
  74.3 1.9 %collective-permute-start.24 = (bf16[64,1024]{1,0:T(8,128)(2,1)S(1)}, bf16[64,1024]{1,0:T(8,128)(2,1)S(1)}, u32[]{:S(2)}, u32[]{:S(2)}) collective-permute-start(bf16[64,1024]{1,0:T(8,128)(2,1)S(1)} %shard_map.110.refs_1_), channel_id=1, source_target_pairs={{0,4},{2,6},{4,0},{6,2},{8,12},{10,14},{12,8},{14,10},{16,20},{18,... | collective-permute-start | bytes 393224 | tf_op jit(solution)/shard_map/ppermute | solution.py:126
  76.2 5.3 %collective-permute-start.23 = (bf16[64,1024]{1,0:T(8,128)(2,1)S(1)}, bf16[64,1024]{1,0:T(8,128)(2,1)S(1)}, u32[]{:S(2)}, u32[]{:S(2)}) collective-permute-start(bf16[64,1024]{1,0:T(8,128)(2,1)S(1)} %shard_map.110.refs_1_), channel_id=1, source_target_pairs={{0,24},{2,26},{4,28},{6,30},{8,16},{10,18},{12,20},{14,22},{16,8},... | collective-permute-start | bytes 393224 | tf_op jit(solution)/shard_map/ppermute | solution.py:126
  81.4 0.6 collective-permute-start.16
  82.0 10.7 %shard_map.111.refs_8_ = bf16[512,4096]{1,0:T(8,128)(2,1)} custom-call(s32[16]{0:T(128)S(1)} %copy-done.2, bf16[64,1024]{1,0:T(8,128)(2,1)S(1)} %shard_map.110.refs_1_, bf16[512,4096]{1,0:T(8,128)(2,1)} %refs_2_.13, bf16[512,4096]{1,0:T(8,128)(2,1)} %get-tuple-element.59.refs_3_.refs_2_, f32[1024,128]{1,0:T(8,128)} %get-tuple-element.41.refs_4_, ...), custom_call_target="tpu_custom_call" | custom-call | flops 4294967296 | bytes 2097152 | tf_op jit(solution)/shard_map/pallas_call | solution.py:142
  92.8 0.4 collective-permute-start.26
  93.2 1.7 %collective-permute-start.27 = (bf16[64,1024]{1,0:T(8,128)(2,1)S(1)}, bf16[64,1024]{1,0:T(8,128)(2,1)S(1)}, u32[]{:S(2)}, u32[]{:S(2)}) collective-permute-start(bf16[64,1024]{1,0:T(8,128)(2,1)S(1)} %collective-permute-done.22), channel_id=1, source_target_pairs={{0,4},{2,6},{4,0},{6,2},{8,12},{10,14},{12,8},{14,10},{16,20},{18,... | collective-permute-start | bytes 393224 | tf_op jit(solution)/shard_map/ppermute | solution.py:126
  94.9 0.3 collective-permute-start.28
  95.3 0.0 copy-start.1
  95.3 0.1 collective-permute-start.25
  95.3 6.9 %shard_map.112.refs_9_ = bf16[512,4096]{1,0:T(8,128)(2,1)} custom-call(s32[16]{0:T(128)S(1)} %copy-done.2, bf16[512,4096]{1,0:T(8,128)(2,1)} %refs_2_.13, bf16[512,4096]{1,0:T(8,128)(2,1)} %get-tuple-element.59.refs_3_.refs_2_, f32[1024,128]{1,0:T(8,128)} %get-tuple-element.45.refs_1_.refs_3_.refs_4_, ...), custom_call_target="tpu_custom_call", output_to_operand_aliasing={{}: (8, {})} | custom-call | flops 2147483648 | bytes 2097152 | tf_op jit(solution)/shard_map/pallas_call | solution.py:142
  102.2 0.2 collective-permute-done.28
  102.4 0.1 collective-permute-start.29
  102.5 1.7 %collective-permute-done.29.refs_3_ = bf16[3,64,1024]{2,1,0:T(8,128)(2,1)S(1)} collective-permute-done((bf16[3,64,1024]{2,1,0:T(8,128)(2,1)S(1)}, bf16[3,64,1024]{2,1,0:T(8,128)(2,1)S(1)}, u32[]{:S(2)}, u32[]{:S(2)}) %collective-permute-start.29) | collective-permute-done | bytes 393248 | tf_op jit(solution)/shard_map/ppermute | solution.py:126
  104.2 1.3 %shard_map.113 = (f32[128,512]{1,0:T(8,128)S(1)}, bf16[128,512]{1,0:T(8,128)(2,1)S(1)}) custom-call(bf16[5,64,1024]{2,1,0:T(8,128)(2,1)S(1)} %bitcast_dynamic-update-slice_fusion.refs_0_, bf16[5,64,1024]{2,1,0:T(8,128)(2,1)S(1)} %collective-permute-done.25.refs_1_, bf16[3,64,1024]{2,1,0:T(8,128)(2,1)S(1)} %pad_maximum_fusion.refs_2_, ...), custom_call_target="tpu_custom_call" | custom-call | flops 1073741824 | bytes 4194304 | tf_op jit(solution)/shard_map/pallas_call | solution.py:142
  105.6 1.6 %collective-permute-start.30 = (bf16[128,512]{1,0:T(8,128)(2,1)S(1)}, bf16[128,512]{1,0:T(8,128)(2,1)S(1)}, u32[]{:S(2)}, u32[]{:S(2)}) collective-permute-start(bf16[128,512]{1,0:T(8,128)(2,1)S(1)} %get-tuple-element.71.refs_1_), channel_id=1, source_target_pairs={{0,1},{1,0},{2,3},{3,2},{4,5},{5,4},{6,7},{7,6},{8,9},{9,8},{10,11... | collective-permute-start | bytes 393224 | tf_op jit(solution)/shard_map/ppermute | solution.py:533
  107.2 6.6 %shard_map.114 = bf16[512,4096]{1,0:T(8,128)(2,1)} custom-call(s32[16]{0:T(128)S(1)} %copy-done.2, bf16[128,512]{1,0:T(8,128)(2,1)S(1)} %get-tuple-element.71.refs_1_, bf16[512,4096]{1,0:T(8,128)(2,1)} %refs_2_.13, bf16[512,4096]{1,0:T(8,128)(2,1)} %get-tuple-element.59.refs_3_.refs_2_, ...), custom_call_target="tpu_custom_call", output_to_operand_aliasing={{}: (9, {})} | custom-call | flops 2147483648 | bytes 2097152 | tf_op jit(solution)/shard_map/pallas_call | solution.py:142
  113.7 0.7 add_convert_fusion
  (32 shorter events, 0.2 us)
Async XLA Ops:
  1.9 14.6 %collective-permute-start.1 = (bf16[128,5120]{1,0:T(8,128)(2,1)S(1)}, bf16[128,5120]{1,0:T(8,128)(2,1)}, u32[]{:S(2)}, u32[]{:S(2)}) collective-permute-start(bf16[128,5120]{1,0:T(8,128)(2,1)S(1)} %shard_map.104.refs_0_), channel_id=1, source_target_pairs={{0,2},{2,0},{4,6},{6,4},{8,10},{10,8},{12,14},{14,12},{16,18},{18,... | collective-permute-start | bytes 3932168 | tf_op jit(solution)/shard_map/ppermute | solution.py:126
  5.3 20.3 %collective-permute-start = (bf16[512,512]{1,0:T(8,128)(2,1)}, bf16[512,512]{1,0:T(8,128)(2,1)}, u32[]{:S(2)}, u32[]{:S(2)}) collective-permute-start(bf16[512,512]{1,0:T(8,128)(2,1)} %get-tuple-element.40), channel_id=1, source_target_pairs={{0,4},{1,5}} | collective-permute-start | bytes 1572872 | tf_op jit(solution)/shard_map/ppermute | solution.py:427
  10.5 17.5 %collective-permute-start.2 = (bf16[1024,128]{1,0:T(8,128)(2,1)S(1)}, bf16[1024,128]{1,0:T(8,128)(2,1)S(1)}, u32[]{:S(2)}, u32[]{:S(2)}) collective-permute-start(bf16[1024,128]{1,0:T(8,128)(2,1)S(1)} %get-tuple-element.43), channel_id=1, source_target_pairs={{0,8},{2,10},{4,12},{6,14},{8,0},{10,2},{12,4},{14,6},{16,24},{18,... | collective-permute-start | bytes 786440 | tf_op jit(solution)/shard_map/ppermute | solution.py:126
  10.5 30.6 %collective-permute-start.8 = (bf16[1024,128]{1,0:T(8,128)(2,1)S(1)}, bf16[1024,128]{1,0:T(8,128)(2,1)}, u32[]{:S(2)}, u32[]{:S(2)}) collective-permute-start(bf16[1024,128]{1,0:T(8,128)(2,1)S(1)} %get-tuple-element.52), channel_id=1, source_target_pairs={{0,16},{2,18},{4,20},{6,22},{8,24},{10,26},{12,28},{14,30},{16,0},... | collective-permute-start | bytes 786440 | tf_op jit(solution)/shard_map/ppermute | solution.py:126
  11.9 33.1 %collective-permute-start.9 = (bf16[1024,128]{1,0:T(8,128)(2,1)S(1)}, bf16[1024,128]{1,0:T(8,128)(2,1)}, u32[]{:S(2)}, u32[]{:S(2)}) collective-permute-start(bf16[1024,128]{1,0:T(8,128)(2,1)S(1)} %get-tuple-element.54), channel_id=1, source_target_pairs={{0,24},{2,26},{4,28},{6,30},{8,16},{10,18},{12,20},{14,22},{16,8},... | collective-permute-start | bytes 786440 | tf_op jit(solution)/shard_map/ppermute | solution.py:126
  17.7 7.8 %copy-start.3 = (bf16[512,512]{1,0:T(8,128)(2,1)S(1)}, bf16[512,512]{1,0:T(8,128)(2,1)}, u32[]{:S(2)}) copy-start(bf16[512,512]{1,0:T(8,128)(2,1)} %get-tuple-element.38) | copy-start | bytes 1572868
  17.7 20.5 %collective-permute-start.3 = (bf16[64,6144]{1,0:T(8,128)(2,1)S(1)}, bf16[64,6144]{1,0:T(8,128)(2,1)S(1)}, u32[]{:S(2)}, u32[]{:S(2)}) collective-permute-start(bf16[64,6144]{1,0:T(8,128)(2,1)S(1)} %shard_map.106.refs_0_), channel_id=1, source_target_pairs={{0,4},{2,6},{4,0},{6,2},{8,12},{10,14},{12,8},{14,10},{16,20},{18,... | collective-permute-start | bytes 2359304 | tf_op jit(solution)/shard_map/ppermute | solution.py:126
  25.6 14.0 %collective-permute-start.17 = (bf16[512,512]{1,0:T(8,128)(2,1)S(1)}, bf16[512,512]{1,0:T(8,128)(2,1)S(1)}, u32[]{:S(2)}, u32[]{:S(2)}) collective-permute-start(bf16[512,512]{1,0:T(8,128)(2,1)S(1)} %broadcast_select_fusion.2.refs_0_), channel_id=1, source_target_pairs={{0,16},{4,20},{1,17},{5,21}} | collective-permute-start | bytes 1572872 | tf_op jit(solution)/shard_map/ppermute | solution.py:427
  28.0 26.3 %collective-permute-start.10 = (bf16[2048,128]{1,0:T(8,128)(2,1)S(1)}, bf16[2048,128]{1,0:T(8,128)(2,1)S(1)}, u32[]{:S(2)}, u32[]{:S(2)}) collective-permute-start(bf16[2048,128]{1,0:T(8,128)(2,1)S(1)} %constant_dynamic-update-slice_fusion.refs_8_), channel_id=1, source_target_pairs={{0,4},{2,6},{4,0},{6,2},{8,12},{10,14},{12,8},{14,10},{16,20},{18,... | collective-permute-start | bytes 1572872 | tf_op jit(solution)/shard_map/ppermute | solution.py:126
  38.3 1.0 copy-start
  39.3 23.0 %copy-start.2 = (s32[16]{0:T(128)S(1)}, s32[16]{0:T(128)}, u32[]{:S(2)}) copy-start(s32[16]{0:T(128)} %refs_0_.10) | copy-start | bytes 196
  39.6 8.5 %collective-permute-start.4 = (bf16[64,1536]{1,0:T(8,128)(2,1)S(1)}, bf16[64,1536]{1,0:T(8,128)(2,1)S(1)}, u32[]{:S(2)}, u32[]{:S(2)}) collective-permute-start(bf16[64,1536]{1,0:T(8,128)(2,1)S(1)} %get-tuple-element.47), channel_id=1, source_target_pairs={{0,8},{2,10},{4,12},{6,14},{8,0},{10,2},{12,4},{14,6},{16,24},{18,... | collective-permute-start | bytes 589832 | tf_op jit(solution)/shard_map/ppermute | solution.py:126
  39.7 14.6 %collective-permute-start.5 = (bf16[64,1536]{1,0:T(8,128)(2,1)S(1)}, bf16[64,1536]{1,0:T(8,128)(2,1)S(1)}, u32[]{:S(2)}, u32[]{:S(2)}) collective-permute-start(bf16[64,1536]{1,0:T(8,128)(2,1)S(1)} %get-tuple-element.48), channel_id=1, source_target_pairs={{0,16},{2,18},{4,20},{6,22},{8,24},{10,26},{12,28},{14,30},{16,0},... | collective-permute-start | bytes 589832 | tf_op jit(solution)/shard_map/ppermute | solution.py:126
  41.1 13.2 %collective-permute-start.6 = (bf16[64,1536]{1,0:T(8,128)(2,1)S(1)}, bf16[64,1536]{1,0:T(8,128)(2,1)S(1)}, u32[]{:S(2)}, u32[]{:S(2)}) collective-permute-start(bf16[64,1536]{1,0:T(8,128)(2,1)S(1)} %get-tuple-element.49), channel_id=1, source_target_pairs={{0,24},{2,26},{4,28},{6,30},{8,16},{10,18},{12,20},{14,22},{16,8},... | collective-permute-start | bytes 589832 | tf_op jit(solution)/shard_map/ppermute | solution.py:126
  46.0 10.6 %collective-permute-start.11 = (bf16[2048,128]{1,0:T(8,128)(2,1)S(1)}, bf16[2048,128]{1,0:T(8,128)(2,1)S(1)}, u32[]{:S(2)}, u32[]{:S(2)}) collective-permute-start(bf16[2048,128]{1,0:T(8,128)(2,1)S(1)} %constant_dynamic-update-slice_fusion.2.refs_9_), channel_id=1, source_target_pairs={{0,4},{2,6},{4,0},{6,2},{8,12},{10,14},{12,8},{14,10},{16,20},{18,... | collective-permute-start | bytes 1572872 | tf_op jit(solution)/shard_map/ppermute | solution.py:126
  48.1 8.5 %collective-permute-start.18 = (bf16[512,512]{1,0:T(8,128)(2,1)}, bf16[512,512]{1,0:T(8,128)(2,1)}, u32[]{:S(2)}, u32[]{:S(2)}) collective-permute-start(bf16[512,512]{1,0:T(8,128)(2,1)} %broadcast_select_fusion), channel_id=1, source_target_pairs={{0,8},{4,12},{16,24},{20,28},{1,9},{5,13},{17,25},{21,29}} | collective-permute-start | bytes 1572872 | tf_op jit(solution)/shard_map/ppermute | solution.py:427
  54.3 6.0 %collective-permute-start.14 = (bf16[2048,128]{1,0:T(8,128)(2,1)S(1)}, bf16[2048,128]{1,0:T(8,128)(2,1)}, u32[]{:S(2)}, u32[]{:S(2)}) collective-permute-start(bf16[2048,128]{1,0:T(8,128)(2,1)S(1)} %collective-permute-done.10.refs_10_), channel_id=1, source_target_pairs={{0,2},{2,0},{4,6},{6,4},{8,10},{10,8},{12,14},{14,12},{16,18},{18,... | collective-permute-start | bytes 1572872 | tf_op jit(solution)/shard_map/ppermute | solution.py:126
  54.4 7.9 %collective-permute-start.13 = (bf16[2048,128]{1,0:T(8,128)(2,1)S(1)}, bf16[2048,128]{1,0:T(8,128)(2,1)}, u32[]{:S(2)}, u32[]{:S(2)}) collective-permute-start(bf16[2048,128]{1,0:T(8,128)(2,1)S(1)} %constant_dynamic-update-slice_fusion.2.refs_9_), channel_id=1, source_target_pairs={{0,2},{2,0},{4,6},{6,4},{8,10},{10,8},{12,14},{14,12},{16,18},{18,... | collective-permute-start | bytes 1572872 | tf_op jit(solution)/shard_map/ppermute | solution.py:126
  54.9 7.4 %collective-permute-start.12 = (bf16[2048,128]{1,0:T(8,128)(2,1)S(1)}, bf16[2048,128]{1,0:T(8,128)(2,1)}, u32[]{:S(2)}, u32[]{:S(2)}) collective-permute-start(bf16[2048,128]{1,0:T(8,128)(2,1)S(1)} %constant_dynamic-update-slice_fusion.refs_8_), channel_id=1, source_target_pairs={{0,2},{2,0},{4,6},{6,4},{8,10},{10,8},{12,14},{14,12},{16,18},{18,... | collective-permute-start | bytes 1572872 | tf_op jit(solution)/shard_map/ppermute | solution.py:126
  56.6 5.7 %collective-permute-start.15 = (bf16[2048,128]{1,0:T(8,128)(2,1)S(1)}, bf16[2048,128]{1,0:T(8,128)(2,1)}, u32[]{:S(2)}, u32[]{:S(2)}) collective-permute-start(bf16[2048,128]{1,0:T(8,128)(2,1)S(1)} %collective-permute-done.11.refs_11_), channel_id=1, source_target_pairs={{0,2},{2,0},{4,6},{6,4},{8,10},{10,8},{12,14},{14,12},{16,18},{18,... | collective-permute-start | bytes 1572872 | tf_op jit(solution)/shard_map/ppermute | solution.py:126
  56.6 2.0 %collective-permute-start.7 = (bf16[64,512]{1,0:T(8,128)(2,1)S(1)}, bf16[64,512]{1,0:T(8,128)(2,1)S(1)}, u32[]{:S(2)}, u32[]{:S(2)}) collective-permute-start(bf16[64,512]{1,0:T(8,128)(2,1)S(1)} %fusion.1.refs_6_), channel_id=1, source_target_pairs={{0,2},{2,0},{4,6},{6,4},{8,10},{10,8},{12,14},{14,12},{16,18},{18,... | collective-permute-start | bytes 196616 | tf_op jit(solution)/shard_map/ppermute | solution.py:126
  58.6 14.1 %collective-permute-start.19 = (bf16[512,512]{1,0:T(8,128)(2,1)S(1)}, bf16[512,512]{1,0:T(8,128)(2,1)S(1)}, u32[]{:S(2)}, u32[]{:S(2)}) collective-permute-start(bf16[512,512]{1,0:T(8,128)(2,1)S(1)} %broadcast_select_fusion.1.refs_5_.refs_4_), channel_id=1, source_target_pairs={{0,4},{2,6},{4,0},{6,2},{8,12},{10,14},{12,8},{14,10},{16,20},{18,... | collective-permute-start | bytes 1572872 | tf_op jit(solution)/shard_map/ppermute | solution.py:126
  60.3 21.2 %collective-permute-start.20 = (bf16[512,512]{1,0:T(8,128)(2,1)S(1)}, bf16[512,512]{1,0:T(8,128)(2,1)S(1)}, u32[]{:S(2)}, u32[]{:S(2)}) collective-permute-start(bf16[512,512]{1,0:T(8,128)(2,1)S(1)} %broadcast_select_fusion.1.refs_5_.refs_4_), channel_id=1, source_target_pairs={{0,2},{4,6},{8,10},{12,14},{16,18},{20,22},{24,26},{28,30},{1,3},{... | collective-permute-start | bytes 1572872 | tf_op jit(solution)/shard_map/ppermute | solution.py:427
  72.7 9.3 %collective-permute-start.21 = (bf16[512,512]{1,0:T(8,128)(2,1)S(1)}, bf16[512,512]{1,0:T(8,128)(2,1)S(1)}, u32[]{:S(2)}, u32[]{:S(2)}) collective-permute-start(bf16[512,512]{1,0:T(8,128)(2,1)S(1)} %collective-permute-done.19.refs_6_.refs_5_), channel_id=1, source_target_pairs={{0,2},{4,6},{8,10},{12,14},{16,18},{20,22},{24,26},{28,30},{1,3},{... | collective-permute-start | bytes 1572872 | tf_op jit(solution)/shard_map/ppermute | solution.py:427
  74.3 18.5 %collective-permute-start.24 = (bf16[64,1024]{1,0:T(8,128)(2,1)S(1)}, bf16[64,1024]{1,0:T(8,128)(2,1)S(1)}, u32[]{:S(2)}, u32[]{:S(2)}) collective-permute-start(bf16[64,1024]{1,0:T(8,128)(2,1)S(1)} %shard_map.110.refs_1_), channel_id=1, source_target_pairs={{0,4},{2,6},{4,0},{6,2},{8,12},{10,14},{12,8},{14,10},{16,20},{18,... | collective-permute-start | bytes 393224 | tf_op jit(solution)/shard_map/ppermute | solution.py:126
  76.2 16.6 %collective-permute-start.23 = (bf16[64,1024]{1,0:T(8,128)(2,1)S(1)}, bf16[64,1024]{1,0:T(8,128)(2,1)S(1)}, u32[]{:S(2)}, u32[]{:S(2)}) collective-permute-start(bf16[64,1024]{1,0:T(8,128)(2,1)S(1)} %shard_map.110.refs_1_), channel_id=1, source_target_pairs={{0,24},{2,26},{4,28},{6,30},{8,16},{10,18},{12,20},{14,22},{16,8},... | collective-permute-start | bytes 393224 | tf_op jit(solution)/shard_map/ppermute | solution.py:126
  81.4 11.3 %collective-permute-start.22 = (bf16[64,1024]{1,0:T(8,128)(2,1)S(1)}, bf16[64,1024]{1,0:T(8,128)(2,1)S(1)}, u32[]{:S(2)}, u32[]{:S(2)}) collective-permute-start(bf16[64,1024]{1,0:T(8,128)(2,1)S(1)} %shard_map.110.refs_1_), channel_id=1, source_target_pairs={{0,16},{2,18},{4,20},{6,22},{8,24},{10,26},{12,28},{14,30},{16,0},... | collective-permute-start | bytes 393224 | tf_op jit(solution)/shard_map/ppermute | solution.py:126
  81.4 11.3 %collective-permute-start.16 = (bf16[64,1024]{1,0:T(8,128)(2,1)S(1)}, bf16[64,1024]{1,0:T(8,128)(2,1)S(1)}, u32[]{:S(2)}, u32[]{:S(2)}) collective-permute-start(bf16[64,1024]{1,0:T(8,128)(2,1)S(1)} %shard_map.110.refs_1_), channel_id=1, source_target_pairs={{0,8},{2,10},{4,12},{6,14},{8,0},{10,2},{12,4},{14,6},{16,24},{18,... | collective-permute-start | bytes 393224 | tf_op jit(solution)/shard_map/ppermute | solution.py:126
  92.8 9.4 %collective-permute-start.26 = (bf16[64,1024]{1,0:T(8,128)(2,1)S(1)}, bf16[64,1024]{1,0:T(8,128)(2,1)S(1)}, u32[]{:S(2)}, u32[]{:S(2)}) collective-permute-start(bf16[64,1024]{1,0:T(8,128)(2,1)S(1)} %collective-permute-done.16), channel_id=1, source_target_pairs={{0,4},{2,6},{4,0},{6,2},{8,12},{10,14},{12,8},{14,10},{16,20},{18,... | collective-permute-start | bytes 393224 | tf_op jit(solution)/shard_map/ppermute | solution.py:126
  93.2 9.1 %collective-permute-start.27 = (bf16[64,1024]{1,0:T(8,128)(2,1)S(1)}, bf16[64,1024]{1,0:T(8,128)(2,1)S(1)}, u32[]{:S(2)}, u32[]{:S(2)}) collective-permute-start(bf16[64,1024]{1,0:T(8,128)(2,1)S(1)} %collective-permute-done.22), channel_id=1, source_target_pairs={{0,4},{2,6},{4,0},{6,2},{8,12},{10,14},{12,8},{14,10},{16,20},{18,... | collective-permute-start | bytes 393224 | tf_op jit(solution)/shard_map/ppermute | solution.py:126
  94.9 7.5 %collective-permute-start.28 = (bf16[64,1024]{1,0:T(8,128)(2,1)S(1)}, bf16[64,1024]{1,0:T(8,128)(2,1)S(1)}, u32[]{:S(2)}, u32[]{:S(2)}) collective-permute-start(bf16[64,1024]{1,0:T(8,128)(2,1)S(1)} %collective-permute-done.23), channel_id=1, source_target_pairs={{0,4},{2,6},{4,0},{6,2},{8,12},{10,14},{12,8},{14,10},{16,20},{18,... | collective-permute-start | bytes 393224 | tf_op jit(solution)/shard_map/ppermute | solution.py:126
  95.3 9.0 %copy-start.1 = (bf16[4096,512]{1,0:T(8,128)(2,1)S(1)}, bf16[4096,512]{1,0:T(8,128)(2,1)}, u32[]{:S(2)}) copy-start(bf16[4096,512]{1,0:T(8,128)(2,1)} %refs_4_.7) | copy-start | bytes 12582916
  95.3 8.9 %collective-permute-start.25 = (bf16[5,64,1024]{2,1,0:T(8,128)(2,1)S(1)}, bf16[5,64,1024]{2,1,0:T(8,128)(2,1)S(1)}, u32[]{:S(2)}, u32[]{:S(2)}) collective-permute-start(bf16[5,64,1024]{2,1,0:T(8,128)(2,1)S(1)} %bitcast_dynamic-update-slice_fusion.refs_0_), channel_id=1, source_target_pairs={{0,2},{2,0},{4,6},{6,4},{8,10},{10,8},{12,14},{14,12},{16,18},{18,... | collective-permute-start | bytes 1966088 | tf_op jit(solution)/shard_map/ppermute | solution.py:126
  102.4 1.8 %collective-permute-start.29 = (bf16[3,64,1024]{2,1,0:T(8,128)(2,1)S(1)}, bf16[3,64,1024]{2,1,0:T(8,128)(2,1)S(1)}, u32[]{:S(2)}, u32[]{:S(2)}) collective-permute-start(bf16[3,64,1024]{2,1,0:T(8,128)(2,1)S(1)} %pad_maximum_fusion.refs_2_), channel_id=1, source_target_pairs={{0,2},{2,0},{4,6},{6,4},{8,10},{10,8},{12,14},{14,12},{16,18},{18,... | collective-permute-start | bytes 1179656 | tf_op jit(solution)/shard_map/ppermute | solution.py:126
  105.6 8.2 %collective-permute-start.30 = (bf16[128,512]{1,0:T(8,128)(2,1)S(1)}, bf16[128,512]{1,0:T(8,128)(2,1)S(1)}, u32[]{:S(2)}, u32[]{:S(2)}) collective-permute-start(bf16[128,512]{1,0:T(8,128)(2,1)S(1)} %get-tuple-element.71.refs_1_), channel_id=1, source_target_pairs={{0,1},{1,0},{2,3},{3,2},{4,5},{5,4},{6,7},{7,6},{8,9},{9,8},{10,11... | collective-permute-start | bytes 393224 | tf_op jit(solution)/shard_map/ppermute | solution.py:533
